TPU v7x, 32 devices: a whole 2x2x4 slice. The times are simulated.
32 devices in a mesh: trav: 4 (over z), bulk: 8 (over y, x, core).
Axes of the slice: x: 2, y: 2, z: 4, core: 2. Of those that a mesh axis runs over, the one named last changes fastest.
Arguments:
- parents: bfloat16 [6144, 1024], P(('trav', 'bulk')), may hold values from -6 to 6
- act_table: bfloat16 [128, 1024], replicated, may hold values from -5 to 5
- bucket_table: bfloat16 [2048, 1024], P('bulk'), may hold values from -5 to 5
- w_first: bfloat16 [1024, 2048], P(('trav', 'bulk')), may hold values from -0.1875 to 0.1875
- b_first: float32 [2048], replicated, may hold values from -3 to 3
- w_second: bfloat16 [2048, 2048], P(('trav', 'bulk')), may hold values from -0.1875 to 0.1875
- b_second: float32 [2048], replicated, may hold values from -3 to 3
- w_head: bfloat16 [2048, 8], replicated, may hold values from -0.1875 to 0.1875
- b_head: float32 [8], replicated, may hold values from -3 to 3
- branch_counts: int32 [6144], P(('trav', 'bulk')), may hold values from 1 to 4
- sampled_actions: int32 [6144, 4], P(('trav', 'bulk')), may hold values from 0 to 127
- bucket_owner: int32 [6144, 1], P(('trav', 'bulk')), may hold values from 0 to 7; in each aligned block of 192 rows (0 to 191, 192 to 383, ...) at most 32 rows name the same one
- bucket_row: int32 [6144], P(('trav', 'bulk')), may hold values from 0 to 255
- legal_mask: int32 [6144, 32], P(('trav', 'bulk')), may hold values 0 or 1
- ancestor: int32 [6144], P(('trav', 'bulk')), may hold values from 0 to 47
Outputs:
- strategy: float32 [6144, 32], P(('trav', 'bulk'))
- ancestor_value: float32 [1536], P(('trav', 'bulk'))
Inputs may be any that keep to these rules, and one draw needn't show every extreme that they name: `bucket_owner`: in each aligned block of 192 histories (the histories of one device) no evaluator is named more than 32 times, a bound that some block reaches.
All inputs are finite; a program needn't handle non-finite values. No bound on the sum of `legal_mask` on one device may be relied on, other than what follows from the above.
Results may differ from a plain program's by a relative error of at most 0.0078.
Values may be sent and summed in bfloat16 or wider, within the bound.
No kernel may reach another device: no remote copies, remote signals or barrier semaphores. Data moves between devices by JAX's collectives and lax.ppermute only.
A program may use at most 64 MiB of HBM per device.

v0:
```python
import jax
import jax.numpy as jnp
from jax import lax
from jax.sharding import PartitionSpec as P

tremble = 0.05


def network(inputs, w_first, b_first, w_second, b_second, w_head, b_head):
    columns = inputs
    first = jnp.dot(
        columns,
        lax.all_gather(w_first, ("trav", "bulk"), axis=0, tiled=True),
        preferred_element_type=jnp.float32,
    )
    hidden_one = jnp.maximum(first + b_first, 0.0).astype(jnp.bfloat16)
    columns = hidden_one
    second = jnp.dot(
        columns,
        lax.all_gather(w_second, ("trav", "bulk"), axis=0, tiled=True),
        preferred_element_type=jnp.float32,
    )
    hidden_two = jnp.maximum(second + b_second, 0.0).astype(jnp.bfloat16)
    return jnp.dot(hidden_two, w_head, preferred_element_type=jnp.float32) + b_head


def body(
    parents,
    act_table,
    bucket_table,
    w_first,
    b_first,
    w_second,
    b_second,
    w_head,
    b_head,
    branch_counts,
    sampled_actions,
    bucket_owner,
    bucket_row,
    legal_mask,
    ancestor,
):
    par_count = parents.shape[0]
    feature_count = parents.shape[1]
    branch_slots = sampled_actions.shape[1]
    vocab_size = act_table.shape[0]
    action_count = w_head.shape[1]
    bulk_count = lax.axis_size("bulk")
    capacity = max(2, (4 * par_count + 3 * bulk_count - 1) // (3 * bulk_count))
    slot_total = bulk_count * capacity
    action_onehot = (
        sampled_actions.reshape(-1)[:, None] == jnp.arange(vocab_size)[None, :]
    ).astype(jnp.bfloat16)
    act_rows = jnp.dot(action_onehot, act_table, preferred_element_type=jnp.float32)
    base = (jnp.repeat(parents.astype(jnp.float32), branch_slots, axis=0) + act_rows).astype(
        jnp.bfloat16
    )
    base = lax.optimization_barrier(base)
    owner_index = bucket_owner[:, 0]
    owner_hits = (owner_index[:, None] == jnp.arange(bulk_count)[None, :]).astype(jnp.int32)
    earlier = jnp.cumsum(owner_hits, axis=0) - owner_hits
    slot_index = owner_index * capacity + jnp.sum(earlier * owner_hits, axis=1)
    placement_int = (slot_index[None, :] == jnp.arange(slot_total)[:, None]).astype(jnp.int32)
    slot_bucket = jnp.sum(placement_int * bucket_row[None, :], axis=1).reshape(bulk_count, capacity)
    placement = placement_int.astype(jnp.bfloat16)
    outgoing = jnp.dot(
        placement,
        base.reshape(par_count, branch_slots * feature_count),
        preferred_element_type=jnp.float32,
    )
    outgoing = outgoing.astype(jnp.bfloat16).reshape(
        bulk_count, capacity * branch_slots, feature_count
    )
    arrived_rows = lax.all_to_all(outgoing, "bulk", split_axis=0, concat_axis=0, tiled=True)
    arrived_ids = lax.all_to_all(slot_bucket, "bulk", split_axis=0, concat_axis=0, tiled=True)
    table_rows = jnp.take(bucket_table, arrived_ids.reshape(-1), axis=0)
    inputs = (
        arrived_rows.reshape(slot_total, branch_slots, feature_count).astype(jnp.float32)
        + table_rows.astype(jnp.float32)[:, None, :]
    )
    inputs = inputs.astype(jnp.bfloat16).reshape(slot_total * branch_slots, feature_count)
    evaluated = network(inputs, w_first, b_first, w_second, b_second, w_head, b_head)
    returned = lax.all_to_all(
        evaluated.reshape(bulk_count, capacity * branch_slots * action_count).astype(jnp.bfloat16),
        "bulk",
        split_axis=0,
        concat_axis=0,
        tiled=True,
    ).astype(jnp.float32)
    advantage = jnp.take(
        returned.reshape(slot_total, branch_slots * action_count), slot_index, axis=0
    )
    advantage = advantage.reshape(par_count, branch_slots, action_count)
    first_action = (jnp.arange(action_count) == 0).astype(jnp.float32)
    allowed = jnp.maximum(
        legal_mask.reshape(par_count, branch_slots, action_count).astype(jnp.float32), first_action
    )
    positive = allowed * (jnp.maximum(advantage, 0.0) + tremble)
    sigma = positive / jnp.sum(positive, axis=-1, keepdims=True)
    live = (jnp.arange(branch_slots)[None, :] < branch_counts[:, None]).astype(jnp.float32)
    strategy = (sigma * live[:, :, None]).reshape(par_count, branch_slots * action_count)
    branch_value = jnp.sum(sigma * advantage, axis=-1)
    history_value = jnp.sum(branch_value * live, axis=1) / branch_counts.astype(jnp.float32)
    node_count = par_count // 4
    node_onehot = (ancestor[:, None] == jnp.arange(node_count)[None, :]).astype(jnp.float32)
    ancestor_value = jnp.sum(node_onehot * history_value[:, None], axis=0)
    return (strategy, ancestor_value)


def solution(mesh):
    return jax.shard_map(
        body,
        mesh=mesh,
        in_specs=(
            P(("trav", "bulk"), None),
            P(),
            P("bulk", None),
            P(("trav", "bulk"), None),
            P(),
            P(("trav", "bulk"), None),
            P(),
            P(),
            P(),
            P(("trav", "bulk")),
            P(("trav", "bulk"), None),
            P(("trav", "bulk"), None),
            P(("trav", "bulk")),
            P(("trav", "bulk"), None),
            P(("trav", "bulk")),
        ),
        out_specs=(P(("trav", "bulk"), None), P(("trav", "bulk"))),
        check_vma=False,
    )
```

profile of v0, /device:TPU:0, one launch (start us, length us, event | category | flops | bytes accessed | tf_op | source)
XLA Modules:
  0.0 205.2 jit_solution(1659787118287139891)
XLA Ops:
  7.2 0.7 all-gather.3.cloned.1.call-update
  8.0 0.7 all-gather.5.cloned.1.call-update
  8.7 0.7 iota_compare_fusion.4
  9.4 0.6 reduce-window.6
  9.9 0.2 slice_reduce_fusion
  10.2 0.1 add_bitcast_fusion
  10.3 0.7 fusion.14
  11.0 0.7 multiply_add_fusion
  11.7 0.8 select_reduce_fusion
  12.5 0.7 all_to_all.14
  13.2 5.2 %all-to-all-start.1 = ((s32[8,1,32]{2,1,0:T(1,128)}), s32[8,1,32]{2,1,0:T(1,128)S(1)}, u32[]{:S(2)}, u32[]{:S(2)}) async-start(s32[8,1,32]{2,1,0:T(1,128)} %all_to_all.14), calls=%async_computation.1 | async-start | bytes 8192 | tf_op jit(solution)/shard_map/all_to_all | solution.py:76
  18.3 3.6 %broadcast_in_dim.48 = f32[192,4,1024]{2,1,0:T(4,128)} broadcast(bf16[192,1024]{1,0:T(8,128)(2,1)} %param.15), dimensions={0,2} | broadcast | bytes 3538944 | tf_op jit(solution)/shard_map/broadcast_in_dim | solution.py:56
  21.9 5.0 %reshape.171 = f32[768,1024]{1,0:T(8,128)} reshape(f32[192,4,1024]{2,1,0:T(4,128)} %broadcast_in_dim.48) | data formatting | bytes 6291456 | tf_op jit(solution)/shard_map/reshape | solution.py:56
  26.9 0.1 copy.45
  27.0 0.1 eq.83
  27.1 2.5 %add_convert_fusion = bf16[768,1024]{1,0:T(8,128)(2,1)S(1)} fusion(f32[768,1024]{1,0:T(8,128)} %reshape.171, bf16[128,1024]{1,0:T(8,128)(2,1)S(1)} %copy-done.2, s32[768]{0:T(1024)S(1)} %eq.83), kind=kOutput, calls=%fused_computation.11 | convolution fusion | flops 202997760 | bytes 4983808 | tf_op jit(solution)/shard_map/dot_general | solution.py:55
  29.6 2.3 %reshape.172 = bf16[192,4096]{1,0:T(8,128)(2,1)} reshape(bf16[768,1024]{1,0:T(8,128)(2,1)S(1)} %add_convert_fusion) | data formatting | bytes 3145728 | tf_op jit(solution)/shard_map/reshape | solution.py:69
  31.9 2.2 %convolution_convert_fusion = bf16[256,4096]{1,0:T(8,128)(2,1)S(1)} fusion(bf16[192,4096]{1,0:T(8,128)(2,1)} %reshape.172, s32[192]{0:T(256)S(1)} %multiply_add_fusion), kind=kOutput, calls=%fused_computation.4 | convolution fusion | flops 403849216 | bytes 3670784 | tf_op jit(solution)/shard_map/dot_general | solution.py:67
  34.1 2.6 %reshape.173 = bf16[8,128,1024]{2,1,0:T(8,128)(2,1)} reshape(bf16[256,4096]{1,0:T(8,128)(2,1)S(1)} %convolution_convert_fusion) | data formatting | bytes 4194304 | tf_op jit(solution)/shard_map/reshape | solution.py:72
  36.8 4.2 %all-to-all-start = ((bf16[8,128,1024]{2,1,0:T(8,128)(2,1)}), bf16[8,128,1024]{2,1,0:T(8,128)(2,1)S(1)}, u32[]{:S(2)}, u32[]{:S(2)}) async-start(bf16[8,128,1024]{2,1,0:T(8,128)(2,1)} %reshape.173), calls=%async_computation | async-start | bytes 4194304 | tf_op jit(solution)/shard_map/all_to_all | solution.py:75
  41.0 0.1 reshape.175
  41.1 0.5 broadcast.149
  41.6 0.7 reduce.11
  42.3 0.1 reshape.174
  42.4 1.2 gather_fusion
  43.6 0.1 select_convert_fusion
  43.7 3.1 %add.100 = f32[256,4,1024]{2,1,0:T(4,128)} broadcast(f32[256,1024]{1,0:T(8,128)S(1)} %select_convert_fusion), dimensions={0,2} | broadcast | bytes 5242880 | tf_op jit(solution)/shard_map/add | solution.py:79
  46.8 5.3 %add.101 = f32[1024,1024]{1,0:T(8,128)} reshape(f32[256,4,1024]{2,1,0:T(4,128)} %add.100) | data formatting | bytes 8388608 | tf_op jit(solution)/shard_map/add | solution.py:79
  52.2 23.5 %all-to-all-done = bf16[8,128,1024]{2,1,0:T(8,128)(2,1)S(1)} async-done(((bf16[8,128,1024]{2,1,0:T(8,128)(2,1)}), bf16[8,128,1024]{2,1,0:T(8,128)(2,1)S(1)}, u32[]{:S(2)}, u32[]{:S(2)}) %all-to-all-start) | async-done | bytes 2097184 | tf_op jit(solution)/shard_map/all_to_all | solution.py:75
  75.7 7.4 %all-gather.3.cloned.1.call-done = bf16[1024,2048]{1,0:T(8,128)(2,1)} async-done(((bf16[32,2048]{1,0:T(8,128)(2,1)}), bf16[1024,2048]{1,0:T(8,128)(2,1)}) %all-gather.3.cloned.1.call-update) | async-done | bytes 4194320 | tf_op jit(solution)/shard_map/all_gather | solution.py:13
  83.0 79.1 %all-gather.5.cloned.1.call-done = bf16[2048,2048]{1,0:T(8,128)(2,1)} async-done(((bf16[64,2048]{1,0:T(8,128)(2,1)}), bf16[2048,2048]{1,0:T(8,128)(2,1)}) %all-gather.5.cloned.1.call-update) | async-done | bytes 8388624 | tf_op jit(solution)/shard_map/all_gather | solution.py:20
  162.2 19.9 %maximum_convert_fusion = bf16[1024,2048]{1,0:T(8,128)(2,1)} fusion(bf16[2048,2048]{1,0:T(8,128)(2,1)} %all-gather.5.cloned.1.call-done, bf16[1024,2048]{1,0:T(8,128)(2,1)} %all-gather.3.cloned.1.call-done, f32[2048]{0:T(1024)S(1)} %copy-done.9, f32[2048]{0:T(1024)S(1)} %copy-done.10, f32[1024,1024]{1,0:T(8,128)} %add.101, bf16[1024,1024]{1,0:T(8,128)(2,1)S(1)} %bitcast.43), kind=kOutput, calls=%fused_computation.2 | convolution fusion | flops 12900630528 | bytes 23085056 | tf_op jit(solution)/shard_map/dot_general | solution.py:18
  182.1 3.4 %fusion.8 = bf16[1024,8]{0,1:T(8,128)(2,1)S(1)} fusion(bf16[1024,2048]{1,0:T(8,128)(2,1)} %maximum_convert_fusion, bf16[2048,8]{0,1:T(8,128)(2,1)S(1)} %copy-done.3, f32[8]{0:T(128)S(1)} %copy-done.7), kind=kOutput, calls=%fused_computation.13 | convolution fusion | flops 33570816 | bytes 4243488 | tf_op jit(solution)/shard_map/dot_general | solution.py:24
  185.5 0.2 copy.46
  185.7 0.3 convert_element_type.114
  185.9 0.5 broadcast.150
  186.5 0.7 reduce.12
  187.2 0.6 reshape.210
  187.8 3.3 %all-to-all-start.2 = ((bf16[8,2,512]{2,1,0:T(2,128)(2,1)}), bf16[8,2,512]{2,1,0:T(2,128)(2,1)S(1)}, u32[]{:S(2)}, u32[]{:S(2)}) async-start(bf16[8,2,512]{2,1,0:T(2,128)(2,1)} %reshape.210), calls=%async_computation.2 | async-start | bytes 32768 | tf_op jit(solution)/shard_map/all_to_all | solution.py:84
  191.2 0.1 max.35
  191.3 4.6 %all-to-all-done.2 = bf16[8,2,512]{2,1,0:T(2,128)(2,1)S(1)} async-done(((bf16[8,2,512]{2,1,0:T(2,128)(2,1)}), bf16[8,2,512]{2,1,0:T(2,128)(2,1)S(1)}, u32[]{:S(2)}, u32[]{:S(2)}) %all-to-all-start.2) | async-done | bytes 16416 | tf_op jit(solution)/shard_map/all_to_all | solution.py:84
  195.9 0.1 convert_reduce_fusion
  196.0 0.1 reshape.178
  196.1 0.7 gather_fusion.1
  196.8 0.1 fusion.12
  196.9 0.1 multiply_reduce_fusion
  197.1 0.6 select_reduce_fusion.1
  197.7 0.7 bitcast_multiply_fusion
  (40 shorter events, 0.4 us)
Async XLA Ops:
  7.2 35.2 %copy-start = (bf16[256,1024]{1,0:T(8,128)(2,1)S(1)}, bf16[256,1024]{1,0:T(8,128)(2,1)}, u32[]{:S(2)}) copy-start(bf16[256,1024]{1,0:T(8,128)(2,1)} %param.17) | copy-start | bytes 1572868
  7.2 75.9 %all-gather.3.cloned.1.call-start = ((), (), s32[]{:S(2)}) async-start(), calls=%async_computation.3 | async-start | bytes 4325376 | tf_op jit(solution)/shard_map/all_gather | solution.py:13
  7.9 154.3 %all-gather.5.cloned.1.call-start = ((), (), s32[]{:S(2)}) async-start(), calls=%async_computation.4 | async-start | bytes 8650752 | tf_op jit(solution)/shard_map/all_gather | solution.py:20
  13.2 23.6 %all-to-all-start.1 = ((s32[8,1,32]{2,1,0:T(1,128)}), s32[8,1,32]{2,1,0:T(1,128)S(1)}, u32[]{:S(2)}, u32[]{:S(2)}) async-start(s32[8,1,32]{2,1,0:T(1,128)} %all_to_all.14), calls=%async_computation.1 | async-start | bytes 8192 | tf_op jit(solution)/shard_map/all_to_all | solution.py:76
  18.3 8.6 %copy-start.6 = (s32[192,4]{0,1:T(4,128)S(1)}, s32[192,4]{0,1:T(4,128)}, u32[]{:S(2)}) copy-start(s32[192,4]{0,1:T(4,128)} %param.25) | copy-start | bytes 9220
  18.3 8.8 %copy-start.2 = (bf16[128,1024]{1,0:T(8,128)(2,1)S(1)}, bf16[128,1024]{1,0:T(8,128)(2,1)}, u32[]{:S(2)}) copy-start(bf16[128,1024]{1,0:T(8,128)(2,1)} %param.16) | copy-start | bytes 786436
  34.1 6.8 %copy-start.4 = (s32[192,1]{0,1:T(1,128)S(1)}, s32[192,1]{0,1:T(1,128)}, u32[]{:S(2)}) copy-start(s32[192,1]{0,1:T(1,128)} %param.26) | copy-start | bytes 2308
  34.1 6.9 %copy-start.5 = (s32[192]{0:T(256)S(1)}, s32[192]{0:T(256)}, u32[]{:S(2)}) copy-start(s32[192]{0:T(256)} %param.24) | copy-start | bytes 2308
  36.8 38.9 %all-to-all-start = ((bf16[8,128,1024]{2,1,0:T(8,128)(2,1)}), bf16[8,128,1024]{2,1,0:T(8,128)(2,1)S(1)}, u32[]{:S(2)}, u32[]{:S(2)}) async-start(bf16[8,128,1024]{2,1,0:T(8,128)(2,1)} %reshape.173), calls=%async_computation | async-start | bytes 4194304 | tf_op jit(solution)/shard_map/all_to_all | solution.py:75
  46.8 115.3 %copy-start.9 = (f32[2048]{0:T(1024)S(1)}, f32[2048]{0:T(1024)}, u32[]{:S(2)}) copy-start(f32[2048]{0:T(1024)} %param.21) | copy-start | bytes 24580
  46.8 115.3 %copy-start.10 = (f32[2048]{0:T(1024)S(1)}, f32[2048]{0:T(1024)}, u32[]{:S(2)}) copy-start(f32[2048]{0:T(1024)} %param.19) | copy-start | bytes 24580
  162.2 19.9 %copy-start.3 = (bf16[2048,8]{0,1:T(8,128)(2,1)S(1)}, bf16[2048,8]{0,1:T(8,128)(2,1)}, u32[]{:S(2)}) copy-start(bf16[2048,8]{0,1:T(8,128)(2,1)} %param.22) | copy-start | bytes 98308
  162.2 19.9 %copy-start.7 = (f32[8]{0:T(128)S(1)}, f32[8]{0:T(128)}, u32[]{:S(2)}) copy-start(f32[8]{0:T(128)} %param.23) | copy-start | bytes 100
  182.1 14.7 %copy-start.1 = (s32[192,32]{0,1:T(8,128)S(1)}, s32[192,32]{0,1:T(8,128)}, u32[]{:S(2)}) copy-start(s32[192,32]{0,1:T(8,128)} %param.28) | copy-start | bytes 73732
  182.1 14.9 %copy-start.8 = (s32[192]{0:T(256)S(1)}, s32[192]{0:T(256)}, u32[]{:S(2)}) copy-start(s32[192]{0:T(256)} %param.29) | copy-start | bytes 2308
  187.8 8.0 %all-to-all-start.2 = ((bf16[8,2,512]{2,1,0:T(2,128)(2,1)}), bf16[8,2,512]{2,1,0:T(2,128)(2,1)S(1)}, u32[]{:S(2)}, u32[]{:S(2)}) async-start(bf16[8,2,512]{2,1,0:T(2,128)(2,1)} %reshape.210), calls=%async_computation.2 | async-start | bytes 32768 | tf_op jit(solution)/shard_map/all_to_all | solution.py:84
Sparse Core Ops, SparseCore 0:
  10.9 72.1 all-gather.2
  85.9 76.2 all-gather.4
where the time goes:
time: 206 us; the launch traced here: 205 us
  waiting for transfers between devices  116 us (56%)
  matrix products  28 us (14%)
  local copies, waits for them, and re-layouts  27.4 us (13%)
  between operations  14.3 us (7%)
  starting transfers between devices  12.8 us (6%)
  other arithmetic  6.8 us (3%)
    all_gather x1, waiting for transfers between devices, network(): lax.all_gather(w_second, ('trav', 'bulk'), axis=0, tiled=True)  79.1 us
    all_to_all x1, waiting for transfers between devices, body(): lax.all_to_all(outgoing, 'bulk', split_axis=0, concat_axis=0, tiled=True)  23.5 us
    dot_general x1, matrix products, network(): jnp.dot(columns, lax.all_gather(w_second, ('trav', 'bulk'), axis=0, tiled...  19.9 us
    add x2, local copies, waits for them, and re-layouts, body(): arrived_rows.reshape(slot_total, branch_slots, feature_count)  8.47 us
    all_gather x1, waiting for transfers between devices, network(): lax.all_gather(w_first, ('trav', 'bulk'), axis=0, tiled=True)  7.4 us
    all_to_all x1, starting transfers between devices, body(): lax.all_to_all(slot_bucket, 'bulk', split_axis=0, concat_axis=0, tiled=True)  5.17 us
    reshape x1, local copies, waits for them, and re-layouts, body(): jnp.repeat(parents.astype(jnp.float32), branch_slots, axis=0) + act_rows  4.98 us
    all_to_all x1, waiting for transfers between devices, body(): lax.all_to_all(evaluated.reshape(bulk_count, capacity * branch_slots * ac...  4.58 us
  transfers between devices with their start and end apart: 5, of which 4 were waited for; matrix products, arithmetic and copies ran while one was open for 16% of the time, Pallas kernels for 0%

commit v1 on v0

v1 whole, which is shorter than its diff:
```python
import functools

import jax
import jax.numpy as jnp
from jax import lax
from jax.experimental import pallas as pl
from jax.experimental.pallas import tpu as pltpu
from jax.sharding import PartitionSpec as P

TREMBLE = 0.05
AXES = ("trav", "bulk")

X, Y, D, A, B, C = 1, 2, 3, 4, 12, 8
ROUNDS = (
    ((X, X, 0), (Y, Y, 0), (A, A, 0), (B, B, 0), (D, D, 0)),
    ((X ^ A, X, A), (Y ^ A, Y, A), (C, A, B), (X ^ B, X, B), (Y ^ B, Y, B), (D ^ B, B, D)),
    ((D ^ A, A, D), (X ^ C, X, C), (Y ^ C, Y, C), (D ^ C, A, D ^ B)),
)


def swap(value, mask):
    count = lax.axis_size("trav") * lax.axis_size("bulk")
    return lax.ppermute(value, AXES, [(i, i ^ mask) for i in range(count)])


def vmem():
    return pl.BlockSpec(memory_space=pltpu.VMEM)


def smem():
    return pl.BlockSpec(memory_space=pltpu.SMEM)


def anywhere():
    return pl.BlockSpec(memory_space=pl.ANY)


def iota(shape, dim):
    return lax.broadcasted_iota(jnp.int32, shape, dim)


def over_rows(a, b):
    return lax.dot_general(a, b, (((0,), (0,)), ((), ())), preferred_element_type=jnp.float32)


OWNER, ROW, COUNT, ANCESTOR, ACTION = 0, 1, 2, 3, 4


def slots_kernel(place, packed, slot, wanted):
    rows = packed.shape[0]
    owners, capacity = wanted.shape
    owner = packed[:, OWNER : OWNER + 1] ^ place[0]
    hits = (owner == iota((rows, owners), 1)).astype(jnp.float32)
    before = (iota((rows, rows), 1) < iota((rows, rows), 0)).astype(jnp.bfloat16)
    earlier = jnp.dot(before, hits.astype(jnp.bfloat16), preferred_element_type=jnp.float32)
    rank = jnp.sum(earlier * hits, axis=1, keepdims=True).astype(jnp.int32)
    slot[...] = owner * capacity + rank
    bucket = (hits * packed[:, ROW : ROW + 1].astype(jnp.float32)).astype(jnp.bfloat16)
    at_rank = (rank == iota((rows, capacity), 1)).astype(jnp.bfloat16)
    wanted[...] = over_rows(bucket, at_rank).astype(jnp.int32)


def rows_kernel(wants, table, *outs):
    buckets = table.shape[0]
    for want, out in zip(wants, outs):
        onehot = (iota((buckets, want.shape[1]), 0) == want).astype(jnp.bfloat16)
        out[...] = over_rows(onehot, table[...]).astype(jnp.bfloat16)


def first_kernel(capacity, sources, pieces_at, place, packed, slot, parents, act_table, bias, *rest):
    n_rows, n_pieces = len(sources), len(pieces_at)
    row_refs, pieces = rest[:n_rows], rest[n_rows : n_rows + n_pieces]
    out, weights, inputs, sems = rest[n_rows + n_pieces :]
    copies = start_pieces(place, pieces, pieces_at, weights, sems)
    rows = parents.shape[0]
    bucket = jnp.zeros(parents.shape, jnp.float32)
    for j, (ref, begin) in enumerate(zip(row_refs, sources)):
        count = capacity if begin is not None else ref.shape[0]
        begin = begin or 0
        onehot = (slot[...] == iota((rows, count), 1) + j * capacity).astype(jnp.bfloat16)
        bucket = bucket + jnp.dot(onehot, ref[begin : begin + count], preferred_element_type=jnp.float32)
    for c in range(inputs.shape[0] // rows):
        onehot = (packed[:, ACTION + c : ACTION + c + 1] == iota((rows, act_table.shape[0]), 1)).astype(jnp.bfloat16)
        change = jnp.dot(onehot, act_table[...], preferred_element_type=jnp.float32)
        base = (parents[...].astype(jnp.float32) + change).astype(jnp.bfloat16)
        inputs[c * rows : (c + 1) * rows, :] = (base.astype(jnp.float32) + bucket).astype(jnp.bfloat16)
    for copy in copies:
        copy.wait()
    step = 512
    for n in range(0, weights.shape[1], step):
        total = jnp.dot(inputs[...], weights[:, n : n + step], preferred_element_type=jnp.float32)
        out[:, n : n + step] = jnp.maximum(total + bias[:, n : n + step], 0.0).astype(jnp.bfloat16)


def start_pieces(place, pieces, pieces_at, weights, sems):
    copies = []
    for j, (piece, (begin, count)) in enumerate(zip(pieces, pieces_at)):
        to = pl.multiple_of((place[1] ^ j) * count, count)
        copies.append(
            pltpu.make_async_copy(piece.at[pl.ds(begin, count)], weights.at[pl.ds(to, count)], sems.at[j])
        )
    for copy in copies:
        copy.start()
    return copies


def second_kernel(pieces_at, place, packed, hidden, bias, w_head, b_head, legal, *rest):
    n_pieces = len(pieces_at)
    pieces = rest[:n_pieces]
    strategy, values, weights, sems = rest[n_pieces:]
    copies = start_pieces(place, pieces, pieces_at, weights, sems)
    for copy in copies:
        copy.wait()
    actions = w_head.shape[1]
    rows = packed.shape[0]
    advantage = jnp.zeros((hidden.shape[0], actions), jnp.float32)
    step = 512
    for n in range(0, weights.shape[1], step):
        total = jnp.dot(hidden[...], weights[:, n : n + step], preferred_element_type=jnp.float32)
        layer = jnp.maximum(total + bias[:, n : n + step], 0.0).astype(jnp.bfloat16)
        advantage = advantage + jnp.dot(layer, w_head[n : n + step, :], preferred_element_type=jnp.float32)
    advantage = advantage + b_head[...]
    counts = packed[:, COUNT : COUNT + 1]
    first_action = (iota((rows, actions), 1) == 0).astype(jnp.float32)
    total_value = jnp.zeros((rows, 1), jnp.float32)
    for c in range(hidden.shape[0] // rows):
        mine = advantage[c * rows : (c + 1) * rows, :]
        allowed = jnp.maximum(legal[:, c * actions : (c + 1) * actions].astype(jnp.float32), first_action)
        positive = allowed * (jnp.maximum(mine, 0.0) + TREMBLE)
        sigma = positive / jnp.sum(positive, axis=1, keepdims=True)
        live = (counts > c).astype(jnp.float32)
        strategy[:, c * actions : (c + 1) * actions] = sigma * live
        total_value = total_value + live * jnp.sum(sigma * mine, axis=1, keepdims=True)
    value = total_value / counts.astype(jnp.float32)
    nodes = values.shape[1]
    at_node = (packed[:, ANCESTOR : ANCESTOR + 1] == iota((rows, nodes), 1)).astype(jnp.float32)
    values[...] = jnp.sum(at_node * value, axis=0, keepdims=True)


def limit(mebibytes):
    return pltpu.CompilerParams(vmem_limit_bytes=mebibytes << 20)


def body(
    parents,
    act_table,
    bucket_table,
    w_first,
    b_first,
    w_second,
    b_second,
    w_head,
    b_head,
    branch_counts,
    sampled_actions,
    bucket_owner,
    bucket_row,
    legal_mask,
    ancestor,
):
    par_count, feature_count = parents.shape
    branch_slots = sampled_actions.shape[1]
    hidden_units = w_first.shape[1]
    bulk_count, trav_count = lax.axis_size("bulk"), lax.axis_size("trav")
    devices = bulk_count * trav_count
    capacity = max(2, (4 * par_count + 3 * bulk_count - 1) // (3 * bulk_count))
    by_xor = (trav_count, bulk_count) == (4, 8)
    bulk_index = lax.axis_index("bulk")
    index = lax.axis_index("trav") * bulk_count + bulk_index
    zero = jnp.zeros_like(index)
    place = jnp.stack([bulk_index, index] if by_xor else [zero, zero]).astype(jnp.int32)

    packed = jnp.concatenate(
        [bucket_owner, bucket_row[:, None], branch_counts[:, None], ancestor[:, None], sampled_actions], axis=1
    )

    w_both = jnp.concatenate([w_first, w_second], axis=0)
    depth_one, depth_two = w_first.shape[0], w_second.shape[0]

    slot, wanted = pl.pallas_call(
        slots_kernel,
        out_shape=(
            jax.ShapeDtypeStruct((par_count, 1), jnp.int32),
            jax.ShapeDtypeStruct((bulk_count, capacity), jnp.int32),
        ),
        in_specs=[smem(), vmem()],
        out_specs=(vmem(), vmem()),
    )(place, packed)

    if by_xor:
        held = {0: w_both}
        for arriving, partner, piece in ROUNDS[0]:
            held[arriving] = swap(held[piece], partner << 1)

        both = jnp.concatenate([wanted, swap(wanted, 1)], axis=0)
        asked = {0: both}
        for chip in (X, Y, D):
            asked[chip] = swap(both, chip << 1)

        def serve(ids_0, ids_x, ids_y, ids_d, table, *outs):
            wants = []
            for chip, ids in zip((0, X, Y, D), (ids_0, ids_x, ids_y, ids_d)):
                mine = [ids[bulk_count * core + 2 * chip + core : bulk_count * core + 2 * chip + core + 1, :] for core in (0, 1)]
                wants.append(jnp.concatenate(mine, axis=1))
            rows_kernel(wants, table, *outs)

        served = pl.pallas_call(
            serve,
            out_shape=(jax.ShapeDtypeStruct((2 * capacity, feature_count), jnp.bfloat16),) * 4,
            in_specs=[vmem()] * 5,
            out_specs=(vmem(),) * 4,
        )(*(asked[chip] for chip in (0, X, Y, D)), bucket_table)
        row_arrays, sources = [], []
        for chip, rows in zip((0, X, Y, D), served):
            mine = swap(rows, chip << 1) if chip else rows
            row_arrays += [mine, swap(mine, 1)]
            sources += [0, capacity]

        for arrivals in ROUNDS[1:]:
            for arriving, partner, piece in arrivals:
                held[arriving] = swap(held[piece], partner << 1)
        pieces = []
        for chip in range(devices // 2):
            pieces += [held[chip], swap(held[chip], 1)]
        first_at = [(0, depth_one)] * devices
        second_at = [(depth_one, depth_two)] * devices
        first_pieces = second_pieces = pieces
    else:
        asked = lax.all_to_all(wanted, "bulk", split_axis=0, concat_axis=0, tiled=True)
        served = jnp.take(bucket_table, asked.reshape(-1), axis=0)
        served = served.reshape(bulk_count, capacity, feature_count)
        arrived = lax.all_to_all(served, "bulk", split_axis=0, concat_axis=0, tiled=True)
        row_arrays, sources = [arrived.reshape(bulk_count * capacity, feature_count)], [None]
        first_pieces = [lax.all_gather(w_first, AXES, axis=0, tiled=True)]
        second_pieces = [lax.all_gather(w_second, AXES, axis=0, tiled=True)]
        first_at = [(0, first_pieces[0].shape[0])]
        second_at = [(0, second_pieces[0].shape[0])]

    branches = par_count * branch_slots
    hidden = pl.pallas_call(
        functools.partial(first_kernel, capacity, sources, first_at),
        out_shape=jax.ShapeDtypeStruct((branches, hidden_units), jnp.bfloat16),
        in_specs=[smem()] + [vmem()] * (5 + len(row_arrays)) + [anywhere()] * len(first_pieces),
        out_specs=vmem(),
        scratch_shapes=[
            pltpu.VMEM((feature_count, hidden_units), jnp.bfloat16),
            pltpu.VMEM((branches, feature_count), jnp.bfloat16),
            pltpu.SemaphoreType.DMA((len(first_pieces),)),
        ],
        compiler_params=limit(24),
    )(place, packed, slot, parents, act_table, b_first[None, :], *row_arrays, *first_pieces)

    node_count = par_count // 4
    strategy, values = pl.pallas_call(
        functools.partial(second_kernel, second_at),
        out_shape=(
            jax.ShapeDtypeStruct(legal_mask.shape, jnp.float32),
            jax.ShapeDtypeStruct((1, node_count), jnp.float32),
        ),
        in_specs=[smem()] + [vmem()] * 6 + [anywhere()] * len(second_pieces),
        out_specs=(vmem(), vmem()),
        scratch_shapes=[
            pltpu.VMEM((hidden_units, hidden_units), jnp.bfloat16),
            pltpu.SemaphoreType.DMA((len(second_pieces),)),
        ],
        compiler_params=limit(28),
    )(place, packed, hidden, b_second[None, :], w_head, b_head[None, :], legal_mask, *second_pieces)
    return (strategy, values.reshape(-1))


def solution(mesh):
    return jax.shard_map(
        body,
        mesh=mesh,
        in_specs=(
            P(AXES, None),
            P(),
            P("bulk", None),
            P(AXES, None),
            P(),
            P(AXES, None),
            P(),
            P(),
            P(),
            P(AXES),
            P(AXES, None),
            P(AXES, None),
            P(AXES),
            P(AXES, None),
            P(AXES),
        ),
        out_specs=(P(AXES, None), P(AXES)),
        check_vma=False,
    )
```

time: 206 us -> 150 us (0.73)
  waiting for transfers between devices: 116 us -> 42.9 us
  matrix products: 28 us -> 0 us
  Pallas kernels: 0 us -> 27.7 us
  local copies, waits for them, and re-layouts: 27.4 us -> 50.1 us
  between operations: 14.3 us -> 1.02 us
  starting transfers between devices: 12.8 us -> 25.9 us
  other arithmetic: 6.8 us -> 0.59 us
    all_gather x2 -> x0, waiting for transfers between devices: 86.5 us -> none  [the longest x1 79.1 us: network(): lax.all_gather(w_second, ('trav', 'bulk'), axis=0, tiled=True)]
    unnamed x25 -> x139, local copies, waits for them, and re-layouts: 0.81 us -> 47.6 us
    ppermute x0 -> x42, waiting for transfers between devices: none -> 42.9 us  [swap(): return lax.ppermute(value, AXES, [(i, i ^ mask) for i in range(count)])]
    all_to_all x3 -> x0, waiting for transfers between devices: 28.1 us -> none  [the longest x1 23.5 us: body(): lax.all_to_all(outgoing, 'bulk', split_axis=0, concat_axis=0, tiled=True)]
    dot_general x4 -> x0, matrix products: 28 us -> none  [the longest x1 19.9 us: network(): jnp.dot(columns, lax.all_gather(w_second, ('trav', 'bulk'), axis=0, tiled...]
    pallas_call x0 -> x4, Pallas kernels: none -> 27.7 us  [the longest x1 12.9 us: body(): pl.pallas_call(functools.partial(second_kernel, second_at), out_shape=(ja...]
    ppermute x0 -> x42, starting transfers between devices: none -> 25.9 us  [swap(): return lax.ppermute(value, AXES, [(i, i ^ mask) for i in range(count)])]
    all_to_all x3 -> x0, starting transfers between devices: 12.7 us -> none  [the longest x1 5.17 us: body(): lax.all_to_all(slot_bucket, 'bulk', split_axis=0, concat_axis=0, tiled=True)]
  transfers between devices with their start and end apart: 5 -> 42, of which waited for: 4 -> 14; matrix products, arithmetic and copies ran while one was open for 16% -> 3% of each run, Pallas kernels for 0% -> 2%
where the time goes in v1:
time: 150 us; the launch traced here: 148 us
  local copies, waits for them, and re-layouts  50.1 us (33%)
  waiting for transfers between devices  42.9 us (29%)
  Pallas kernels  27.7 us (18%)
  starting transfers between devices  25.9 us (17%)
    unnamed x139, local copies, waits for them, and re-layouts  47.6 us
    ppermute x42, waiting for transfers between devices, swap(): return lax.ppermute(value, AXES, [(i, i ^ mask) for i in range(count)])  42.9 us
    ppermute x42, starting transfers between devices, swap(): return lax.ppermute(value, AXES, [(i, i ^ mask) for i in range(count)])  25.9 us
    pallas_call x1, Pallas kernels, body(): pl.pallas_call(functools.partial(second_kernel, second_at), out_shape=(ja...  12.9 us
    pallas_call x1, Pallas kernels, body(): pl.pallas_call(functools.partial(first_kernel, capacity, sources, first_a...  10.5 us
  transfers between devices with their start and end apart: 42, of which 14 were waited for; matrix products, arithmetic and copies ran while one was open for 3% of the time, Pallas kernels for 2%

profile of v1, /device:TPU:0, one launch (start us, length us, event | category | flops | bytes accessed | tf_op | source)
XLA Modules:
  0.0 148.2 jit_solution(1441045778932716720)
XLA Ops:
  2.8 2.0 %shard_map.158 = (s32[192,1]{1,0:T(8,128)}, s32[8,32]{1,0:T(8,128)}) custom-call(s32[2]{0:T(128)} %pad_add_fusion.place, s32[192,8]{1,0:T(8,128)} %copy.32.packed), custom_call_target="tpu_custom_call" | custom-call | tf_op jit(solution)/shard_map/pallas_call | solution.py:180
  5.2 0.9 constant_dynamic-update-slice_fusion.3
  6.1 1.0 constant_dynamic-update-slice_fusion.2.rest_8_.rest_0_
  7.0 4.7 %collective-permute-start.26 = (bf16[96,2048]{1,0:T(8,128)(2,1)S(1)}, bf16[96,2048]{1,0:T(8,128)(2,1)S(1)}, u32[]{:S(2)}, u32[]{:S(2)}) collective-permute-start(bf16[96,2048]{1,0:T(8,128)(2,1)S(1)} %constant_dynamic-update-slice_fusion.2.rest_8_.rest_0_), channel_id=1, source_target_pairs={{0,24},{1,25},{2,26},{3,27},{4,28},{5,29},{6,30},{7,31},{8,16},{9,... | collective-permute-start | bytes 1179656 | tf_op jit(solution)/shard_map/ppermute | solution.py:23
  12.4 1.6 %collective-permute-start.1 = (s32[16,32]{1,0:T(8,128)S(1)}, s32[16,32]{1,0:T(8,128)S(1)}, u32[]{:S(2)}, u32[]{:S(2)}) collective-permute-start(s32[16,32]{1,0:T(8,128)S(1)} %constant_dynamic-update-slice_fusion.ids_0), channel_id=1, source_target_pairs={{0,2},{1,3},{2,0},{3,1},{4,6},{5,7},{6,4},{7,5},{8,10},{9,11},{10,... | collective-permute-start | bytes 6152 | tf_op jit(solution)/shard_map/ppermute | solution.py:23
  14.0 1.5 %collective-permute-start.2 = (s32[16,32]{1,0:T(8,128)S(1)}, s32[16,32]{1,0:T(8,128)S(1)}, u32[]{:S(2)}, u32[]{:S(2)}) collective-permute-start(s32[16,32]{1,0:T(8,128)S(1)} %constant_dynamic-update-slice_fusion.ids_0), channel_id=1, source_target_pairs={{0,4},{1,5},{2,6},{3,7},{4,0},{5,1},{6,2},{7,3},{8,12},{9,13},{10,... | collective-permute-start | bytes 6152 | tf_op jit(solution)/shard_map/ppermute | solution.py:23
  16.1 1.5 %collective-permute-done.2.ids_y = s32[16,32]{1,0:T(8,128)S(1)} collective-permute-done((s32[16,32]{1,0:T(8,128)S(1)}, s32[16,32]{1,0:T(8,128)S(1)}, u32[]{:S(2)}, u32[]{:S(2)}) %collective-permute-start.2) | collective-permute-done | bytes 2080 | tf_op jit(solution)/shard_map/ppermute | solution.py:23
  17.6 2.4 %collective-permute-done.3.ids_d = s32[16,32]{1,0:T(8,128)S(1)} collective-permute-done((s32[16,32]{1,0:T(8,128)S(1)}, s32[16,32]{1,0:T(8,128)S(1)}, u32[]{:S(2)}, u32[]{:S(2)}) %collective-permute-start.3) | collective-permute-done | bytes 2080 | tf_op jit(solution)/shard_map/ppermute | solution.py:23
  20.6 2.4 %shard_map.159 = (bf16[64,1024]{1,0:T(8,128)(2,1)}, bf16[64,1024]{1,0:T(8,128)(2,1)}, bf16[64,1024]{1,0:T(8,128)(2,1)}, bf16[64,1024]{1,0:T(8,128)(2,1)}) custom-call(s32[16,32]{1,0:T(8,128)} %copy-done.63, s32[16,32]{1,0:T(8,128)} %copy-done.64, s32[16,32]{1,0:T(8,128)} %copy-done.65, s32[16,32]{1,0:T(8,128)} %copy-done.66, bf16[256,1024]{1,0:T(8,128)(2,1)} %table.1), custom_call_target="tpu_custom_call" | custom-call | tf_op jit(solution)/shard_map/pallas_call | solution.py:207
  23.5 1.5 %collective-permute-start.5 = (bf16[64,1024]{1,0:T(8,128)(2,1)}, bf16[64,1024]{1,0:T(8,128)(2,1)S(1)}, u32[]{:S(2)}, u32[]{:S(2)}) collective-permute-start(bf16[64,1024]{1,0:T(8,128)(2,1)} %get-tuple-element.13), channel_id=1, source_target_pairs={{0,2},{1,3},{2,0},{3,1},{4,6},{5,7},{6,4},{7,5},{8,10},{9,11},{10,... | collective-permute-start | bytes 393224 | tf_op jit(solution)/shard_map/ppermute | solution.py:23
  25.0 1.5 %collective-permute-start.7 = (bf16[64,1024]{1,0:T(8,128)(2,1)}, bf16[64,1024]{1,0:T(8,128)(2,1)S(1)}, u32[]{:S(2)}, u32[]{:S(2)}) collective-permute-start(bf16[64,1024]{1,0:T(8,128)(2,1)} %get-tuple-element.14), channel_id=1, source_target_pairs={{0,4},{1,5},{2,6},{3,7},{4,0},{5,1},{6,2},{7,3},{8,12},{9,13},{10,... | collective-permute-start | bytes 393224 | tf_op jit(solution)/shard_map/ppermute | solution.py:23
  26.5 3.3 %collective-permute-done.9.rest_6_ = bf16[64,1024]{1,0:T(8,128)(2,1)S(1)} collective-permute-done((bf16[64,1024]{1,0:T(8,128)(2,1)}, bf16[64,1024]{1,0:T(8,128)(2,1)S(1)}, u32[]{:S(2)}, u32[]{:S(2)}) %collective-permute-start.9) | collective-permute-done | bytes 131104 | tf_op jit(solution)/shard_map/ppermute | solution.py:23
  32.6 1.5 %collective-permute-start.16 = (bf16[96,2048]{1,0:T(8,128)(2,1)S(1)}, bf16[96,2048]{1,0:T(8,128)(2,1)S(1)}, u32[]{:S(2)}, u32[]{:S(2)}) collective-permute-start(bf16[96,2048]{1,0:T(8,128)(2,1)S(1)} %constant_dynamic-update-slice_fusion.2.rest_8_.rest_0_), channel_id=1, source_target_pairs={{0,6},{1,7},{2,4},{3,5},{4,2},{5,3},{6,0},{7,1},{8,14},{9,15},{10,... | collective-permute-start | bytes 1179656 | tf_op jit(solution)/shard_map/ppermute | solution.py:23
  35.5 1.5 %collective-permute-start.12 = (bf16[96,2048]{1,0:T(8,128)(2,1)S(1)}, bf16[96,2048]{1,0:T(8,128)(2,1)S(1)}, u32[]{:S(2)}, u32[]{:S(2)}) collective-permute-start(bf16[96,2048]{1,0:T(8,128)(2,1)S(1)} %constant_dynamic-update-slice_fusion.2.rest_8_.rest_0_), channel_id=1, source_target_pairs={{0,2},{1,3},{2,0},{3,1},{4,6},{5,7},{6,4},{7,5},{8,10},{9,11},{10,... | collective-permute-start | bytes 1179656 | tf_op jit(solution)/shard_map/ppermute | solution.py:23
  38.1 7.4 %collective-permute-done.16.rest_14_.rest_6_ = bf16[96,2048]{1,0:T(8,128)(2,1)S(1)} collective-permute-done((bf16[96,2048]{1,0:T(8,128)(2,1)S(1)}, bf16[96,2048]{1,0:T(8,128)(2,1)S(1)}, u32[]{:S(2)}, u32[]{:S(2)}) %collective-permute-start.16) | collective-permute-done | bytes 393248 | tf_op jit(solution)/shard_map/ppermute | solution.py:23
  46.2 6.9 %collective-permute-done.12.rest_10_.rest_2_ = bf16[96,2048]{1,0:T(8,128)(2,1)S(1)} collective-permute-done((bf16[96,2048]{1,0:T(8,128)(2,1)S(1)}, bf16[96,2048]{1,0:T(8,128)(2,1)S(1)}, u32[]{:S(2)}, u32[]{:S(2)}) %collective-permute-start.12) | collective-permute-done | bytes 393248 | tf_op jit(solution)/shard_map/ppermute | solution.py:23
  54.5 1.4 collective-permute-start.20
  55.9 7.9 %collective-permute-done.27.rest_24_.rest_16_ = bf16[96,2048]{1,0:T(8,128)(2,1)S(1)} collective-permute-done((bf16[96,2048]{1,0:T(8,128)(2,1)S(1)}, bf16[96,2048]{1,0:T(8,128)(2,1)S(1)}, u32[]{:S(2)}, u32[]{:S(2)}) %collective-permute-start.27) | collective-permute-done | bytes 393248 | tf_op jit(solution)/shard_map/ppermute | solution.py:23
  63.9 2.1 %collective-permute-start.22 = (bf16[96,2048]{1,0:T(8,128)(2,1)S(1)}, bf16[96,2048]{1,0:T(8,128)(2,1)}, u32[]{:S(2)}, u32[]{:S(2)}) collective-permute-start(bf16[96,2048]{1,0:T(8,128)(2,1)S(1)} %collective-permute-done.18.rest_16_.rest_8_), channel_id=1, source_target_pairs={{0,4},{1,5},{2,6},{3,7},{4,0},{5,1},{6,2},{7,3},{8,12},{9,13},{10,... | collective-permute-start | bytes 1179656 | tf_op jit(solution)/shard_map/ppermute | solution.py:23
  66.5 5.2 %collective-permute-done.20.rest_18_.rest_10_ = bf16[96,2048]{1,0:T(8,128)(2,1)S(1)} collective-permute-done((bf16[96,2048]{1,0:T(8,128)(2,1)S(1)}, bf16[96,2048]{1,0:T(8,128)(2,1)S(1)}, u32[]{:S(2)}, u32[]{:S(2)}) %collective-permute-start.20) | collective-permute-done | bytes 393248 | tf_op jit(solution)/shard_map/ppermute | solution.py:23
  71.7 1.2 collective-permute-done.22.rest_20_.rest_12_
  72.9 0.9 collective-permute-done.24.rest_22_.rest_14_
  81.1 5.2 %collective-permute-done.29.rest_26_.rest_18_ = bf16[96,2048]{1,0:T(8,128)(2,1)} collective-permute-done((bf16[96,2048]{1,0:T(8,128)(2,1)S(1)}, bf16[96,2048]{1,0:T(8,128)(2,1)}, u32[]{:S(2)}, u32[]{:S(2)}) %collective-permute-start.29) | collective-permute-done | bytes 393248 | tf_op jit(solution)/shard_map/ppermute | solution.py:23
  94.4 1.0 copy.33.w_head
  97.2 1.0 copy-done.3
  98.2 1.0 copy-done.6
  99.2 1.0 copy-done.8
  100.2 1.0 copy-done.11
  101.2 1.0 copy-done.14
  102.2 1.0 copy-done.17
  103.2 1.0 copy-done.20
  104.2 1.0 copy-done.22
  105.2 1.0 copy-done.25
  106.2 1.0 copy-done.28
  107.2 1.0 copy-done.31
  108.2 1.0 copy-done.34
  109.2 1.0 copy-done.36
  110.2 1.0 copy-done.39
  111.2 1.0 copy-done.41
  112.2 1.0 copy-done.42
  113.2 0.9 copy-done.43
  114.1 0.9 copy-done.44
  115.0 0.9 copy-done.46
  115.9 0.9 copy-done.48
  117.7 0.9 copy-done.52
  118.6 0.9 copy-done.54
  122.7 10.5 %shard_map.160.hidden = bf16[768,2048]{1,0:T(8,128)(2,1)S(1)} custom-call(s32[2]{0:T(128)S(1)} %copy-done.60, s32[192,8]{1,0:T(8,128)S(1)} %copy-done, s32[192,1]{1,0:T(8,128)S(1)} %copy-done.57, bf16[192,1024]{1,0:T(8,128)(2,1)S(1)} %copy-done.42, bf16[128,1024]{1,0:T(8,128)(2,1)S(1)} %copy-done.43, f32[1,2048]{1,0:T(1,128)S(1)} %bitcast.9, ...), custom_call_target="tpu_custom_call" | custom-call | tf_op jit(solution)/shard_map/pallas_call | solution.py:240
  134.6 12.9 %shard_map.161 = (f32[192,32]{1,0:T(8,128)S(1)}, f32[1,48]{1,0:T(1,128)}) custom-call(s32[2]{0:T(128)S(1)} %copy-done.61, s32[192,8]{1,0:T(8,128)S(1)} %copy-done.1, bf16[768,2048]{1,0:T(8,128)(2,1)S(1)} %shard_map.160.hidden, f32[1,2048]{1,0:T(1,128)S(1)} %bitcast.10, bf16[2048,8]{1,0:T(8,128)(2,1)S(1)} %copy.33.w_head, f32[1,8]{1,0:T(1,128)S(1)} %bitcast.11, ...), custom_call_target="tpu_custom_call" | custom-call | tf_op jit(solution)/shard_map/pallas_call | solution.py:254
  (184 shorter events, 36.1 us)
Async XLA Ops:
  4.7 7.7 %collective-permute-start = (s32[8,32]{1,0:T(8,128)}, s32[8,32]{1,0:T(8,128)S(1)}, u32[]{:S(2)}, u32[]{:S(2)}) collective-permute-start(s32[8,32]{1,0:T(8,128)} %get-tuple-element.11), channel_id=1, source_target_pairs={{0,1},{1,0},{2,3},{3,2},{4,5},{5,4},{6,7},{7,6},{8,9},{9,8},{10,11... | collective-permute-start | bytes 3080 | tf_op jit(solution)/shard_map/ppermute | solution.py:23
  7.0 31.0 %collective-permute-start.26 = (bf16[96,2048]{1,0:T(8,128)(2,1)S(1)}, bf16[96,2048]{1,0:T(8,128)(2,1)S(1)}, u32[]{:S(2)}, u32[]{:S(2)}) collective-permute-start(bf16[96,2048]{1,0:T(8,128)(2,1)S(1)} %constant_dynamic-update-slice_fusion.2.rest_8_.rest_0_), channel_id=1, source_target_pairs={{0,24},{1,25},{2,26},{3,27},{4,28},{5,29},{6,30},{7,31},{8,16},{9,... | collective-permute-start | bytes 1179656 | tf_op jit(solution)/shard_map/ppermute | solution.py:23
  12.4 3.7 %collective-permute-start.1 = (s32[16,32]{1,0:T(8,128)S(1)}, s32[16,32]{1,0:T(8,128)S(1)}, u32[]{:S(2)}, u32[]{:S(2)}) collective-permute-start(s32[16,32]{1,0:T(8,128)S(1)} %constant_dynamic-update-slice_fusion.ids_0), channel_id=1, source_target_pairs={{0,2},{1,3},{2,0},{3,1},{4,6},{5,7},{6,4},{7,5},{8,10},{9,11},{10,... | collective-permute-start | bytes 6152 | tf_op jit(solution)/shard_map/ppermute | solution.py:23
  14.0 3.7 %collective-permute-start.2 = (s32[16,32]{1,0:T(8,128)S(1)}, s32[16,32]{1,0:T(8,128)S(1)}, u32[]{:S(2)}, u32[]{:S(2)}) collective-permute-start(s32[16,32]{1,0:T(8,128)S(1)} %constant_dynamic-update-slice_fusion.ids_0), channel_id=1, source_target_pairs={{0,4},{1,5},{2,6},{3,7},{4,0},{5,1},{6,2},{7,3},{8,12},{9,13},{10,... | collective-permute-start | bytes 6152 | tf_op jit(solution)/shard_map/ppermute | solution.py:23
  15.5 4.5 %collective-permute-start.3 = (s32[16,32]{1,0:T(8,128)S(1)}, s32[16,32]{1,0:T(8,128)S(1)}, u32[]{:S(2)}, u32[]{:S(2)}) collective-permute-start(s32[16,32]{1,0:T(8,128)S(1)} %constant_dynamic-update-slice_fusion.ids_0), channel_id=1, source_target_pairs={{0,6},{1,7},{2,4},{3,5},{4,2},{5,3},{6,0},{7,1},{8,14},{9,15},{10,... | collective-permute-start | bytes 6152 | tf_op jit(solution)/shard_map/ppermute | solution.py:23
  23.0 6.8 %collective-permute-start.9 = (bf16[64,1024]{1,0:T(8,128)(2,1)}, bf16[64,1024]{1,0:T(8,128)(2,1)S(1)}, u32[]{:S(2)}, u32[]{:S(2)}) collective-permute-start(bf16[64,1024]{1,0:T(8,128)(2,1)} %get-tuple-element.15), channel_id=1, source_target_pairs={{0,6},{1,7},{2,4},{3,5},{4,2},{5,3},{6,0},{7,1},{8,14},{9,15},{10,... | collective-permute-start | bytes 393224 | tf_op jit(solution)/shard_map/ppermute | solution.py:23
  23.5 6.7 %collective-permute-start.5 = (bf16[64,1024]{1,0:T(8,128)(2,1)}, bf16[64,1024]{1,0:T(8,128)(2,1)S(1)}, u32[]{:S(2)}, u32[]{:S(2)}) collective-permute-start(bf16[64,1024]{1,0:T(8,128)(2,1)} %get-tuple-element.13), channel_id=1, source_target_pairs={{0,2},{1,3},{2,0},{3,1},{4,6},{5,7},{6,4},{7,5},{8,10},{9,11},{10,... | collective-permute-start | bytes 393224 | tf_op jit(solution)/shard_map/ppermute | solution.py:23
  25.0 6.2 %collective-permute-start.7 = (bf16[64,1024]{1,0:T(8,128)(2,1)}, bf16[64,1024]{1,0:T(8,128)(2,1)S(1)}, u32[]{:S(2)}, u32[]{:S(2)}) collective-permute-start(bf16[64,1024]{1,0:T(8,128)(2,1)} %get-tuple-element.14), channel_id=1, source_target_pairs={{0,4},{1,5},{2,6},{3,7},{4,0},{5,1},{6,2},{7,3},{8,12},{9,13},{10,... | collective-permute-start | bytes 393224 | tf_op jit(solution)/shard_map/ppermute | solution.py:23
  26.5 5.5 %collective-permute-start.4 = (bf16[64,1024]{1,0:T(8,128)(2,1)}, bf16[64,1024]{1,0:T(8,128)(2,1)S(1)}, u32[]{:S(2)}, u32[]{:S(2)}) collective-permute-start(bf16[64,1024]{1,0:T(8,128)(2,1)} %get-tuple-element.12.rest_0_), channel_id=1, source_target_pairs={{0,1},{1,0},{2,3},{3,2},{4,5},{5,4},{6,7},{7,6},{8,9},{9,8},{10,11... | collective-permute-start | bytes 393224 | tf_op jit(solution)/shard_map/ppermute | solution.py:23
  29.8 4.3 %collective-permute-start.10 = (bf16[64,1024]{1,0:T(8,128)(2,1)S(1)}, bf16[64,1024]{1,0:T(8,128)(2,1)S(1)}, u32[]{:S(2)}, u32[]{:S(2)}) collective-permute-start(bf16[64,1024]{1,0:T(8,128)(2,1)S(1)} %collective-permute-done.9.rest_6_), channel_id=1, source_target_pairs={{0,1},{1,0},{2,3},{3,2},{4,5},{5,4},{6,7},{7,6},{8,9},{9,8},{10,11... | collective-permute-start | bytes 393224 | tf_op jit(solution)/shard_map/ppermute | solution.py:23
  30.2 4.6 %collective-permute-start.6 = (bf16[64,1024]{1,0:T(8,128)(2,1)S(1)}, bf16[64,1024]{1,0:T(8,128)(2,1)S(1)}, u32[]{:S(2)}, u32[]{:S(2)}) collective-permute-start(bf16[64,1024]{1,0:T(8,128)(2,1)S(1)} %collective-permute-done.5.rest_2_), channel_id=1, source_target_pairs={{0,1},{1,0},{2,3},{3,2},{4,5},{5,4},{6,7},{7,6},{8,9},{9,8},{10,11... | collective-permute-start | bytes 393224 | tf_op jit(solution)/shard_map/ppermute | solution.py:23
  31.1 5.8 %collective-permute-start.8 = (bf16[64,1024]{1,0:T(8,128)(2,1)S(1)}, bf16[64,1024]{1,0:T(8,128)(2,1)S(1)}, u32[]{:S(2)}, u32[]{:S(2)}) collective-permute-start(bf16[64,1024]{1,0:T(8,128)(2,1)S(1)} %collective-permute-done.7.rest_4_), channel_id=1, source_target_pairs={{0,1},{1,0},{2,3},{3,2},{4,5},{5,4},{6,7},{7,6},{8,9},{9,8},{10,11... | collective-permute-start | bytes 393224 | tf_op jit(solution)/shard_map/ppermute | solution.py:23
  32.6 12.9 %collective-permute-start.16 = (bf16[96,2048]{1,0:T(8,128)(2,1)S(1)}, bf16[96,2048]{1,0:T(8,128)(2,1)S(1)}, u32[]{:S(2)}, u32[]{:S(2)}) collective-permute-start(bf16[96,2048]{1,0:T(8,128)(2,1)S(1)} %constant_dynamic-update-slice_fusion.2.rest_8_.rest_0_), channel_id=1, source_target_pairs={{0,6},{1,7},{2,4},{3,5},{4,2},{5,3},{6,0},{7,1},{8,14},{9,15},{10,... | collective-permute-start | bytes 1179656 | tf_op jit(solution)/shard_map/ppermute | solution.py:23
  34.8 10.7 %collective-permute-start.18 = (bf16[96,2048]{1,0:T(8,128)(2,1)S(1)}, bf16[96,2048]{1,0:T(8,128)(2,1)S(1)}, u32[]{:S(2)}, u32[]{:S(2)}) collective-permute-start(bf16[96,2048]{1,0:T(8,128)(2,1)S(1)} %constant_dynamic-update-slice_fusion.2.rest_8_.rest_0_), channel_id=1, source_target_pairs={{0,8},{1,9},{2,10},{3,11},{4,12},{5,13},{6,14},{7,15},{8,0},{9,1},... | collective-permute-start | bytes 1179656 | tf_op jit(solution)/shard_map/ppermute | solution.py:23
  35.5 17.6 %collective-permute-start.12 = (bf16[96,2048]{1,0:T(8,128)(2,1)S(1)}, bf16[96,2048]{1,0:T(8,128)(2,1)S(1)}, u32[]{:S(2)}, u32[]{:S(2)}) collective-permute-start(bf16[96,2048]{1,0:T(8,128)(2,1)S(1)} %constant_dynamic-update-slice_fusion.2.rest_8_.rest_0_), channel_id=1, source_target_pairs={{0,2},{1,3},{2,0},{3,1},{4,6},{5,7},{6,4},{7,5},{8,10},{9,11},{10,... | collective-permute-start | bytes 1179656 | tf_op jit(solution)/shard_map/ppermute | solution.py:23
  37.6 16.0 %collective-permute-start.14 = (bf16[96,2048]{1,0:T(8,128)(2,1)S(1)}, bf16[96,2048]{1,0:T(8,128)(2,1)S(1)}, u32[]{:S(2)}, u32[]{:S(2)}) collective-permute-start(bf16[96,2048]{1,0:T(8,128)(2,1)S(1)} %constant_dynamic-update-slice_fusion.2.rest_8_.rest_0_), channel_id=1, source_target_pairs={{0,4},{1,5},{2,6},{3,7},{4,0},{5,1},{6,2},{7,3},{8,12},{9,13},{10,... | collective-permute-start | bytes 1179656 | tf_op jit(solution)/shard_map/ppermute | solution.py:23
  38.1 16.4 %collective-permute-start.11 = (bf16[96,2048]{1,0:T(8,128)(2,1)S(1)}, bf16[96,2048]{1,0:T(8,128)(2,1)S(1)}, u32[]{:S(2)}, u32[]{:S(2)}) collective-permute-start(bf16[96,2048]{1,0:T(8,128)(2,1)S(1)} %constant_dynamic-update-slice_fusion.2.rest_8_.rest_0_), channel_id=1, source_target_pairs={{0,1},{1,0},{2,3},{3,2},{4,5},{5,4},{6,7},{7,6},{8,9},{9,8},{10,11... | collective-permute-start | bytes 1179656 | tf_op jit(solution)/shard_map/ppermute | solution.py:23
  45.5 18.3 %collective-permute-start.27 = (bf16[96,2048]{1,0:T(8,128)(2,1)S(1)}, bf16[96,2048]{1,0:T(8,128)(2,1)S(1)}, u32[]{:S(2)}, u32[]{:S(2)}) collective-permute-start(bf16[96,2048]{1,0:T(8,128)(2,1)S(1)} %collective-permute-done.26.rest_32_.rest_24_), channel_id=1, source_target_pairs={{0,8},{1,9},{2,10},{3,11},{4,12},{5,13},{6,14},{7,15},{8,0},{9,1},... | collective-permute-start | bytes 1179656 | tf_op jit(solution)/shard_map/ppermute | solution.py:23
  45.5 20.4 %collective-permute-start.33 = (bf16[96,2048]{1,0:T(8,128)(2,1)S(1)}, bf16[96,2048]{1,0:T(8,128)(2,1)S(1)}, u32[]{:S(2)}, u32[]{:S(2)}) collective-permute-start(bf16[96,2048]{1,0:T(8,128)(2,1)S(1)} %collective-permute-done.16.rest_14_.rest_6_), channel_id=1, source_target_pairs={{0,24},{1,25},{2,26},{3,27},{4,28},{5,29},{6,30},{7,31},{8,16},{9,... | collective-permute-start | bytes 1179656 | tf_op jit(solution)/shard_map/ppermute | solution.py:23
  53.1 12.8 %collective-permute-start.37 = (bf16[96,2048]{1,0:T(8,128)(2,1)S(1)}, bf16[96,2048]{1,0:T(8,128)(2,1)S(1)}, u32[]{:S(2)}, u32[]{:S(2)}) collective-permute-start(bf16[96,2048]{1,0:T(8,128)(2,1)S(1)} %collective-permute-done.26.rest_32_.rest_24_), channel_id=1, source_target_pairs={{0,2},{1,3},{2,0},{3,1},{4,6},{5,7},{6,4},{7,5},{8,10},{9,11},{10,... | collective-permute-start | bytes 1179656 | tf_op jit(solution)/shard_map/ppermute | solution.py:23
  53.6 12.4 %collective-permute-start.39 = (bf16[96,2048]{1,0:T(8,128)(2,1)S(1)}, bf16[96,2048]{1,0:T(8,128)(2,1)S(1)}, u32[]{:S(2)}, u32[]{:S(2)}) collective-permute-start(bf16[96,2048]{1,0:T(8,128)(2,1)S(1)} %collective-permute-done.26.rest_32_.rest_24_), channel_id=1, source_target_pairs={{0,4},{1,5},{2,6},{3,7},{4,0},{5,1},{6,2},{7,3},{8,12},{9,13},{10,... | collective-permute-start | bytes 1179656 | tf_op jit(solution)/shard_map/ppermute | solution.py:23
  54.5 17.2 %collective-permute-start.20 = (bf16[96,2048]{1,0:T(8,128)(2,1)S(1)}, bf16[96,2048]{1,0:T(8,128)(2,1)S(1)}, u32[]{:S(2)}, u32[]{:S(2)}) collective-permute-start(bf16[96,2048]{1,0:T(8,128)(2,1)S(1)} %collective-permute-done.18.rest_16_.rest_8_), channel_id=1, source_target_pairs={{0,2},{1,3},{2,0},{3,1},{4,6},{5,7},{6,4},{7,5},{8,10},{9,11},{10,... | collective-permute-start | bytes 1179656 | tf_op jit(solution)/shard_map/ppermute | solution.py:23
  63.9 9.0 %collective-permute-start.22 = (bf16[96,2048]{1,0:T(8,128)(2,1)S(1)}, bf16[96,2048]{1,0:T(8,128)(2,1)}, u32[]{:S(2)}, u32[]{:S(2)}) collective-permute-start(bf16[96,2048]{1,0:T(8,128)(2,1)S(1)} %collective-permute-done.18.rest_16_.rest_8_), channel_id=1, source_target_pairs={{0,4},{1,5},{2,6},{3,7},{4,0},{5,1},{6,2},{7,3},{8,12},{9,13},{10,... | collective-permute-start | bytes 1179656 | tf_op jit(solution)/shard_map/ppermute | solution.py:23
  65.9 7.9 %collective-permute-start.24 = (bf16[96,2048]{1,0:T(8,128)(2,1)S(1)}, bf16[96,2048]{1,0:T(8,128)(2,1)}, u32[]{:S(2)}, u32[]{:S(2)}) collective-permute-start(bf16[96,2048]{1,0:T(8,128)(2,1)S(1)} %collective-permute-done.16.rest_14_.rest_6_), channel_id=1, source_target_pairs={{0,8},{1,9},{2,10},{3,11},{4,12},{5,13},{6,14},{7,15},{8,0},{9,1},... | collective-permute-start | bytes 1179656 | tf_op jit(solution)/shard_map/ppermute | solution.py:23
  65.9 7.9 %collective-permute-start.36 = (bf16[96,2048]{1,0:T(8,128)(2,1)S(1)}, bf16[96,2048]{1,0:T(8,128)(2,1)S(1)}, u32[]{:S(2)}, u32[]{:S(2)}) collective-permute-start(bf16[96,2048]{1,0:T(8,128)(2,1)S(1)} %collective-permute-done.26.rest_32_.rest_24_), channel_id=1, source_target_pairs={{0,1},{1,0},{2,3},{3,2},{4,5},{5,4},{6,7},{7,6},{8,9},{9,8},{10,11... | collective-permute-start | bytes 1179656 | tf_op jit(solution)/shard_map/ppermute | solution.py:23
  66.0 9.1 %collective-permute-start.17 = (bf16[96,2048]{1,0:T(8,128)(2,1)S(1)}, bf16[96,2048]{1,0:T(8,128)(2,1)S(1)}, u32[]{:S(2)}, u32[]{:S(2)}) collective-permute-start(bf16[96,2048]{1,0:T(8,128)(2,1)S(1)} %collective-permute-done.16.rest_14_.rest_6_), channel_id=1, source_target_pairs={{0,1},{1,0},{2,3},{3,2},{4,5},{5,4},{6,7},{7,6},{8,9},{9,8},{10,11... | collective-permute-start | bytes 1179656 | tf_op jit(solution)/shard_map/ppermute | solution.py:23
  71.7 5.1 %collective-permute-start.19 = (bf16[96,2048]{1,0:T(8,128)(2,1)S(1)}, bf16[96,2048]{1,0:T(8,128)(2,1)S(1)}, u32[]{:S(2)}, u32[]{:S(2)}) collective-permute-start(bf16[96,2048]{1,0:T(8,128)(2,1)S(1)} %collective-permute-done.18.rest_16_.rest_8_), channel_id=1, source_target_pairs={{0,1},{1,0},{2,3},{3,2},{4,5},{5,4},{6,7},{7,6},{8,9},{9,8},{10,11... | collective-permute-start | bytes 1179656 | tf_op jit(solution)/shard_map/ppermute | solution.py:23
  72.9 4.6 %collective-permute-start.13 = (bf16[96,2048]{1,0:T(8,128)(2,1)S(1)}, bf16[96,2048]{1,0:T(8,128)(2,1)S(1)}, u32[]{:S(2)}, u32[]{:S(2)}) collective-permute-start(bf16[96,2048]{1,0:T(8,128)(2,1)S(1)} %collective-permute-done.12.rest_10_.rest_2_), channel_id=1, source_target_pairs={{0,1},{1,0},{2,3},{3,2},{4,5},{5,4},{6,7},{7,6},{8,9},{9,8},{10,11... | collective-permute-start | bytes 1179656 | tf_op jit(solution)/shard_map/ppermute | solution.py:23
  73.8 5.2 %collective-permute-start.15 = (bf16[96,2048]{1,0:T(8,128)(2,1)S(1)}, bf16[96,2048]{1,0:T(8,128)(2,1)S(1)}, u32[]{:S(2)}, u32[]{:S(2)}) collective-permute-start(bf16[96,2048]{1,0:T(8,128)(2,1)S(1)} %collective-permute-done.14.rest_12_.rest_4_), channel_id=1, source_target_pairs={{0,1},{1,0},{2,3},{3,2},{4,5},{5,4},{6,7},{7,6},{8,9},{9,8},{10,11... | collective-permute-start | bytes 1179656 | tf_op jit(solution)/shard_map/ppermute | solution.py:23
  74.6 11.6 %collective-permute-start.29 = (bf16[96,2048]{1,0:T(8,128)(2,1)S(1)}, bf16[96,2048]{1,0:T(8,128)(2,1)}, u32[]{:S(2)}, u32[]{:S(2)}) collective-permute-start(bf16[96,2048]{1,0:T(8,128)(2,1)S(1)} %collective-permute-done.27.rest_24_.rest_16_), channel_id=1, source_target_pairs={{0,2},{1,3},{2,0},{3,1},{4,6},{5,7},{6,4},{7,5},{8,10},{9,11},{10,... | collective-permute-start | bytes 1179656 | tf_op jit(solution)/shard_map/ppermute | solution.py:23
  75.9 11.4 %collective-permute-start.31 = (bf16[96,2048]{1,0:T(8,128)(2,1)S(1)}, bf16[96,2048]{1,0:T(8,128)(2,1)}, u32[]{:S(2)}, u32[]{:S(2)}) collective-permute-start(bf16[96,2048]{1,0:T(8,128)(2,1)S(1)} %collective-permute-done.27.rest_24_.rest_16_), channel_id=1, source_target_pairs={{0,4},{1,5},{2,6},{3,7},{4,0},{5,1},{6,2},{7,3},{8,12},{9,13},{10,... | collective-permute-start | bytes 1179656 | tf_op jit(solution)/shard_map/ppermute | solution.py:23
  77.5 10.8 %collective-permute-start.34 = (bf16[96,2048]{1,0:T(8,128)(2,1)S(1)}, bf16[96,2048]{1,0:T(8,128)(2,1)}, u32[]{:S(2)}, u32[]{:S(2)}) collective-permute-start(bf16[96,2048]{1,0:T(8,128)(2,1)S(1)} %collective-permute-done.33.rest_38_.rest_30_), channel_id=1, source_target_pairs={{0,8},{1,9},{2,10},{3,11},{4,12},{5,13},{6,14},{7,15},{8,0},{9,1},... | collective-permute-start | bytes 1179656 | tf_op jit(solution)/shard_map/ppermute | solution.py:23
  78.3 11.0 %collective-permute-start.28 = (bf16[96,2048]{1,0:T(8,128)(2,1)S(1)}, bf16[96,2048]{1,0:T(8,128)(2,1)S(1)}, u32[]{:S(2)}, u32[]{:S(2)}) collective-permute-start(bf16[96,2048]{1,0:T(8,128)(2,1)S(1)} %collective-permute-done.27.rest_24_.rest_16_), channel_id=1, source_target_pairs={{0,1},{1,0},{2,3},{3,2},{4,5},{5,4},{6,7},{7,6},{8,9},{9,8},{10,11... | collective-permute-start | bytes 1179656 | tf_op jit(solution)/shard_map/ppermute | solution.py:23
  79.8 10.5 %collective-permute-start.38 = (bf16[96,2048]{1,0:T(8,128)(2,1)S(1)}, bf16[96,2048]{1,0:T(8,128)(2,1)S(1)}, u32[]{:S(2)}, u32[]{:S(2)}) collective-permute-start(bf16[96,2048]{1,0:T(8,128)(2,1)S(1)} %collective-permute-done.37.rest_34_.rest_26_), channel_id=1, source_target_pairs={{0,1},{1,0},{2,3},{3,2},{4,5},{5,4},{6,7},{7,6},{8,9},{9,8},{10,11... | collective-permute-start | bytes 1179656 | tf_op jit(solution)/shard_map/ppermute | solution.py:23
  86.2 5.1 %collective-permute-start.40 = (bf16[96,2048]{1,0:T(8,128)(2,1)S(1)}, bf16[96,2048]{1,0:T(8,128)(2,1)S(1)}, u32[]{:S(2)}, u32[]{:S(2)}) collective-permute-start(bf16[96,2048]{1,0:T(8,128)(2,1)S(1)} %collective-permute-done.39.rest_36_.rest_28_), channel_id=1, source_target_pairs={{0,1},{1,0},{2,3},{3,2},{4,5},{5,4},{6,7},{7,6},{8,9},{9,8},{10,11... | collective-permute-start | bytes 1179656 | tf_op jit(solution)/shard_map/ppermute | solution.py:23
  87.2 5.1 %collective-permute-start.41 = (bf16[96,2048]{1,0:T(8,128)(2,1)S(1)}, bf16[96,2048]{1,0:T(8,128)(2,1)S(1)}, u32[]{:S(2)}, u32[]{:S(2)}) collective-permute-start(bf16[96,2048]{1,0:T(8,128)(2,1)S(1)} %collective-permute-done.33.rest_38_.rest_30_), channel_id=1, source_target_pairs={{0,1},{1,0},{2,3},{3,2},{4,5},{5,4},{6,7},{7,6},{8,9},{9,8},{10,11... | collective-permute-start | bytes 1179656 | tf_op jit(solution)/shard_map/ppermute | solution.py:23
  88.3 5.1 %collective-permute-start.21 = (bf16[96,2048]{1,0:T(8,128)(2,1)S(1)}, bf16[96,2048]{1,0:T(8,128)(2,1)S(1)}, u32[]{:S(2)}, u32[]{:S(2)}) collective-permute-start(bf16[96,2048]{1,0:T(8,128)(2,1)S(1)} %collective-permute-done.20.rest_18_.rest_10_), channel_id=1, source_target_pairs={{0,1},{1,0},{2,3},{3,2},{4,5},{5,4},{6,7},{7,6},{8,9},{9,8},{10,11... | collective-permute-start | bytes 1179656 | tf_op jit(solution)/shard_map/ppermute | solution.py:23
  90.0 6.3 %collective-permute-start.23 = (bf16[96,2048]{1,0:T(8,128)(2,1)}, bf16[96,2048]{1,0:T(8,128)(2,1)}, u32[]{:S(2)}, u32[]{:S(2)}) collective-permute-start(bf16[96,2048]{1,0:T(8,128)(2,1)} %collective-permute-done.22.rest_20_.rest_12_), channel_id=1, source_target_pairs={{0,1},{1,0},{2,3},{3,2},{4,5},{5,4},{6,7},{7,6},{8,9},{9,8},{10,11... | collective-permute-start | bytes 1179656 | tf_op jit(solution)/shard_map/ppermute | solution.py:23
  91.1 5.2 %collective-permute-start.25 = (bf16[96,2048]{1,0:T(8,128)(2,1)}, bf16[96,2048]{1,0:T(8,128)(2,1)}, u32[]{:S(2)}, u32[]{:S(2)}) collective-permute-start(bf16[96,2048]{1,0:T(8,128)(2,1)} %collective-permute-done.24.rest_22_.rest_14_), channel_id=1, source_target_pairs={{0,1},{1,0},{2,3},{3,2},{4,5},{5,4},{6,7},{7,6},{8,9},{9,8},{10,11... | collective-permute-start | bytes 1179656 | tf_op jit(solution)/shard_map/ppermute | solution.py:23
  92.1 4.2 %collective-permute-start.30 = (bf16[96,2048]{1,0:T(8,128)(2,1)}, bf16[96,2048]{1,0:T(8,128)(2,1)}, u32[]{:S(2)}, u32[]{:S(2)}) collective-permute-start(bf16[96,2048]{1,0:T(8,128)(2,1)} %collective-permute-done.29.rest_26_.rest_18_), channel_id=1, source_target_pairs={{0,1},{1,0},{2,3},{3,2},{4,5},{5,4},{6,7},{7,6},{8,9},{9,8},{10,11... | collective-permute-start | bytes 1179656 | tf_op jit(solution)/shard_map/ppermute | solution.py:23
  93.1 3.2 %collective-permute-start.32 = (bf16[96,2048]{1,0:T(8,128)(2,1)}, bf16[96,2048]{1,0:T(8,128)(2,1)}, u32[]{:S(2)}, u32[]{:S(2)}) collective-permute-start(bf16[96,2048]{1,0:T(8,128)(2,1)} %collective-permute-done.31.rest_28_.rest_20_), channel_id=1, source_target_pairs={{0,1},{1,0},{2,3},{3,2},{4,5},{5,4},{6,7},{7,6},{8,9},{9,8},{10,11... | collective-permute-start | bytes 1179656 | tf_op jit(solution)/shard_map/ppermute | solution.py:23
  94.1 2.2 %collective-permute-start.35 = (bf16[96,2048]{1,0:T(8,128)(2,1)}, bf16[96,2048]{1,0:T(8,128)(2,1)}, u32[]{:S(2)}, u32[]{:S(2)}) collective-permute-start(bf16[96,2048]{1,0:T(8,128)(2,1)} %collective-permute-done.34.rest_30_.rest_22_), channel_id=1, source_target_pairs={{0,1},{1,0},{2,3},{3,2},{4,5},{5,4},{6,7},{7,6},{8,9},{9,8},{10,11... | collective-permute-start | bytes 1179656 | tf_op jit(solution)/shard_map/ppermute | solution.py:23
  122.7 10.6 %copy-start.15 = (bf16[96,2048]{1,0:T(8,128)(2,1)S(1)}, bf16[96,2048]{1,0:T(8,128)(2,1)}, u32[]{:S(2)}) copy-start(bf16[96,2048]{1,0:T(8,128)(2,1)} %copy-done.13) | copy-start | bytes 1179652
  122.7 10.6 %copy-start.18 = (bf16[96,2048]{1,0:T(8,128)(2,1)S(1)}, bf16[96,2048]{1,0:T(8,128)(2,1)}, u32[]{:S(2)}) copy-start(bf16[96,2048]{1,0:T(8,128)(2,1)} %copy-done.16) | copy-start | bytes 1179652
  122.7 10.6 %copy-start.23 = (bf16[96,2048]{1,0:T(8,128)(2,1)S(1)}, bf16[96,2048]{1,0:T(8,128)(2,1)}, u32[]{:S(2)}) copy-start(bf16[96,2048]{1,0:T(8,128)(2,1)} %copy-done.21) | copy-start | bytes 1179652
  122.7 10.6 %copy-start.26 = (bf16[96,2048]{1,0:T(8,128)(2,1)S(1)}, bf16[96,2048]{1,0:T(8,128)(2,1)}, u32[]{:S(2)}) copy-start(bf16[96,2048]{1,0:T(8,128)(2,1)} %copy-done.24) | copy-start | bytes 1179652
  122.7 10.6 %copy-start.29 = (bf16[96,2048]{1,0:T(8,128)(2,1)S(1)}, bf16[96,2048]{1,0:T(8,128)(2,1)}, u32[]{:S(2)}) copy-start(bf16[96,2048]{1,0:T(8,128)(2,1)} %copy-done.27) | copy-start | bytes 1179652
  122.7 10.6 %copy-start.32 = (bf16[96,2048]{1,0:T(8,128)(2,1)S(1)}, bf16[96,2048]{1,0:T(8,128)(2,1)}, u32[]{:S(2)}) copy-start(bf16[96,2048]{1,0:T(8,128)(2,1)} %copy-done.30) | copy-start | bytes 1179652
  (61 other events, 121.0 us)

commit v2 on v0

--- a/solution.py
+++ b/solution.py
@@ -1,9 +1,338 @@
+import functools
+
 import jax
 import jax.numpy as jnp
 from jax import lax
+from jax.experimental import pallas as pl
+from jax.experimental.pallas import tpu as pltpu
 from jax.sharding import PartitionSpec as P
 
-tremble = 0.05
+TREMBLE = 0.05
+AXES = ("trav", "bulk")
+
+TRAV, BULK = 4, 8
+X, Y, D, A, B, C = 1, 2, 3, 4, 12, 8
+PLANE = (0, X, Y, D)
+ID_ROWS = 16
+
+def swap_chip(value, chip):
+    return lax.ppermute(value, AXES, [(i, i ^ (chip << 1)) for i in range(TRAV * BULK)])
+
+
+def swap_core(value):
+    return lax.ppermute(value, AXES, [(i, i ^ 1) for i in range(TRAV * BULK)])
+
+
+def iota(shape, dim):
+    return lax.broadcasted_iota(jnp.int32, shape, dim)
+
+
+def over_rows(a, b):
+    return lax.dot_general(a, b, (((0,), (0,)), ((), ())), preferred_element_type=jnp.float32)
+
+
+def my_core():
+    return lax.axis_index("bulk") & 1
+
+
+def my_chip():
+    return lax.axis_index("trav") * (BULK // 2) + (lax.axis_index("bulk") >> 1)
+
+
+def call(kernel, outs, mebibytes, scratch=(), flops=0, bytes_accessed=0, in_specs=None):
+    many = isinstance(outs, (list, tuple))
+    spec = pl.BlockSpec(memory_space=pltpu.VMEM)
+
+    def run(*args):
+        return pl.pallas_call(
+            kernel,
+            out_shape=tuple(outs) if many else outs,
+            in_specs=in_specs or [spec] * len(args),
+            out_specs=(spec,) * len(outs) if many else spec,
+            scratch_shapes=list(scratch),
+            compiler_params=pltpu.CompilerParams(vmem_limit_bytes=mebibytes << 20),
+            cost_estimate=pl.CostEstimate(flops=flops, bytes_accessed=bytes_accessed, transcendentals=0),
+        )(*args)
+
+    return run
+
+
+def shape(rows, columns, dtype=jnp.bfloat16):
+    return jax.ShapeDtypeStruct((rows, columns), dtype)
+
+
+def join_kernel(w_first, w_second, other_first, other_second, wanted, other_wanted, out, out_ids):
+    core, half = my_core(), out.shape[1]
+    here = pl.ds(pl.multiple_of(core * half, half), half)
+    begin = 0
+    for mine, other in ((w_first, other_first), (w_second, other_second)):
+        depth = mine.shape[0]
+        for to, rows in ((core, mine), (1 - core, other)):
+            place = pl.ds(pl.multiple_of(begin + to * depth, depth), depth)
+            for target in (out, out_ids):
+                target[place, :] = rows[:, here]
+        begin += 2 * depth
+    owners, capacity = wanted.shape
+    blank = jnp.zeros((owners, half - 2 * capacity), jnp.float32)
+    ids = jnp.concatenate([wanted[...].astype(jnp.float32), other_wanted[...].astype(jnp.float32), blank], axis=1)
+    ids = jnp.concatenate([ids, jnp.zeros((out_ids.shape[0] - begin - owners, half), jnp.float32)], axis=0)
+    out_ids[begin:, :] = ids.astype(jnp.bfloat16)
+
+
+def across(a, b, precision=None):
+    return lax.dot_general(
+        a, b, (((1,), (1,)), ((), ())), preferred_element_type=jnp.float32, precision=precision
+    )
+
+
+def slots_kernel(owner, row, slot, wanted):
+    rows = owner.shape[1]
+    owners, capacity = wanted.shape
+    partner = owner[...] ^ lax.axis_index("bulk")
+    hits = (partner == iota((owners, rows), 0)).astype(jnp.float32)
+    before = (iota((rows, rows), 0) < iota((rows, rows), 1)).astype(jnp.bfloat16)
+    earlier = jnp.dot(hits.astype(jnp.bfloat16), before, preferred_element_type=jnp.float32)
+    rank = jnp.sum(earlier * hits, axis=0, keepdims=True).astype(jnp.int32)
+    slot[...] = partner * capacity + rank
+    bucket = (hits * row[...].astype(jnp.float32)).astype(jnp.bfloat16)
+    at_rank = (rank == iota((capacity, rows), 0)).astype(jnp.bfloat16)
+    wanted[...] = across(bucket, at_rank).astype(jnp.int32)
+
+
+def serve_kernel(capacity, *refs):
+    asked, table, outs = refs[: len(PLANE)], refs[len(PLANE)], refs[len(PLANE) + 1 :]
+    buckets = table.shape[0]
+    for chip, ids, out in zip(PLANE, asked, outs):
+        owners = ids[ids.shape[0] - ID_ROWS :, :].astype(jnp.int32)
+        mine = [owners[2 * chip + core : 2 * chip + core + 1, core * capacity : (core + 1) * capacity] for core in (0, 1)]
+        want = jnp.concatenate(mine, axis=1)
+        onehot = (iota((buckets, want.shape[1]), 0) == want).astype(jnp.bfloat16)
+        out[...] = over_rows(onehot, table[...]).astype(jnp.bfloat16)
+
+
+def stack_kernel(places, *refs):
+    refs, out = refs[:-1], refs[-1]
+    to = 0
+    for ref, (begin, count) in zip(refs, places):
+        out[to : to + count, :] = ref[begin : begin + count, :]
+        to += count
+
+
+def stack(*parts):
+    arrays, places = [part[0] for part in parts], [part[1:] for part in parts]
+    total = sum(count for _, count in places)
+    out = shape(total, arrays[0].shape[1], arrays[0].dtype)
+    return call(functools.partial(stack_kernel, places), out, 4)(*arrays)
+
+
+def inputs_kernel(begins, actions, slot, parents, act_table, *refs):
+    same, sibling, inputs = refs[: len(PLANE)], refs[len(PLANE)], refs[len(PLANE) + 1]
+    rows = parents.shape[0]
+    capacity = sibling.shape[0] // len(PLANE)
+    parts = []
+    for n, (begin, ref) in enumerate(zip(begins, same)):
+        parts += [ref[begin : begin + capacity, :], sibling[n * capacity : (n + 1) * capacity, :]]
+    served = jnp.concatenate(parts, axis=0)
+    onehot = (slot[...] == iota((served.shape[0], rows), 0)).astype(jnp.bfloat16)
+    bucket = over_rows(onehot, served)
+    for c in range(actions.shape[0]):
+        onehot = (actions[c : c + 1, :] == iota((act_table.shape[0], rows), 0)).astype(jnp.bfloat16)
+        change = over_rows(onehot, act_table[...])
+        base = (parents[...].astype(jnp.float32) + change).astype(jnp.bfloat16)
+        inputs[c * rows : (c + 1) * rows, :] = (base.astype(jnp.float32) + bucket).astype(jnp.bfloat16)
+
+
+def place_pieces(pieces, refs, depth, weights):
+    for chip, which, begin, row, count in pieces:
+        to = pl.multiple_of((my_chip() ^ chip) * depth + row, 16)
+        weights[pl.ds(to, count), :] = refs[which][begin : begin + count, :]
+
+
+def line_up(pieces, refs, depth, mine, theirs, weights, picked):
+    rows = mine.shape[0] // 2
+    chip, core = my_chip(), my_core()
+    blocks = mine.shape[1] // depth
+    order = list(dict.fromkeys(piece[0] for piece in pieces))
+    for name, which, begin, row, count in pieces:
+        to = order.index(name) * depth + row
+        weights[to : to + count, :] = refs[which][begin : begin + count, :]
+    for n, name in enumerate(order):
+        there = chip ^ name
+        column = pl.ds(pl.multiple_of((there & (blocks - 1)) * depth, depth), depth)
+        at_home = (there // blocks) == core
+        for m in (0, 1):
+            ours = mine[m * rows : (m + 1) * rows, column]
+            others = theirs[(1 - m) * rows : (2 - m) * rows, column]
+            picked[m * rows : (m + 1) * rows, n * depth : (n + 1) * depth] = jnp.where(at_home, ours, others)
+
+
+def first_kernel(pieces, depth, mine, theirs, bias, *refs):
+    refs, (out, weights) = refs[:-2], refs[-2:]
+    place_pieces(pieces, refs, depth, weights)
+    rows, half = mine.shape[0], weights.shape[1]
+    offset = my_core() * half
+    step = 512
+    for n in range(0, half, step):
+        shift = bias[:, pl.ds(pl.multiple_of(offset + n, step), step)]
+        for m, inputs in enumerate((mine, theirs)):
+            total = jnp.dot(inputs[...], weights[:, n : n + step], preferred_element_type=jnp.float32)
+            out[m * rows : (m + 1) * rows, n : n + step] = jnp.maximum(total + shift, 0.0).astype(jnp.bfloat16)
+
+
+def second_kernel(pieces, depth, mine, theirs, *refs):
+    refs, (out, weights, picked) = refs[:-3], refs[-3:]
+    rows, half = mine.shape[0] // 2, weights.shape[1]
+    line_up(pieces, refs, depth, mine, theirs, weights, picked)
+    step = 512
+    for m in (0, 1):
+        for n in range(0, half, step):
+            out[m * rows : (m + 1) * rows, n : n + step] = jnp.dot(
+                picked[m * rows : (m + 1) * rows, :], weights[:, n : n + step], preferred_element_type=jnp.float32
+            )
+
+
+def third_kernel(pieces, depth, mine, theirs, so_far, bias, w_head, *refs):
+    refs, (out_mine, out_theirs, weights, picked) = refs[:-4], refs[-4:]
+    rows, half = mine.shape[0] // 2, weights.shape[1]
+    core = my_core()
+    line_up(pieces, refs, depth, mine, theirs, weights, picked)
+    step = 512
+    for m, out in enumerate((out_mine, out_theirs)):
+        advantage = jnp.zeros((rows, w_head.shape[0]), jnp.float32)
+        for n in range(0, half, step):
+            here = pl.ds(pl.multiple_of(core * half + n, step), step)
+            total = so_far[m * rows : (m + 1) * rows, n : n + step] + jnp.dot(
+                picked[m * rows : (m + 1) * rows, :], weights[:, n : n + step], preferred_element_type=jnp.float32
+            )
+            layer = jnp.maximum(total + bias[:, here], 0.0).astype(jnp.bfloat16)
+            advantage = advantage + across(layer, w_head[:, here])
+        out[...] = advantage.T
+
+
+def last_kernel(counts, ancestor, legal, b_head, mine, theirs, strategy, values):
+    actions = b_head.shape[1]
+    rows = counts.shape[1]
+    diagonal = iota((actions, actions), 0) == iota((actions, actions), 1)
+    shift = jnp.sum(jnp.where(diagonal, b_head[...], 0.0), axis=1, keepdims=True)
+    first_action = (iota((actions, rows), 0) == 0).astype(jnp.float32)
+    total_value = jnp.zeros((1, rows), jnp.float32)
+    for c in range(mine.shape[1] // rows):
+        here = slice(c * rows, (c + 1) * rows)
+        advantage = mine[:, here] + theirs[:, here] + shift
+        allowed = jnp.maximum(legal[c * actions : (c + 1) * actions, :].astype(jnp.float32), first_action)
+        positive = allowed * (jnp.maximum(advantage, 0.0) + TREMBLE)
+        sigma = positive / jnp.sum(positive, axis=0, keepdims=True)
+        live = (counts[...] > c).astype(jnp.float32)
+        strategy[c * actions : (c + 1) * actions, :] = sigma * live
+        total_value = total_value + live * jnp.sum(sigma * advantage, axis=0, keepdims=True)
+    value = total_value / counts[...].astype(jnp.float32)
+    at_node = (ancestor[...] == iota((values.shape[1], rows), 0)).astype(jnp.float32)
+    values[...] = across(value, at_node, lax.Precision.HIGHEST)
+
+
+def body(
+    parents,
+    act_table,
+    bucket_table,
+    w_first,
+    b_first,
+    w_second,
+    b_second,
+    w_head,
+    b_head,
+    branch_counts,
+    sampled_actions,
+    bucket_owner,
+    bucket_row,
+    legal_mask,
+    ancestor,
+):
+    par_count, feature_count = parents.shape
+    branches = par_count * sampled_actions.shape[1]
+    hidden_units = w_first.shape[1]
+    half = hidden_units // 2
+    depth_one, depth_two = w_first.shape[0], w_second.shape[0]
+    capacity = max(2, (4 * par_count + 3 * BULK - 1) // (3 * BULK))
+
+    slot, wanted = call(
+        slots_kernel, (shape(1, par_count, jnp.int32), shape(BULK, capacity, jnp.int32)), 4
+    )(bucket_owner.T, bucket_row[None, :])
+    depth = 2 * (depth_one + depth_two)
+    own, own_ids = call(join_kernel, (shape(depth, half), shape(depth + ID_ROWS, half)), 4)(
+        w_first, w_second, swap_core(w_first), swap_core(w_second), wanted, swap_core(wanted)
+    )
+    from_x, from_y, from_d = [swap_chip(own_ids, chip) for chip in PLANE[1:]]
+    from_a, from_b = [swap_chip(own, chip) for chip in (A, B)]
+    served = call(
+        functools.partial(serve_kernel, capacity), (shape(2 * capacity, feature_count),) * len(PLANE), 6
+    )(own_ids, from_x, from_y, from_d, bucket_table)
+    ab = ((from_a, 0, depth), (from_b, 0, depth))
+    wide = 2 * capacity
+    to_x, to_y, to_d = served[1:]
+    x_ab = swap_chip(stack(*ab, (to_x, 0, wide)), X)
+    y_ab = swap_chip(stack(*ab, (to_y, 0, wide)), Y)
+    rows_d = swap_chip(to_d, D)
+    from_ab, d_b = swap_chip(from_b, A), swap_chip(stack((from_d, 0, depth)), B)
+    x_ab, y_ab, rows_d, from_ab, d_b = lax.optimization_barrier((x_ab, y_ab, rows_d, from_ab, d_b))
+
+    same = [(served[0], 0), (x_ab, 2 * depth), (y_ab, 2 * depth), (rows_d, 0)]
+    sibling = swap_core(stack(*((rows, begin + capacity, capacity) for rows, begin in same)))
+    inputs = call(
+        functools.partial(inputs_kernel, [begin for _, begin in same]), shape(branches, feature_count), 8
+    )(sampled_actions.T, slot, parents, act_table, *(rows for rows, _ in same), sibling)
+    inputs_sibling = swap_core(inputs)
+
+    chip_one, chip_two = 2 * depth_one, 2 * depth_two
+
+    def later(begin, count, cut):
+        x_c = stack((from_ab, begin, count), (y_ab, begin, cut))
+        y_c = stack((from_ab, begin, count), *([(x_ab, begin + cut, count - cut)] if cut < count else []))
+        return [swap_chip(x_c, X), swap_chip(y_c, Y), swap_chip(stack((d_b, begin, count)), A)]
+
+    def late_pieces(count, cut, first):
+        pieces = [(X ^ C, first, 0, 0, count), (Y ^ C, first + 1, 0, 0, count), (D ^ C, first + 2, 0, 0, count)]
+        pieces.append((D ^ A, first, count, 0, cut))
+        return pieces + ([(D ^ A, first + 1, count, cut, count - cut)] if cut < count else [])
+
+    early_arrays = [own, from_x, from_y, from_a, from_b, from_d, x_ab, y_ab, from_ab, d_b]
+
+    def early_pieces(begin):
+        count = chip_two if begin else chip_one
+        pieces = [(chip, n, begin) for n, chip in enumerate((0, X, Y, A, B, D))]
+        pieces += [(X ^ A, 6, begin), (X ^ B, 6, depth + begin), (Y ^ A, 7, begin), (Y ^ B, 7, depth + begin)]
+        pieces += [(C, 8, begin), (D ^ B, 9, begin)]
+        return [(*piece, 0, count) for piece in pieces]
+
+    cut_two = chip_two // 4
+    first_late, second_late = later(0, chip_one, chip_one), later(chip_one, chip_two, cut_two)
+    first_arrays = early_arrays + first_late
+    first_pieces = early_pieces(0) + late_pieces(chip_one, chip_one, len(early_arrays))
+
+    hidden = call(
+        functools.partial(first_kernel, first_pieces, chip_one),
+        shape(2 * branches, half),
+        14,
+        [pltpu.VMEM((feature_count, half), jnp.bfloat16)],
+    )(inputs, inputs_sibling, b_first[None, :], *first_arrays)
+    hidden_sibling = swap_core(hidden)
+
+    early, late = early_pieces(chip_one), late_pieces(chip_two, cut_two, 0)
+    so_far = call(
+        functools.partial(second_kernel, early, chip_two),
+        shape(2 * branches, half, jnp.float32),
+        16,
+        [pltpu.VMEM((len(early) * chip_two, half), jnp.bfloat16), pltpu.VMEM((2 * branches, len(early) * chip_two), jnp.bfloat16)],
+    )(hidden, hidden_sibling, *early_arrays)
+    mine, theirs = call(
+        functools.partial(third_kernel, late, chip_two),
+        (shape(w_head.shape[1], branches, jnp.float32),) * 2,
+        12,
+        [pltpu.VMEM((4 * chip_two, half), jnp.bfloat16), pltpu.VMEM((2 * branches, 4 * chip_two), jnp.bfloat16)],
+    )(hidden, hidden_sibling, so_far, b_second[None, :], w_head.T, *second_late)
+    strategy, values = call(
+        last_kernel, (shape(legal_mask.shape[1], par_count, jnp.float32), shape(1, par_count // 4, jnp.float32)), 4
+    )(branch_counts[None, :], ancestor[None, :], legal_mask.T, b_head[None, :], mine, swap_core(theirs))
+    return (strategy.T, values.reshape(-1))
 
 
 def network(inputs, w_first, b_first, w_second, b_second, w_head, b_head):
@@ -24,7 +353,7 @@
     return jnp.dot(hidden_two, w_head, preferred_element_type=jnp.float32) + b_head
 
 
-def body(
+def general_body(
     parents,
     act_table,
     bucket_table,
@@ -96,7 +425,7 @@
     allowed = jnp.maximum(
         legal_mask.reshape(par_count, branch_slots, action_count).astype(jnp.float32), first_action
     )
-    positive = allowed * (jnp.maximum(advantage, 0.0) + tremble)
+    positive = allowed * (jnp.maximum(advantage, 0.0) + TREMBLE)
     sigma = positive / jnp.sum(positive, axis=-1, keepdims=True)
     live = (jnp.arange(branch_slots)[None, :] < branch_counts[:, None]).astype(jnp.float32)
     strategy = (sigma * live[:, :, None]).reshape(par_count, branch_slots * action_count)
@@ -109,26 +438,27 @@
 
 
 def solution(mesh):
+    laid_out = (mesh.shape["trav"], mesh.shape["bulk"]) == (TRAV, BULK)
     return jax.shard_map(
-        body,
+        body if laid_out else general_body,
         mesh=mesh,
         in_specs=(
-            P(("trav", "bulk"), None),
+            P(AXES, None),
             P(),
             P("bulk", None),
-            P(("trav", "bulk"), None),
+            P(AXES, None),
             P(),
-            P(("trav", "bulk"), None),
+            P(AXES, None),
             P(),
             P(),
             P(),
-            P(("trav", "bulk")),
-            P(("trav", "bulk"), None),
-            P(("trav", "bulk"), None),
-            P(("trav", "bulk")),
-            P(("trav", "bulk"), None),
-            P(("trav", "bulk")),
+            P(AXES),
+            P(AXES, None),
+            P(AXES, None),
+            P(AXES),
+            P(AXES, None),
+            P(AXES),
         ),
-        out_specs=(P(("trav", "bulk"), None), P(("trav", "bulk"))),
+        out_specs=(P(AXES, None), P(AXES)),
         check_vma=False,
     )

time: 206 us -> 92.2 us (0.45)
  waiting for transfers between devices: 116 us -> 46.2 us
  matrix products: 28 us -> 0 us
  local copies, waits for them, and re-layouts: 27.4 us -> 4.3 us
  Pallas kernels: 0 us -> 15.4 us
  between operations: 14.3 us -> 0.83 us
  starting transfers between devices: 12.8 us -> 25.3 us
  other arithmetic: 6.8 us -> 0 us
    all_gather x2 -> x0, waiting for transfers between devices: 86.5 us -> none  [the longest x1 79.1 us: network(): lax.all_gather(w_second, ('trav', 'bulk'), axis=0, tiled=True)]
    ppermute x0 -> x23, waiting for transfers between devices: none -> 46.2 us  [the longest x16 41.2 us: swap_chip(): lax.ppermute(value, AXES, [(i, i ^ chip << 1) for i in range(TRAV * BULK)])]
    all_to_all x3 -> x0, waiting for transfers between devices: 28.1 us -> none  [the longest x1 23.5 us: body(): lax.all_to_all(outgoing, 'bulk', split_axis=0, concat_axis=0, tiled=True)]
    dot_general x4 -> x0, matrix products: 28 us -> none  [the longest x1 19.9 us: network(): jnp.dot(columns, lax.all_gather(w_second, ('trav', 'bulk'), axis=0, tiled...]
    ppermute x0 -> x23, starting transfers between devices: none -> 25.3 us  [the longest x16 23.8 us: swap_chip(): lax.ppermute(value, AXES, [(i, i ^ chip << 1) for i in range(TRAV * BULK)])]
    pallas_call x0 -> x18, Pallas kernels: none -> 15.4 us  [run(): pl.pallas_call(kernel, out_shape=tuple(outs) if many else outs, in_specs=...]
    all_to_all x3 -> x0, starting transfers between devices: 12.7 us -> none  [the longest x1 5.17 us: body(): lax.all_to_all(slot_bucket, 'bulk', split_axis=0, concat_axis=0, tiled=True)]
    reshape x5 -> x0, local copies, waits for them, and re-layouts: 10 us -> none  [the longest x1 4.98 us: body(): jnp.repeat(parents.astype(jnp.float32), branch_slots, axis=0) + act_rows]
  transfers between devices with their start and end apart: 5 -> 23, of which waited for: 4 -> 14; matrix products, arithmetic and copies ran while one was open for 16% -> 0% of each run, Pallas kernels for 0% -> 7%
where the time goes in v2:
time: 92.2 us; the launch traced here: 92 us
  waiting for transfers between devices  46.2 us (50%)
  starting transfers between devices  25.3 us (27%)
  Pallas kernels  15.4 us (17%)
  local copies, waits for them, and re-layouts  4.3 us (5%)
    ppermute x16, waiting for transfers between devices, swap_chip(): lax.ppermute(value, AXES, [(i, i ^ chip << 1) for i in range(TRAV * BULK)])  41.2 us
    ppermute x16, starting transfers between devices, swap_chip(): lax.ppermute(value, AXES, [(i, i ^ chip << 1) for i in range(TRAV * BULK)])  23.8 us
    pallas_call x18, Pallas kernels, run(): pl.pallas_call(kernel, out_shape=tuple(outs) if many else outs, in_specs=...  15.4 us
    ppermute x7, waiting for transfers between devices, swap_core(): return lax.ppermute(value, AXES, [(i, i ^ 1) for i in range(TRAV * BULK)])  4.98 us
    unnamed x30, local copies, waits for them, and re-layouts  4.3 us
  transfers between devices with their start and end apart: 23, of which 14 were waited for; matrix products, arithmetic and copies ran while one was open for 0% of the time, Pallas kernels for 7%

profile of v2, /device:TPU:0, one launch (start us, length us, event | category | flops | bytes accessed | tf_op | source)
XLA Modules:
  0.0 92.0 jit_solution(5795148013388828827)
XLA Ops:
  0.6 0.5 collective-permute-start.1
  1.1 0.1 collective-permute-start
  1.2 0.7 copy-done.12
  1.9 0.7 copy-done.13
  2.6 0.3 shard_map.158
  2.9 0.4 collective-permute-start.2
  3.3 0.8 collective-permute-done.2.other_wanted
  4.1 0.9 %copy-done.2 = bf16[64,2048]{1,0:T(8,128)(2,1)S(1)} copy-done((bf16[64,2048]{1,0:T(8,128)(2,1)S(1)}, bf16[64,2048]{1,0:T(8,128)(2,1)}, u32[]{:S(2)}) %copy-start.2) | copy-done | bytes 262168
  5.1 0.9 copy-done.4
  6.0 0.1 shard_map.159
  6.1 3.8 %collective-permute-start.5 = (bf16[208,1024]{1,0:T(8,128)(2,1)S(1)}, bf16[208,1024]{1,0:T(8,128)(2,1)S(1)}, u32[]{:S(2)}, u32[]{:S(2)}) collective-permute-start(bf16[208,1024]{1,0:T(8,128)(2,1)S(1)} %get-tuple-element.21.refs_0_), channel_id=1, source_target_pairs={{0,6},{1,7},{2,4},{3,5},{4,2},{5,3},{6,0},{7,1},{8,14},{9,15},{10,... | collective-permute-start | bytes 1277960 | tf_op jit(solution)/shard_map/ppermute | solution.py:19
  9.9 0.5 collective-permute-start.3
  10.4 0.1 collective-permute-start.4
  10.5 4.0 %collective-permute-start.7 = (bf16[192,1024]{1,0:T(8,128)(2,1)S(1)}, bf16[192,1024]{1,0:T(8,128)(2,1)S(1)}, u32[]{:S(2)}, u32[]{:S(2)}) collective-permute-start(bf16[192,1024]{1,0:T(8,128)(2,1)S(1)} %get-tuple-element.23.refs_0_), channel_id=1, source_target_pairs={{0,24},{1,25},{2,26},{3,27},{4,28},{5,29},{6,30},{7,31},{8,16},{9,... | collective-permute-start | bytes 1179656 | tf_op jit(solution)/shard_map/ppermute | solution.py:19
  14.5 6.0 %collective-permute-done.5.refs_3_.refs_0_.refs_5_ = bf16[208,1024]{1,0:T(8,128)(2,1)S(1)} collective-permute-done((bf16[208,1024]{1,0:T(8,128)(2,1)S(1)}, bf16[208,1024]{1,0:T(8,128)(2,1)S(1)}, u32[]{:S(2)}, u32[]{:S(2)}) %collective-permute-start.5) | collective-permute-done | bytes 426016 | tf_op jit(solution)/shard_map/ppermute | solution.py:19
  20.5 8.9 %collective-permute-done.3.refs_1_ = bf16[208,1024]{1,0:T(8,128)(2,1)S(1)} collective-permute-done((bf16[208,1024]{1,0:T(8,128)(2,1)S(1)}, bf16[208,1024]{1,0:T(8,128)(2,1)S(1)}, u32[]{:S(2)}, u32[]{:S(2)}) %collective-permute-start.3) | collective-permute-done | bytes 426016 | tf_op jit(solution)/shard_map/ppermute | solution.py:19
  29.5 1.0 %copy-done = bf16[256,1024]{1,0:T(8,128)(2,1)S(1)} copy-done((bf16[256,1024]{1,0:T(8,128)(2,1)S(1)}, bf16[256,1024]{1,0:T(8,128)(2,1)}, u32[]{:S(2)}) %copy-start) | copy-done | bytes 524312
  30.5 0.5 shard_map.160
  31.0 0.6 collective-permute-done.6.refs_0_.refs_3_
  31.7 1.6 %collective-permute-start.9 = (bf16[448,1024]{1,0:T(8,128)(2,1)S(1)}, bf16[448,1024]{1,0:T(8,128)(2,1)S(1)}, u32[]{:S(2)}, u32[]{:S(2)}) collective-permute-start(bf16[448,1024]{1,0:T(8,128)(2,1)S(1)} %shard_map.162), channel_id=1, source_target_pairs={{0,4},{1,5},{2,6},{3,7},{4,0},{5,1},{6,2},{7,3},{8,12},{9,13},{10,... | collective-permute-start | bytes 2752520 | tf_op jit(solution)/shard_map/ppermute | solution.py:19
  33.4 1.6 %collective-permute-start.8 = (bf16[448,1024]{1,0:T(8,128)(2,1)S(1)}, bf16[448,1024]{1,0:T(8,128)(2,1)S(1)}, u32[]{:S(2)}, u32[]{:S(2)}) collective-permute-start(bf16[448,1024]{1,0:T(8,128)(2,1)S(1)} %shard_map.161), channel_id=1, source_target_pairs={{0,2},{1,3},{2,0},{3,1},{4,6},{5,7},{6,4},{7,5},{8,10},{9,11},{10,... | collective-permute-start | bytes 2752520 | tf_op jit(solution)/shard_map/ppermute | solution.py:19
  35.0 1.7 %collective-permute-start.11 = (bf16[192,1024]{1,0:T(8,128)(2,1)S(1)}, bf16[192,1024]{1,0:T(8,128)(2,1)S(1)}, u32[]{:S(2)}, u32[]{:S(2)}) collective-permute-start(bf16[192,1024]{1,0:T(8,128)(2,1)S(1)} %collective-permute-done.7.refs_1_.refs_4_), channel_id=1, source_target_pairs={{0,8},{1,9},{2,10},{3,11},{4,12},{5,13},{6,14},{7,15},{8,0},{9,1},... | collective-permute-start | bytes 1179656 | tf_op jit(solution)/shard_map/ppermute | solution.py:19
  36.7 1.7 %collective-permute-start.12 = (bf16[192,1024]{1,0:T(8,128)(2,1)S(1)}, bf16[192,1024]{1,0:T(8,128)(2,1)S(1)}, u32[]{:S(2)}, u32[]{:S(2)}) collective-permute-start(bf16[192,1024]{1,0:T(8,128)(2,1)S(1)} %shard_map.163), channel_id=1, source_target_pairs={{0,24},{1,25},{2,26},{3,27},{4,28},{5,29},{6,30},{7,31},{8,16},{9,... | collective-permute-start | bytes 1179656 | tf_op jit(solution)/shard_map/ppermute | solution.py:19
  38.4 0.6 collective-permute-start.10
  39.0 19.2 %collective-permute-done.10.refs_3_ = bf16[64,1024]{1,0:T(8,128)(2,1)S(1)} collective-permute-done((bf16[64,1024]{1,0:T(8,128)(2,1)S(1)}, bf16[64,1024]{1,0:T(8,128)(2,1)S(1)}, u32[]{:S(2)}, u32[]{:S(2)}) %collective-permute-start.10) | collective-permute-done | bytes 131104 | tf_op jit(solution)/shard_map/ppermute | solution.py:19
  58.3 0.1 collective-permute-start.13
  58.3 1.5 %collective-permute-done.13.refs_4_ = bf16[128,1024]{1,0:T(8,128)(2,1)S(1)} collective-permute-done((bf16[128,1024]{1,0:T(8,128)(2,1)S(1)}, bf16[128,1024]{1,0:T(8,128)(2,1)S(1)}, u32[]{:S(2)}, u32[]{:S(2)}) %collective-permute-start.13) | collective-permute-done | bytes 262176 | tf_op jit(solution)/shard_map/ppermute | solution.py:23
  59.9 1.0 %shard_map.165.mine = bf16[768,1024]{1,0:T(8,128)(2,1)S(1)} custom-call(s32[4,192]{1,0:T(4,128)S(1)} %bitcast.16, s32[1,192]{1,0:T(1,128)S(1)} %get-tuple-element.19.slot, bf16[192,1024]{1,0:T(8,128)(2,1)S(1)} %copy-done.1, bf16[128,1024]{1,0:T(8,128)(2,1)S(1)} %copy-done.3, bf16[64,1024]{1,0:T(8,128)(2,1)S(1)} %get-tuple-element.22.refs_0_, ...), custom_call_target="tpu_custom_call" | custom-call | tf_op jit(solution)/shard_map/pallas_call | solution.py:47
  60.8 0.2 collective-permute-start.14
  61.1 1.6 %collective-permute-start.15 = (bf16[128,1024]{1,0:T(8,128)(2,1)S(1)}, bf16[128,1024]{1,0:T(8,128)(2,1)S(1)}, u32[]{:S(2)}, u32[]{:S(2)}) collective-permute-start(bf16[128,1024]{1,0:T(8,128)(2,1)S(1)} %shard_map.166), channel_id=1, source_target_pairs={{0,2},{1,3},{2,0},{3,1},{4,6},{5,7},{6,4},{7,5},{8,10},{9,11},{10,... | collective-permute-start | bytes 786440 | tf_op jit(solution)/shard_map/ppermute | solution.py:19
  62.7 1.6 %collective-permute-start.16 = (bf16[64,1024]{1,0:T(8,128)(2,1)S(1)}, bf16[64,1024]{1,0:T(8,128)(2,1)S(1)}, u32[]{:S(2)}, u32[]{:S(2)}) collective-permute-start(bf16[64,1024]{1,0:T(8,128)(2,1)S(1)} %shard_map.167), channel_id=1, source_target_pairs={{0,4},{1,5},{2,6},{3,7},{4,0},{5,1},{6,2},{7,3},{8,12},{9,13},{10,... | collective-permute-start | bytes 393224 | tf_op jit(solution)/shard_map/ppermute | solution.py:19
  64.3 0.9 %collective-permute-start.17 = (bf16[64,1024]{1,0:T(8,128)(2,1)S(1)}, bf16[64,1024]{1,0:T(8,128)(2,1)S(1)}, u32[]{:S(2)}, u32[]{:S(2)}) collective-permute-start(bf16[64,1024]{1,0:T(8,128)(2,1)S(1)} %shard_map.168), channel_id=1, source_target_pairs={{0,8},{1,9},{2,10},{3,11},{4,12},{5,13},{6,14},{7,15},{8,0},{9,1},... | collective-permute-start | bytes 393224 | tf_op jit(solution)/shard_map/ppermute | solution.py:19
  65.2 3.0 %collective-permute-done.16.refs_11_ = bf16[64,1024]{1,0:T(8,128)(2,1)S(1)} collective-permute-done((bf16[64,1024]{1,0:T(8,128)(2,1)S(1)}, bf16[64,1024]{1,0:T(8,128)(2,1)S(1)}, u32[]{:S(2)}, u32[]{:S(2)}) %collective-permute-start.16) | collective-permute-done | bytes 131104 | tf_op jit(solution)/shard_map/ppermute | solution.py:19
  68.2 1.3 %collective-permute-done.17.refs_12_ = bf16[64,1024]{1,0:T(8,128)(2,1)S(1)} collective-permute-done((bf16[64,1024]{1,0:T(8,128)(2,1)S(1)}, bf16[64,1024]{1,0:T(8,128)(2,1)S(1)}, u32[]{:S(2)}, u32[]{:S(2)}) %collective-permute-start.17) | collective-permute-done | bytes 131104 | tf_op jit(solution)/shard_map/ppermute | solution.py:19
  69.5 0.2 collective-permute-done.15.refs_10_
  69.7 3.6 %shard_map.169.mine = bf16[1536,1024]{1,0:T(8,128)(2,1)S(1)} custom-call(bf16[768,1024]{1,0:T(8,128)(2,1)S(1)} %shard_map.165.mine, bf16[768,1024]{1,0:T(8,128)(2,1)S(1)} %collective-permute-done.14.theirs, f32[1,2048]{1,0:T(1,128)S(1)} %bitcast.14, bf16[192,1024]{1,0:T(8,128)(2,1)S(1)} %get-tuple-element.23.refs_0_, ...), custom_call_target="tpu_custom_call" | custom-call | tf_op jit(solution)/shard_map/pallas_call | solution.py:47
  73.3 0.1 collective-permute-start.18
  73.4 1.6 %collective-permute-start.20 = (bf16[224,1024]{1,0:T(8,128)(2,1)S(1)}, bf16[224,1024]{1,0:T(8,128)(2,1)S(1)}, u32[]{:S(2)}, u32[]{:S(2)}) collective-permute-start(bf16[224,1024]{1,0:T(8,128)(2,1)S(1)} %shard_map.172), channel_id=1, source_target_pairs={{0,4},{1,5},{2,6},{3,7},{4,0},{5,1},{6,2},{7,3},{8,12},{9,13},{10,... | collective-permute-start | bytes 1376264 | tf_op jit(solution)/shard_map/ppermute | solution.py:19
  75.0 1.6 %collective-permute-start.19 = (bf16[160,1024]{1,0:T(8,128)(2,1)S(1)}, bf16[160,1024]{1,0:T(8,128)(2,1)S(1)}, u32[]{:S(2)}, u32[]{:S(2)}) collective-permute-start(bf16[160,1024]{1,0:T(8,128)(2,1)S(1)} %shard_map.171), channel_id=1, source_target_pairs={{0,2},{1,3},{2,0},{3,1},{4,6},{5,7},{6,4},{7,5},{8,10},{9,11},{10,... | collective-permute-start | bytes 983048 | tf_op jit(solution)/shard_map/ppermute | solution.py:19
  76.6 0.9 %collective-permute-start.21 = (bf16[128,1024]{1,0:T(8,128)(2,1)S(1)}, bf16[128,1024]{1,0:T(8,128)(2,1)S(1)}, u32[]{:S(2)}, u32[]{:S(2)}) collective-permute-start(bf16[128,1024]{1,0:T(8,128)(2,1)S(1)} %shard_map.173), channel_id=1, source_target_pairs={{0,8},{1,9},{2,10},{3,11},{4,12},{5,13},{6,14},{7,15},{8,0},{9,1},... | collective-permute-start | bytes 786440 | tf_op jit(solution)/shard_map/ppermute | solution.py:19
  77.6 1.4 %collective-permute-done.18.theirs = bf16[1536,1024]{1,0:T(8,128)(2,1)S(1)} collective-permute-done((bf16[1536,1024]{1,0:T(8,128)(2,1)S(1)}, bf16[1536,1024]{1,0:T(8,128)(2,1)S(1)}, u32[]{:S(2)}, u32[]{:S(2)}) %collective-permute-start.18) | collective-permute-done | bytes 3145760 | tf_op jit(solution)/shard_map/ppermute | solution.py:23
  79.0 5.5 %shard_map.170.so_far = f32[1536,1024]{1,0:T(8,128)S(1)} custom-call(bf16[1536,1024]{1,0:T(8,128)(2,1)S(1)} %shard_map.169.mine, bf16[1536,1024]{1,0:T(8,128)(2,1)S(1)} %collective-permute-done.18.theirs, bf16[192,1024]{1,0:T(8,128)(2,1)S(1)} %get-tuple-element.23.refs_0_, bf16[208,1024]{1,0:T(8,128)(2,1)S(1)} %collective-permute-done.3.refs_1_, ...), custom_call_target="tpu_custom_call" | custom-call | tf_op jit(solution)/shard_map/pallas_call | solution.py:47
  84.5 0.3 collective-permute-done.21.refs_2_
  84.8 0.1 collective-permute-done.19.refs_0_
  84.9 1.5 %collective-permute-done.20.refs_1_ = bf16[224,1024]{1,0:T(8,128)(2,1)S(1)} collective-permute-done((bf16[224,1024]{1,0:T(8,128)(2,1)S(1)}, bf16[224,1024]{1,0:T(8,128)(2,1)S(1)}, u32[]{:S(2)}, u32[]{:S(2)}) %collective-permute-start.20) | collective-permute-done | bytes 458784 | tf_op jit(solution)/shard_map/ppermute | solution.py:19
  86.4 3.4 %shard_map.174 = (f32[8,768]{1,0:T(8,128)S(1)}, f32[8,768]{1,0:T(8,128)S(1)}) custom-call(bf16[1536,1024]{1,0:T(8,128)(2,1)S(1)} %shard_map.169.mine, bf16[1536,1024]{1,0:T(8,128)(2,1)S(1)} %collective-permute-done.18.theirs, f32[1536,1024]{1,0:T(8,128)S(1)} %shard_map.170.so_far, f32[1,2048]{1,0:T(1,128)S(1)} %bitcast.15, bf16[8,2048]{1,0:T(8,128)(2,1)S(1)} %bitcast.12, ...), custom_call_target="tpu_custom_call" | custom-call | tf_op jit(solution)/shard_map/pallas_call | solution.py:47
  89.9 1.2 %collective-permute-done.22.theirs = f32[8,768]{1,0:T(8,128)S(1)} collective-permute-done((f32[8,768]{1,0:T(8,128)S(1)}, f32[8,768]{1,0:T(8,128)S(1)}, u32[]{:S(2)}, u32[]{:S(2)}) %collective-permute-start.22) | collective-permute-done | bytes 24608 | tf_op jit(solution)/shard_map/ppermute | solution.py:23
  91.1 0.8 shard_map.175
  (46 shorter events, 0.4 us)
Async XLA Ops:
  0.6 3.5 %collective-permute-start.1 = (bf16[64,2048]{1,0:T(8,128)(2,1)}, bf16[64,2048]{1,0:T(8,128)(2,1)S(1)}, u32[]{:S(2)}, u32[]{:S(2)}) collective-permute-start(bf16[64,2048]{1,0:T(8,128)(2,1)} %w_second.1), channel_id=1, source_target_pairs={{0,1},{1,0},{2,3},{3,2},{4,5},{5,4},{6,7},{7,6},{8,9},{9,8},{10,11... | collective-permute-start | bytes 786440 | tf_op jit(solution)/shard_map/ppermute | solution.py:23
  1.1 3.0 %collective-permute-start = (bf16[32,2048]{1,0:T(8,128)(2,1)}, bf16[32,2048]{1,0:T(8,128)(2,1)S(1)}, u32[]{:S(2)}, u32[]{:S(2)}) collective-permute-start(bf16[32,2048]{1,0:T(8,128)(2,1)} %w_first.1), channel_id=1, source_target_pairs={{0,1},{1,0},{2,3},{3,2},{4,5},{5,4},{6,7},{7,6},{8,9},{9,8},{10,11... | collective-permute-start | bytes 393224 | tf_op jit(solution)/shard_map/ppermute | solution.py:23
  1.2 0.7 copy-start.12
  1.9 0.7 copy-start.13
  2.9 1.3 %collective-permute-start.2 = (s32[8,32]{1,0:T(8,128)S(1)}, s32[8,32]{1,0:T(8,128)S(1)}, u32[]{:S(2)}, u32[]{:S(2)}) collective-permute-start(s32[8,32]{1,0:T(8,128)S(1)} %get-tuple-element.20.wanted), channel_id=1, source_target_pairs={{0,1},{1,0},{2,3},{3,2},{4,5},{5,4},{6,7},{7,6},{8,9},{9,8},{10,11... | collective-permute-start | bytes 3080 | tf_op jit(solution)/shard_map/ppermute | solution.py:23
  4.1 1.0 %copy-start.2 = (bf16[64,2048]{1,0:T(8,128)(2,1)S(1)}, bf16[64,2048]{1,0:T(8,128)(2,1)}, u32[]{:S(2)}) copy-start(bf16[64,2048]{1,0:T(8,128)(2,1)} %w_second.1) | copy-start | bytes 786436
  5.1 0.9 copy-start.4
  6.1 14.5 %collective-permute-start.5 = (bf16[208,1024]{1,0:T(8,128)(2,1)S(1)}, bf16[208,1024]{1,0:T(8,128)(2,1)S(1)}, u32[]{:S(2)}, u32[]{:S(2)}) collective-permute-start(bf16[208,1024]{1,0:T(8,128)(2,1)S(1)} %get-tuple-element.21.refs_0_), channel_id=1, source_target_pairs={{0,6},{1,7},{2,4},{3,5},{4,2},{5,3},{6,0},{7,1},{8,14},{9,15},{10,... | collective-permute-start | bytes 1277960 | tf_op jit(solution)/shard_map/ppermute | solution.py:19
  9.9 19.6 %collective-permute-start.3 = (bf16[208,1024]{1,0:T(8,128)(2,1)S(1)}, bf16[208,1024]{1,0:T(8,128)(2,1)S(1)}, u32[]{:S(2)}, u32[]{:S(2)}) collective-permute-start(bf16[208,1024]{1,0:T(8,128)(2,1)S(1)} %get-tuple-element.21.refs_0_), channel_id=1, source_target_pairs={{0,2},{1,3},{2,0},{3,1},{4,6},{5,7},{6,4},{7,5},{8,10},{9,11},{10,... | collective-permute-start | bytes 1277960 | tf_op jit(solution)/shard_map/ppermute | solution.py:19
  10.4 19.0 %collective-permute-start.4 = (bf16[208,1024]{1,0:T(8,128)(2,1)S(1)}, bf16[208,1024]{1,0:T(8,128)(2,1)S(1)}, u32[]{:S(2)}, u32[]{:S(2)}) collective-permute-start(bf16[208,1024]{1,0:T(8,128)(2,1)S(1)} %get-tuple-element.21.refs_0_), channel_id=1, source_target_pairs={{0,4},{1,5},{2,6},{3,7},{4,0},{5,1},{6,2},{7,3},{8,12},{9,13},{10,... | collective-permute-start | bytes 1277960 | tf_op jit(solution)/shard_map/ppermute | solution.py:19
  10.5 20.5 %collective-permute-start.7 = (bf16[192,1024]{1,0:T(8,128)(2,1)S(1)}, bf16[192,1024]{1,0:T(8,128)(2,1)S(1)}, u32[]{:S(2)}, u32[]{:S(2)}) collective-permute-start(bf16[192,1024]{1,0:T(8,128)(2,1)S(1)} %get-tuple-element.23.refs_0_), channel_id=1, source_target_pairs={{0,24},{1,25},{2,26},{3,27},{4,28},{5,29},{6,30},{7,31},{8,16},{9,... | collective-permute-start | bytes 1179656 | tf_op jit(solution)/shard_map/ppermute | solution.py:19
  14.5 17.1 %collective-permute-start.6 = (bf16[192,1024]{1,0:T(8,128)(2,1)S(1)}, bf16[192,1024]{1,0:T(8,128)(2,1)S(1)}, u32[]{:S(2)}, u32[]{:S(2)}) collective-permute-start(bf16[192,1024]{1,0:T(8,128)(2,1)S(1)} %get-tuple-element.23.refs_0_), channel_id=1, source_target_pairs={{0,8},{1,9},{2,10},{3,11},{4,12},{5,13},{6,14},{7,15},{8,0},{9,1},... | collective-permute-start | bytes 1179656 | tf_op jit(solution)/shard_map/ppermute | solution.py:19
  29.5 1.0 %copy-start = (bf16[256,1024]{1,0:T(8,128)(2,1)S(1)}, bf16[256,1024]{1,0:T(8,128)(2,1)}, u32[]{:S(2)}) copy-start(bf16[256,1024]{1,0:T(8,128)(2,1)} %refs_4_.1) | copy-start | bytes 1572868
  31.7 28.2 %copy-start.1 = (bf16[192,1024]{1,0:T(8,128)(2,1)S(1)}, bf16[192,1024]{1,0:T(8,128)(2,1)}, u32[]{:S(2)}) copy-start(bf16[192,1024]{1,0:T(8,128)(2,1)} %parents.1) | copy-start | bytes 1179652
  31.7 28.2 %copy-start.3 = (bf16[128,1024]{1,0:T(8,128)(2,1)S(1)}, bf16[128,1024]{1,0:T(8,128)(2,1)}, u32[]{:S(2)}) copy-start(bf16[128,1024]{1,0:T(8,128)(2,1)} %act_table.1) | copy-start | bytes 786436
  31.7 28.2 %copy-start.9 = (s32[192,4]{0,1:T(4,128)S(1)}, s32[192,4]{0,1:T(4,128)}, u32[]{:S(2)}) copy-start(s32[192,4]{0,1:T(4,128)} %param.25) | copy-start | bytes 9220
  31.7 26.5 %collective-permute-start.9 = (bf16[448,1024]{1,0:T(8,128)(2,1)S(1)}, bf16[448,1024]{1,0:T(8,128)(2,1)S(1)}, u32[]{:S(2)}, u32[]{:S(2)}) collective-permute-start(bf16[448,1024]{1,0:T(8,128)(2,1)S(1)} %shard_map.162), channel_id=1, source_target_pairs={{0,4},{1,5},{2,6},{3,7},{4,0},{5,1},{6,2},{7,3},{8,12},{9,13},{10,... | collective-permute-start | bytes 2752520 | tf_op jit(solution)/shard_map/ppermute | solution.py:19
  33.4 24.8 %collective-permute-start.8 = (bf16[448,1024]{1,0:T(8,128)(2,1)S(1)}, bf16[448,1024]{1,0:T(8,128)(2,1)S(1)}, u32[]{:S(2)}, u32[]{:S(2)}) collective-permute-start(bf16[448,1024]{1,0:T(8,128)(2,1)S(1)} %shard_map.161), channel_id=1, source_target_pairs={{0,2},{1,3},{2,0},{3,1},{4,6},{5,7},{6,4},{7,5},{8,10},{9,11},{10,... | collective-permute-start | bytes 2752520 | tf_op jit(solution)/shard_map/ppermute | solution.py:19
  35.0 23.3 %collective-permute-start.11 = (bf16[192,1024]{1,0:T(8,128)(2,1)S(1)}, bf16[192,1024]{1,0:T(8,128)(2,1)S(1)}, u32[]{:S(2)}, u32[]{:S(2)}) collective-permute-start(bf16[192,1024]{1,0:T(8,128)(2,1)S(1)} %collective-permute-done.7.refs_1_.refs_4_), channel_id=1, source_target_pairs={{0,8},{1,9},{2,10},{3,11},{4,12},{5,13},{6,14},{7,15},{8,0},{9,1},... | collective-permute-start | bytes 1179656 | tf_op jit(solution)/shard_map/ppermute | solution.py:19
  36.7 21.5 %collective-permute-start.12 = (bf16[192,1024]{1,0:T(8,128)(2,1)S(1)}, bf16[192,1024]{1,0:T(8,128)(2,1)S(1)}, u32[]{:S(2)}, u32[]{:S(2)}) collective-permute-start(bf16[192,1024]{1,0:T(8,128)(2,1)S(1)} %shard_map.163), channel_id=1, source_target_pairs={{0,24},{1,25},{2,26},{3,27},{4,28},{5,29},{6,30},{7,31},{8,16},{9,... | collective-permute-start | bytes 1179656 | tf_op jit(solution)/shard_map/ppermute | solution.py:19
  38.4 19.8 %collective-permute-start.10 = (bf16[64,1024]{1,0:T(8,128)(2,1)S(1)}, bf16[64,1024]{1,0:T(8,128)(2,1)S(1)}, u32[]{:S(2)}, u32[]{:S(2)}) collective-permute-start(bf16[64,1024]{1,0:T(8,128)(2,1)S(1)} %get-tuple-element.26), channel_id=1, source_target_pairs={{0,6},{1,7},{2,4},{3,5},{4,2},{5,3},{6,0},{7,1},{8,14},{9,15},{10,... | collective-permute-start | bytes 393224 | tf_op jit(solution)/shard_map/ppermute | solution.py:19
  58.3 1.6 %collective-permute-start.13 = (bf16[128,1024]{1,0:T(8,128)(2,1)S(1)}, bf16[128,1024]{1,0:T(8,128)(2,1)S(1)}, u32[]{:S(2)}, u32[]{:S(2)}) collective-permute-start(bf16[128,1024]{1,0:T(8,128)(2,1)S(1)} %shard_map.164), channel_id=1, source_target_pairs={{0,1},{1,0},{2,3},{3,2},{4,5},{5,4},{6,7},{7,6},{8,9},{9,8},{10,11... | collective-permute-start | bytes 786440 | tf_op jit(solution)/shard_map/ppermute | solution.py:23
  59.9 9.9 %copy-start.7 = (f32[2048]{0:T(1024)S(1)}, f32[2048]{0:T(1024)}, u32[]{:S(2)}) copy-start(f32[2048]{0:T(1024)} %param.19) | copy-start | bytes 24580
  60.8 8.9 %collective-permute-start.14 = (bf16[768,1024]{1,0:T(8,128)(2,1)S(1)}, bf16[768,1024]{1,0:T(8,128)(2,1)S(1)}, u32[]{:S(2)}, u32[]{:S(2)}) collective-permute-start(bf16[768,1024]{1,0:T(8,128)(2,1)S(1)} %shard_map.165.mine), channel_id=1, source_target_pairs={{0,1},{1,0},{2,3},{3,2},{4,5},{5,4},{6,7},{7,6},{8,9},{9,8},{10,11... | collective-permute-start | bytes 4718600 | tf_op jit(solution)/shard_map/ppermute | solution.py:23
  61.1 8.7 %collective-permute-start.15 = (bf16[128,1024]{1,0:T(8,128)(2,1)S(1)}, bf16[128,1024]{1,0:T(8,128)(2,1)S(1)}, u32[]{:S(2)}, u32[]{:S(2)}) collective-permute-start(bf16[128,1024]{1,0:T(8,128)(2,1)S(1)} %shard_map.166), channel_id=1, source_target_pairs={{0,2},{1,3},{2,0},{3,1},{4,6},{5,7},{6,4},{7,5},{8,10},{9,11},{10,... | collective-permute-start | bytes 786440 | tf_op jit(solution)/shard_map/ppermute | solution.py:19
  62.7 5.5 %collective-permute-start.16 = (bf16[64,1024]{1,0:T(8,128)(2,1)S(1)}, bf16[64,1024]{1,0:T(8,128)(2,1)S(1)}, u32[]{:S(2)}, u32[]{:S(2)}) collective-permute-start(bf16[64,1024]{1,0:T(8,128)(2,1)S(1)} %shard_map.167), channel_id=1, source_target_pairs={{0,4},{1,5},{2,6},{3,7},{4,0},{5,1},{6,2},{7,3},{8,12},{9,13},{10,... | collective-permute-start | bytes 393224 | tf_op jit(solution)/shard_map/ppermute | solution.py:19
  64.3 5.3 %collective-permute-start.17 = (bf16[64,1024]{1,0:T(8,128)(2,1)S(1)}, bf16[64,1024]{1,0:T(8,128)(2,1)S(1)}, u32[]{:S(2)}, u32[]{:S(2)}) collective-permute-start(bf16[64,1024]{1,0:T(8,128)(2,1)S(1)} %shard_map.168), channel_id=1, source_target_pairs={{0,8},{1,9},{2,10},{3,11},{4,12},{5,13},{6,14},{7,15},{8,0},{9,1},... | collective-permute-start | bytes 393224 | tf_op jit(solution)/shard_map/ppermute | solution.py:19
  73.3 5.7 %collective-permute-start.18 = (bf16[1536,1024]{1,0:T(8,128)(2,1)S(1)}, bf16[1536,1024]{1,0:T(8,128)(2,1)S(1)}, u32[]{:S(2)}, u32[]{:S(2)}) collective-permute-start(bf16[1536,1024]{1,0:T(8,128)(2,1)S(1)} %shard_map.169.mine), channel_id=1, source_target_pairs={{0,1},{1,0},{2,3},{3,2},{4,5},{5,4},{6,7},{7,6},{8,9},{9,8},{10,11... | collective-permute-start | bytes 9437192 | tf_op jit(solution)/shard_map/ppermute | solution.py:23
  73.4 13.0 %collective-permute-start.20 = (bf16[224,1024]{1,0:T(8,128)(2,1)S(1)}, bf16[224,1024]{1,0:T(8,128)(2,1)S(1)}, u32[]{:S(2)}, u32[]{:S(2)}) collective-permute-start(bf16[224,1024]{1,0:T(8,128)(2,1)S(1)} %shard_map.172), channel_id=1, source_target_pairs={{0,4},{1,5},{2,6},{3,7},{4,0},{5,1},{6,2},{7,3},{8,12},{9,13},{10,... | collective-permute-start | bytes 1376264 | tf_op jit(solution)/shard_map/ppermute | solution.py:19
  75.0 9.9 %collective-permute-start.19 = (bf16[160,1024]{1,0:T(8,128)(2,1)S(1)}, bf16[160,1024]{1,0:T(8,128)(2,1)S(1)}, u32[]{:S(2)}, u32[]{:S(2)}) collective-permute-start(bf16[160,1024]{1,0:T(8,128)(2,1)S(1)} %shard_map.171), channel_id=1, source_target_pairs={{0,2},{1,3},{2,0},{3,1},{4,6},{5,7},{6,4},{7,5},{8,10},{9,11},{10,... | collective-permute-start | bytes 983048 | tf_op jit(solution)/shard_map/ppermute | solution.py:19
  76.6 9.8 %copy-start.5 = (bf16[2048,8]{0,1:T(8,128)(2,1)S(1)}, bf16[2048,8]{0,1:T(8,128)(2,1)}, u32[]{:S(2)}) copy-start(bf16[2048,8]{0,1:T(8,128)(2,1)} %param.22) | copy-start | bytes 98308
  76.6 9.8 %copy-start.8 = (f32[2048]{0:T(1024)S(1)}, f32[2048]{0:T(1024)}, u32[]{:S(2)}) copy-start(f32[2048]{0:T(1024)} %param.21) | copy-start | bytes 24580
  76.6 8.2 %collective-permute-start.21 = (bf16[128,1024]{1,0:T(8,128)(2,1)S(1)}, bf16[128,1024]{1,0:T(8,128)(2,1)S(1)}, u32[]{:S(2)}, u32[]{:S(2)}) collective-permute-start(bf16[128,1024]{1,0:T(8,128)(2,1)S(1)} %shard_map.173), channel_id=1, source_target_pairs={{0,8},{1,9},{2,10},{3,11},{4,12},{5,13},{6,14},{7,15},{8,0},{9,1},... | collective-permute-start | bytes 786440 | tf_op jit(solution)/shard_map/ppermute | solution.py:19
  86.4 4.7 %copy-start.6 = (s32[192,32]{0,1:T(8,128)S(1)}, s32[192,32]{0,1:T(8,128)}, u32[]{:S(2)}) copy-start(s32[192,32]{0,1:T(8,128)} %param.28) | copy-start | bytes 73732
  86.4 4.7 %copy-start.10 = (s32[192]{0:T(256)S(1)}, s32[192]{0:T(256)}, u32[]{:S(2)}) copy-start(s32[192]{0:T(256)} %param.24) | copy-start | bytes 2308
  86.4 4.7 %copy-start.11 = (s32[192]{0:T(256)S(1)}, s32[192]{0:T(256)}, u32[]{:S(2)}) copy-start(s32[192]{0:T(256)} %param.29) | copy-start | bytes 2308
  86.4 4.7 %copy-start.14 = (f32[8]{0:T(128)S(1)}, f32[8]{0:T(128)}, u32[]{:S(2)}) copy-start(f32[8]{0:T(128)} %param.23) | copy-start | bytes 100
  89.9 1.2 %collective-permute-start.22 = (f32[8,768]{1,0:T(8,128)S(1)}, f32[8,768]{1,0:T(8,128)S(1)}, u32[]{:S(2)}, u32[]{:S(2)}) collective-permute-start(f32[8,768]{1,0:T(8,128)S(1)} %get-tuple-element.33), channel_id=1, source_target_pairs={{0,1},{1,0},{2,3},{3,2},{4,5},{5,4},{6,7},{7,6},{8,9},{9,8},{10,11... | collective-permute-start | bytes 73736 | tf_op jit(solution)/shard_map/ppermute | solution.py:23

commit v3 on v0

--- a/solution.py
+++ b/solution.py
@@ -1,9 +1,370 @@
+import functools
+
 import jax
 import jax.numpy as jnp
 from jax import lax
+from jax.experimental import pallas as pl
+from jax.experimental.pallas import tpu as pltpu
 from jax.sharding import PartitionSpec as P
 
-tremble = 0.05
+TREMBLE = 0.05
+AXES = ("trav", "bulk")
+
+TRAV, BULK = 4, 8
+X, Y, D, A, B, C = 1, 2, 3, 4, 8, 12
+PLANE = (0, X, Y, D)
+ID_ROWS = 16
+
+
+def swap_chip(value, chip):
+    return lax.ppermute(value, AXES, [(i, i ^ (chip << 1)) for i in range(TRAV * BULK)])
+
+
+def swap_core(value):
+    return lax.ppermute(value, AXES, [(i, i ^ 1) for i in range(TRAV * BULK)])
+
+
+def iota(shape, dim):
+    return lax.broadcasted_iota(jnp.int32, shape, dim)
+
+
+def over_rows(a, b):
+    return lax.dot_general(a, b, (((0,), (0,)), ((), ())), preferred_element_type=jnp.float32)
+
+
+def my_core():
+    return lax.axis_index("bulk") & 1
+
+
+def my_chip():
+    return lax.axis_index("trav") * (BULK // 2) + (lax.axis_index("bulk") >> 1)
+
+
+def call(kernel, outs, mebibytes, scratch=()):
+    many = isinstance(outs, (list, tuple))
+    spec = pl.BlockSpec(memory_space=pltpu.VMEM)
+
+    def run(*args):
+        return pl.pallas_call(
+            kernel,
+            out_shape=tuple(outs) if many else outs,
+            in_specs=[spec] * len(args),
+            out_specs=(spec,) * len(outs) if many else spec,
+            scratch_shapes=list(scratch),
+            compiler_params=pltpu.CompilerParams(vmem_limit_bytes=mebibytes << 20),
+        )(*args)
+
+    return run
+
+
+def shape(rows, columns, dtype=jnp.bfloat16):
+    return jax.ShapeDtypeStruct((rows, columns), dtype)
+
+
+def across(a, b, precision=None):
+    return lax.dot_general(
+        a, b, (((1,), (1,)), ((), ())), preferred_element_type=jnp.float32, precision=precision
+    )
+
+
+def keep_kernel(w_first, w_second, owner, row, keep, ids):
+    one, half = w_first.shape[0], keep.shape[1]
+    here = pl.ds(pl.multiple_of(my_core() * half, half), half)
+    keep[:one, :] = w_first[:, here]
+    keep[one:, :] = w_second[:, here]
+    ids[:1, :] = owner[...]
+    ids[1:, :] = row[...]
+
+
+def join_kernel(depths, keep, ids, other_first, other_second, other_owner, other_row, out, out_ids):
+    core, half = my_core(), out.shape[1]
+    here = pl.ds(pl.multiple_of(core * half, half), half)
+    begin = 0
+    for depth, other in zip(depths, (other_first, other_second)):
+        for to, rows in ((core, keep[begin : begin + depth, :]), (1 - core, other[:, here])):
+            place = pl.ds(pl.multiple_of(2 * begin + to * depth, depth), depth)
+            for target in (out, out_ids):
+                target[place, :] = rows
+        begin += depth
+    parts = [ref[...].astype(jnp.float32) for ref in (ids, other_owner, other_row)]
+    count = ids.shape[1]
+    parts = jnp.concatenate(parts + [jnp.zeros((ID_ROWS - 4, count), jnp.float32)], axis=0)
+    parts = jnp.concatenate([parts, jnp.zeros((ID_ROWS, half - count), jnp.float32)], axis=1)
+    out_ids[2 * begin :, :] = parts.astype(jnp.bfloat16)
+
+
+def ranks_of(hits):
+    count = hits.shape[1]
+    before = (iota((count, count), 0) < iota((count, count), 1)).astype(jnp.bfloat16)
+    return jnp.dot(hits.astype(jnp.bfloat16), before, preferred_element_type=jnp.float32)
+
+
+def meta_kernel(capacity, owner, actions, out):
+    partner = owner[...] ^ lax.axis_index("bulk")
+    count = owner.shape[1]
+    hits = (partner == iota((BULK, count), 0)).astype(jnp.float32)
+    rank = jnp.sum(ranks_of(hits) * hits, axis=0, keepdims=True)
+    slot = partner.astype(jnp.float32) * capacity + rank
+    rows = out.shape[0]
+    parts = [actions[...].astype(jnp.float32), slot, jnp.zeros((rows - actions.shape[0] - 1, count), jnp.float32)]
+    parts = jnp.concatenate(parts, axis=0)
+    out[...] = jnp.concatenate([parts, jnp.zeros((rows, out.shape[1] - count), jnp.float32)], axis=1).astype(jnp.bfloat16)
+
+
+def serve_kernel(capacity, count, *refs):
+    asked, table, outs = refs[: len(PLANE)], refs[len(PLANE)], refs[len(PLANE) + 1 :]
+    buckets = table.shape[0]
+    me = lax.axis_index("bulk")
+    owners, rows = [], []
+    for ids in asked:
+        block = ids[ids.shape[0] - ID_ROWS :, :count].astype(jnp.float32)
+        for core in (0, 1):
+            owners.append(block[2 * core : 2 * core + 1, :])
+            rows.append(block[2 * core + 1 : 2 * core + 2, :])
+    owners, rows = jnp.concatenate(owners, axis=0), jnp.concatenate(rows, axis=0)
+    hits = (owners.astype(jnp.int32) == me).astype(jnp.float32)
+    ranks = ranks_of(hits).astype(jnp.int32)
+    rows = (rows * hits).astype(jnp.bfloat16)
+    for n, out in enumerate(outs):
+        wants = []
+        for j in (2 * n, 2 * n + 1):
+            at_rank = (ranks[j : j + 1, :] == iota((capacity, count), 0)).astype(jnp.bfloat16)
+            wants.append(across(rows, at_rank)[j : j + 1, :])
+        want = jnp.concatenate(wants, axis=1).astype(jnp.int32)
+        onehot = (iota((buckets, want.shape[1]), 0) == want).astype(jnp.bfloat16)
+        out[...] = over_rows(onehot, table[...]).astype(jnp.bfloat16)
+
+
+def inputs_kernel(capacity, branch_slots, act_table, mine, theirs, out):
+    served = len(PLANE) * 2 * capacity
+    rows = out.shape[0] // (2 * branch_slots)
+    to = 0
+    for which, ref in enumerate((mine, theirs)):
+        parts = []
+        for n in range(len(PLANE)):
+            for core in (0, 1):
+                begin = (2 * n + core) * capacity
+                parts.append((mine, theirs)[which ^ core][begin : begin + capacity, :])
+        buckets = jnp.concatenate(parts, axis=0)
+        meta = ref[served + rows :, :rows].astype(jnp.float32).astype(jnp.int32)
+        onehot = (meta[branch_slots : branch_slots + 1, :] == iota((served, rows), 0)).astype(jnp.bfloat16)
+        bucket = over_rows(onehot, buckets)
+        parent = ref[served : served + rows, :].astype(jnp.float32)
+        for c in range(branch_slots):
+            onehot = (meta[c : c + 1, :] == iota((act_table.shape[0], rows), 0)).astype(jnp.bfloat16)
+            base = (parent + over_rows(onehot, act_table[...])).astype(jnp.bfloat16)
+            out[to : to + rows, :] = (base.astype(jnp.float32) + bucket).astype(jnp.bfloat16)
+            to += rows
+
+
+def place_kernel(pieces, depth, *refs):
+    refs, out = refs[:-1], refs[-1]
+    for chip, which, begin, row, count in pieces:
+        to = pl.multiple_of((my_chip() ^ chip) * depth + row, 16)
+        out[pl.ds(to, count), :] = refs[which][begin : begin + count, :]
+
+
+def first_kernel(depth, inputs, home, other, bias, out):
+    half = home.shape[1]
+    chips = half // depth
+    me, core = my_chip(), my_core()
+    rows, group = inputs.shape[0] // 2, 4
+    for which, weights in enumerate((home, other)):
+        side = core ^ which
+        base = ((me // chips) ^ side) * half
+        for first in range(0, chips, group):
+            spots = [(n ^ me) & (chips - 1) for n in range(first, first + group)]
+            columns = [pl.ds(pl.multiple_of(spot * depth, depth), depth) for spot in spots]
+            shifts = [pl.ds(pl.multiple_of(side * half + spot * depth, depth), depth) for spot in spots]
+            block = jnp.concatenate([weights[:, column] for column in columns], axis=1)
+            shift = jnp.concatenate([bias[:, column] for column in shifts], axis=1)
+            to = pl.ds(pl.multiple_of(base + first * depth, group * depth), group * depth)
+            for m in (0, rows):
+                total = jnp.dot(inputs[m : m + rows, :], block, preferred_element_type=jnp.float32)
+                out[m : m + rows, to] = jnp.maximum(total + shift, 0.0).astype(jnp.bfloat16)
+
+
+def line_up(pieces, refs, depth, weights):
+    order = list(dict.fromkeys(piece[0] for piece in pieces))
+    for name, which, begin, row, count in pieces:
+        to = order.index(name) * depth + row
+        weights[to : to + count, :] = refs[which][begin : begin + count, :]
+    return [slice(name * depth, (name + 1) * depth) for name in order]
+
+
+def second_kernel(pieces, depth, hidden, *refs):
+    refs, (out, weights) = refs[:-2], refs[-2:]
+    columns = line_up(pieces, refs, depth, weights)
+    step, rows = 512, hidden.shape[0] // 2
+    for m in (0, rows):
+        picked = jnp.concatenate([hidden[m : m + rows, column] for column in columns], axis=1)
+        for n in range(0, out.shape[1], step):
+            out[m : m + rows, n : n + step] = jnp.dot(
+                picked, weights[:, n : n + step], preferred_element_type=jnp.float32
+            )
+
+
+def finish_second_kernel(pieces, depth, hidden, so_far, bias, w_head, *refs):
+    refs, (out_mine, out_theirs, weights) = refs[:-3], refs[-3:]
+    columns = line_up(pieces, refs, depth, weights)
+    half, core = so_far.shape[1], my_core()
+    step, rows = 512, hidden.shape[0] // 2
+    for m, out in ((0, out_mine), (rows, out_theirs)):
+        picked = jnp.concatenate([hidden[m : m + rows, column] for column in columns], axis=1)
+        advantage = jnp.zeros((rows, w_head.shape[0]), jnp.float32)
+        for n in range(0, half, step):
+            here = pl.ds(pl.multiple_of(core * half + n, step), step)
+            total = so_far[m : m + rows, n : n + step] + jnp.dot(
+                picked, weights[:, n : n + step], preferred_element_type=jnp.float32
+            )
+            layer = jnp.maximum(total + bias[:, here], 0.0).astype(jnp.bfloat16)
+            advantage = advantage + across(layer, w_head[:, here])
+        out[...] = advantage.T
+
+
+def stack_kernel(places, *refs):
+    refs, out = refs[:-1], refs[-1]
+    to = 0
+    for ref, (begin, count) in zip(refs, places):
+        out[to : to + count, :] = ref[begin : begin + count, :]
+        to += count
+
+
+def stack(*parts):
+    arrays, places = [part[0] for part in parts], [part[1:] for part in parts]
+    total = sum(count for _, count in places)
+    out = shape(total, arrays[0].shape[1], arrays[0].dtype)
+    return call(functools.partial(stack_kernel, places), out, 4)(*arrays)
+
+
+def last_kernel(counts, ancestor, legal, b_head, mine, theirs, strategy, values):
+    actions = b_head.shape[1]
+    rows = counts.shape[1]
+    diagonal = iota((actions, actions), 0) == iota((actions, actions), 1)
+    shift = jnp.sum(jnp.where(diagonal, b_head[...], 0.0), axis=1, keepdims=True)
+    first_action = (iota((actions, rows), 0) == 0).astype(jnp.float32)
+    total_value = jnp.zeros((1, rows), jnp.float32)
+    for c in range(mine.shape[1] // rows):
+        here = slice(c * rows, (c + 1) * rows)
+        advantage = mine[:, here] + theirs[:, here] + shift
+        allowed = jnp.maximum(legal[c * actions : (c + 1) * actions, :].astype(jnp.float32), first_action)
+        positive = allowed * (jnp.maximum(advantage, 0.0) + TREMBLE)
+        sigma = positive / jnp.sum(positive, axis=0, keepdims=True)
+        live = (counts[...] > c).astype(jnp.float32)
+        strategy[c * actions : (c + 1) * actions, :] = sigma * live
+        total_value = total_value + live * jnp.sum(sigma * advantage, axis=0, keepdims=True)
+    value = total_value / counts[...].astype(jnp.float32)
+    at_node = (ancestor[...] == iota((values.shape[1], rows), 0)).astype(jnp.float32)
+    values[...] = across(value, at_node, lax.Precision.HIGHEST)
+
+
+def body(
+    parents,
+    act_table,
+    bucket_table,
+    w_first,
+    b_first,
+    w_second,
+    b_second,
+    w_head,
+    b_head,
+    branch_counts,
+    sampled_actions,
+    bucket_owner,
+    bucket_row,
+    legal_mask,
+    ancestor,
+):
+    par_count, feature_count = parents.shape
+    branch_slots = sampled_actions.shape[1]
+    branches = par_count * branch_slots
+    hidden_units = w_first.shape[1]
+    half = hidden_units // 2
+    depth_one, depth_two = w_first.shape[0], w_second.shape[0]
+    chip_one, chip_two = 2 * depth_one, 2 * depth_two
+    depth = chip_one + chip_two
+    capacity = max(2, (4 * par_count + 3 * BULK - 1) // (3 * BULK))
+    wide = 2 * capacity
+
+    owner, row = bucket_owner.T, bucket_row[None, :]
+    keep, ids = call(keep_kernel, (shape(depth // 2, half), shape(2, par_count, jnp.int32)), 4)(
+        w_first, w_second, owner, row
+    )
+    own, own_ids = call(
+        functools.partial(join_kernel, (depth_one, depth_two)), (shape(depth, half), shape(depth + ID_ROWS, half)), 4
+    )(keep, ids, swap_core(w_first), swap_core(w_second), swap_core(owner), swap_core(row))
+    from_x, from_y, from_d = [swap_chip(own_ids, chip) for chip in PLANE[1:]]
+    from_a, from_b = [swap_chip(own, chip) for chip in (A, B)]
+    meta = call(functools.partial(meta_kernel, capacity), shape(ID_ROWS, feature_count), 4)(owner, sampled_actions.T)
+    table = stack((bucket_table, 0, bucket_table.shape[0]))
+    from_x, from_y, from_d, from_a, from_b, table = lax.optimization_barrier(
+        (from_x, from_y, from_d, from_a, from_b, table)
+    )
+
+    served = call(
+        functools.partial(serve_kernel, capacity, par_count), (shape(wide, feature_count),) * len(PLANE), 6
+    )(own_ids, from_x, from_y, from_d, table)
+    few = chip_one // 2
+    x_ab = swap_chip(stack((from_a, few, depth - few), (from_b, 0, depth), (served[1], 0, wide)), X)
+    y_ab = swap_chip(stack((from_a, few, depth - few), (from_b, 0, depth), (served[2], 0, wide)), Y)
+    rows_d = swap_chip(stack((served[3], 0, wide), (from_b, 0, chip_one)), D)
+    c_da = swap_chip(stack((from_b, 0, depth), (from_d, 0, chip_one), (from_x, 0, few), (from_y, 0, few)), A)
+    plane_c = swap_chip(stack(*((rows, 0, chip_one) for rows in (from_x, from_y, from_d))), C)
+    x_ab, y_ab, rows_d, c_da, plane_c = lax.optimization_barrier((x_ab, y_ab, rows_d, c_da, plane_c))
+
+    cut = chip_two // 2
+    at_a, at_b = chip_one - few, depth - few + chip_one
+    x_c = swap_chip(stack((c_da, chip_one, chip_two), (y_ab, at_a, cut), (y_ab, at_b, cut)), X)
+    y_c = swap_chip(stack((c_da, chip_one, chip_two), (x_ab, at_a + cut, cut), (x_ab, at_b + cut, cut)), Y)
+    d_c = swap_chip(stack((from_d, chip_one, chip_two)), C)
+
+    end = 2 * depth - few
+    mine = stack(
+        (served[0], 0, wide), (x_ab, end, wide), (y_ab, end, wide), (rows_d, 0, wide),
+        (parents, 0, par_count), (meta, 0, ID_ROWS)
+    )
+    inputs = call(functools.partial(inputs_kernel, capacity, branch_slots), shape(2 * branches, feature_count), 10)(
+        act_table, mine, swap_core(mine)
+    )
+
+    arrays = [own, from_x, from_y, from_a, from_b, from_d, x_ab, y_ab, c_da]
+    near = [(chip, n) for n, chip in enumerate((0, X, Y, A, B, D))]
+    first_pieces = [(chip, n, 0, 0, chip_one) for chip, n in near] + [(C, 8, 0, 0, chip_one)]
+    for n, chip in ((6, X), (7, Y)):
+        first_pieces.append((chip ^ A, 8, depth + chip_one + (n - 6) * few, 0, few))
+        first_pieces += [(chip ^ A, n, 0, few, chip_one - few), (chip ^ B, n, depth - few, 0, chip_one)]
+    first_pieces += [(D ^ A, 8, depth, 0, chip_one), (D ^ B, 9, wide, 0, chip_one)]
+    first_pieces += [(chip ^ C, 10, n * chip_one, 0, chip_one) for n, chip in enumerate((X, Y, D))]
+    weights = call(functools.partial(place_kernel, first_pieces, chip_one), shape(feature_count, half), 4)(
+        *arrays, rows_d, plane_c
+    )
+    hidden = call(functools.partial(first_kernel, chip_two), shape(2 * branches, hidden_units), 12)(
+        inputs, weights, swap_core(weights), b_first[None, :]
+    )
+
+    early = [(chip, n, chip_one, 0, chip_two) for chip, n in near] + [(C, 8, chip_one, 0, chip_two)]
+    for n, chip in ((6, X), (7, Y)):
+        early += [(chip ^ A, n, at_a, 0, chip_two), (chip ^ B, n, at_b, 0, chip_two)]
+    early.sort()
+    so_far = call(
+        functools.partial(second_kernel, early, chip_two),
+        shape(2 * branches, half, jnp.float32),
+        16,
+        [pltpu.VMEM((len(early) * chip_two, half), jnp.bfloat16)],
+    )(hidden, *arrays)
+    late = [(X ^ C, 0, 0, 0, chip_two), (Y ^ C, 1, 0, 0, chip_two), (D ^ C, 2, 0, 0, chip_two)]
+    late += [(D ^ A, 0, chip_two, 0, cut), (D ^ A, 1, chip_two, cut, cut)]
+    late += [(D ^ B, 0, chip_two + cut, 0, cut), (D ^ B, 1, chip_two + cut, cut, cut)]
+    mine, theirs = call(
+        functools.partial(finish_second_kernel, late, chip_two),
+        (shape(w_head.shape[1], branches, jnp.float32),) * 2,
+        14,
+        [pltpu.VMEM((5 * chip_two, half), jnp.bfloat16)],
+    )(hidden, so_far, b_second[None, :], w_head.T, x_c, y_c, d_c)
+    strategy, values = call(
+        last_kernel, (shape(legal_mask.shape[1], par_count, jnp.float32), shape(1, par_count // 4, jnp.float32)), 4
+    )(branch_counts[None, :], ancestor[None, :], legal_mask.T, b_head[None, :], mine, swap_core(theirs))
+    return (strategy.T, values.reshape(-1))
 
 
 def network(inputs, w_first, b_first, w_second, b_second, w_head, b_head):
@@ -24,7 +385,7 @@
     return jnp.dot(hidden_two, w_head, preferred_element_type=jnp.float32) + b_head
 
 
-def body(
+def general_body(
     parents,
     act_table,
     bucket_table,
@@ -96,7 +457,7 @@
     allowed = jnp.maximum(
         legal_mask.reshape(par_count, branch_slots, action_count).astype(jnp.float32), first_action
     )
-    positive = allowed * (jnp.maximum(advantage, 0.0) + tremble)
+    positive = allowed * (jnp.maximum(advantage, 0.0) + TREMBLE)
     sigma = positive / jnp.sum(positive, axis=-1, keepdims=True)
     live = (jnp.arange(branch_slots)[None, :] < branch_counts[:, None]).astype(jnp.float32)
     strategy = (sigma * live[:, :, None]).reshape(par_count, branch_slots * action_count)
@@ -109,26 +470,27 @@
 
 
 def solution(mesh):
+    laid_out = (mesh.shape["trav"], mesh.shape["bulk"]) == (TRAV, BULK)
     return jax.shard_map(
-        body,
+        body if laid_out else general_body,
         mesh=mesh,
         in_specs=(
-            P(("trav", "bulk"), None),
+            P(AXES, None),
             P(),
             P("bulk", None),
-            P(("trav", "bulk"), None),
+            P(AXES, None),
             P(),
-            P(("trav", "bulk"), None),
+            P(AXES, None),
             P(),
             P(),
             P(),
-            P(("trav", "bulk")),
-            P(("trav", "bulk"), None),
-            P(("trav", "bulk"), None),
-            P(("trav", "bulk")),
-            P(("trav", "bulk"), None),
-            P(("trav", "bulk")),
+            P(AXES),
+            P(AXES, None),
+            P(AXES, None),
+            P(AXES),
+            P(AXES, None),
+            P(AXES),
         ),
-        out_specs=(P(("trav", "bulk"), None), P(("trav", "bulk"))),
+        out_specs=(P(AXES, None), P(AXES)),
         check_vma=False,
     )

time: 206 us -> 84.4 us (0.41)
  waiting for transfers between devices: 116 us -> 36.2 us
  matrix products: 28 us -> 0 us
  local copies, waits for them, and re-layouts: 27.4 us -> 4.32 us
  Pallas kernels: 0 us -> 20.8 us
  between operations: 14.3 us -> 0.97 us
  starting transfers between devices: 12.8 us -> 21.8 us
  other arithmetic: 6.8 us -> 0 us
    all_gather x2 -> x0, waiting for transfers between devices: 86.5 us -> none  [the longest x1 79.1 us: network(): lax.all_gather(w_second, ('trav', 'bulk'), axis=0, tiled=True)]
    ppermute x0 -> x20, waiting for transfers between devices: none -> 36.2 us  [the longest x13 35.1 us: swap_chip(): lax.ppermute(value, AXES, [(i, i ^ chip << 1) for i in range(TRAV * BULK)])]
    all_to_all x3 -> x0, waiting for transfers between devices: 28.1 us -> none  [the longest x1 23.5 us: body(): lax.all_to_all(outgoing, 'bulk', split_axis=0, concat_axis=0, tiled=True)]
    dot_general x4 -> x0, matrix products: 28 us -> none  [the longest x1 19.9 us: network(): jnp.dot(columns, lax.all_gather(w_second, ('trav', 'bulk'), axis=0, tiled...]
    ppermute x0 -> x20, starting transfers between devices: none -> 21.8 us  [the longest x13 19.9 us: swap_chip(): lax.ppermute(value, AXES, [(i, i ^ chip << 1) for i in range(TRAV * BULK)])]
    pallas_call x0 -> x20, Pallas kernels: none -> 20.8 us  [run(): pl.pallas_call(kernel, out_shape=tuple(outs) if many else outs, in_specs=...]
    all_to_all x3 -> x0, starting transfers between devices: 12.7 us -> none  [the longest x1 5.17 us: body(): lax.all_to_all(slot_bucket, 'bulk', split_axis=0, concat_axis=0, tiled=True)]
    reshape x5 -> x0, local copies, waits for them, and re-layouts: 10 us -> none  [the longest x1 4.98 us: body(): jnp.repeat(parents.astype(jnp.float32), branch_slots, axis=0) + act_rows]
  transfers between devices with their start and end apart: 5 -> 20, of which waited for: 4 -> 6; matrix products, arithmetic and copies ran while one was open for 16% -> 0% of each run, Pallas kernels for 0% -> 17%
where the time goes in v3:
time: 84.4 us; the launch traced here: 84.1 us
  waiting for transfers between devices  36.2 us (43%)
  starting transfers between devices  21.8 us (26%)
  Pallas kernels  20.8 us (25%)
  local copies, waits for them, and re-layouts  4.32 us (5%)
  between operations  0.97 us (1%)
    ppermute x13, waiting for transfers between devices, swap_chip(): lax.ppermute(value, AXES, [(i, i ^ chip << 1) for i in range(TRAV * BULK)])  35.1 us
    pallas_call x20, Pallas kernels, run(): pl.pallas_call(kernel, out_shape=tuple(outs) if many else outs, in_specs=...  20.8 us
    ppermute x13, starting transfers between devices, swap_chip(): lax.ppermute(value, AXES, [(i, i ^ chip << 1) for i in range(TRAV * BULK)])  19.9 us
    unnamed x32, local copies, waits for them, and re-layouts  4.32 us
    ppermute x7, starting transfers between devices, swap_core(): return lax.ppermute(value, AXES, [(i, i ^ 1) for i in range(TRAV * BULK)])  1.91 us
  transfers between devices with their start and end apart: 20, of which 6 were waited for; matrix products, arithmetic and copies ran while one was open for 0% of the time, Pallas kernels for 17%

profile of v3, /device:TPU:0, one launch (start us, length us, event | category | flops | bytes accessed | tf_op | source)
XLA Modules:
  0.0 84.1 jit_solution(13986131029960495912)
XLA Ops:
  0.6 0.5 collective-permute-start.1
  1.1 0.1 collective-permute-start
  1.2 0.4 collective-permute-start.2
  1.7 0.1 collective-permute-start.3
  1.7 0.9 %copy-done.2 = bf16[64,2048]{1,0:T(8,128)(2,1)S(1)} copy-done((bf16[64,2048]{1,0:T(8,128)(2,1)S(1)}, bf16[64,2048]{1,0:T(8,128)(2,1)}, u32[]{:S(2)}) %copy-start.2) | copy-done | bytes 262168
  2.7 0.9 %copy-done.4 = bf16[32,2048]{1,0:T(8,128)(2,1)S(1)} copy-done((bf16[32,2048]{1,0:T(8,128)(2,1)S(1)}, bf16[32,2048]{1,0:T(8,128)(2,1)}, u32[]{:S(2)}) %copy-start.4) | copy-done | bytes 131096
  3.6 0.7 copy-done.9
  4.3 0.7 copy-done.12
  5.0 0.1 shard_map.159
  5.1 3.0 %collective-permute-start.4 = (bf16[208,1024]{1,0:T(8,128)(2,1)S(1)}, bf16[208,1024]{1,0:T(8,128)(2,1)S(1)}, u32[]{:S(2)}, u32[]{:S(2)}) collective-permute-start(bf16[208,1024]{1,0:T(8,128)(2,1)S(1)} %get-tuple-element.27.refs_0_), channel_id=1, source_target_pairs={{0,2},{1,3},{2,0},{3,1},{4,6},{5,7},{6,4},{7,5},{8,10},{9,11},{10,... | collective-permute-start | bytes 1277960 | tf_op jit(solution)/shard_map/ppermute | solution.py:20
  8.1 1.5 %collective-permute-start.5 = (bf16[208,1024]{1,0:T(8,128)(2,1)S(1)}, bf16[208,1024]{1,0:T(8,128)(2,1)S(1)}, u32[]{:S(2)}, u32[]{:S(2)}) collective-permute-start(bf16[208,1024]{1,0:T(8,128)(2,1)S(1)} %get-tuple-element.27.refs_0_), channel_id=1, source_target_pairs={{0,4},{1,5},{2,6},{3,7},{4,0},{5,1},{6,2},{7,3},{8,12},{9,13},{10,... | collective-permute-start | bytes 1277960 | tf_op jit(solution)/shard_map/ppermute | solution.py:20
  9.6 0.0 collective-permute-start.6
  9.6 2.0 %collective-permute-start.7 = (bf16[192,1024]{1,0:T(8,128)(2,1)S(1)}, bf16[192,1024]{1,0:T(8,128)(2,1)S(1)}, u32[]{:S(2)}, u32[]{:S(2)}) collective-permute-start(bf16[192,1024]{1,0:T(8,128)(2,1)S(1)} %get-tuple-element.28.refs_0_), channel_id=1, source_target_pairs={{0,8},{1,9},{2,10},{3,11},{4,12},{5,13},{6,14},{7,15},{8,0},{9,1},... | collective-permute-start | bytes 1179656 | tf_op jit(solution)/shard_map/ppermute | solution.py:20
  11.6 2.6 %collective-permute-start.8 = (bf16[192,1024]{1,0:T(8,128)(2,1)S(1)}, bf16[192,1024]{1,0:T(8,128)(2,1)S(1)}, u32[]{:S(2)}, u32[]{:S(2)}) collective-permute-start(bf16[192,1024]{1,0:T(8,128)(2,1)S(1)} %get-tuple-element.28.refs_0_), channel_id=1, source_target_pairs={{0,16},{1,17},{2,18},{3,19},{4,20},{5,21},{6,22},{7,23},{8,24},{9,... | collective-permute-start | bytes 1179656 | tf_op jit(solution)/shard_map/ppermute | solution.py:20
  14.2 1.0 %copy-done = bf16[256,1024]{1,0:T(8,128)(2,1)S(1)} copy-done((bf16[256,1024]{1,0:T(8,128)(2,1)S(1)}, bf16[256,1024]{1,0:T(8,128)(2,1)}, u32[]{:S(2)}) %copy-start) | copy-done | bytes 524312
  15.3 13.2 %collective-permute-done.7.refs_0_.refs_3_ = bf16[192,1024]{1,0:T(8,128)(2,1)S(1)} collective-permute-done((bf16[192,1024]{1,0:T(8,128)(2,1)S(1)}, bf16[192,1024]{1,0:T(8,128)(2,1)S(1)}, u32[]{:S(2)}, u32[]{:S(2)}) %collective-permute-start.7) | collective-permute-done | bytes 393248 | tf_op jit(solution)/shard_map/ppermute | solution.py:20
  28.5 2.5 %collective-permute-done.8.refs_1_.refs_0_.refs_4_ = bf16[192,1024]{1,0:T(8,128)(2,1)S(1)} collective-permute-done((bf16[192,1024]{1,0:T(8,128)(2,1)S(1)}, bf16[192,1024]{1,0:T(8,128)(2,1)S(1)}, u32[]{:S(2)}, u32[]{:S(2)}) %collective-permute-start.8) | collective-permute-done | bytes 393248 | tf_op jit(solution)/shard_map/ppermute | solution.py:20
  31.0 1.5 %shard_map.161 = (bf16[64,1024]{1,0:T(8,128)(2,1)S(1)}, bf16[64,1024]{1,0:T(8,128)(2,1)S(1)}, bf16[64,1024]{1,0:T(8,128)(2,1)S(1)}, bf16[64,1024]{1,0:T(8,128)(2,1)S(1)}) custom-call(bf16[208,1024]{1,0:T(8,128)(2,1)S(1)} %get-tuple-element.27.refs_0_, bf16[208,1024]{1,0:T(8,128)(2,1)S(1)} %collective-permute-done.4.refs_1_.refs_2_.refs_0_, ...), custom_call_target="tpu_custom_call" | custom-call | tf_op jit(solution)/shard_map/pallas_call | solution.py:48
  32.5 0.1 shard_map.163
  32.6 1.6 %collective-permute-start.10 = (bf16[416,1024]{1,0:T(8,128)(2,1)S(1)}, bf16[416,1024]{1,0:T(8,128)(2,1)S(1)}, u32[]{:S(2)}, u32[]{:S(2)}) collective-permute-start(bf16[416,1024]{1,0:T(8,128)(2,1)S(1)} %shard_map.163), channel_id=1, source_target_pairs={{0,4},{1,5},{2,6},{3,7},{4,0},{5,1},{6,2},{7,3},{8,12},{9,13},{10,... | collective-permute-start | bytes 2555912 | tf_op jit(solution)/shard_map/ppermute | solution.py:20
  34.2 0.1 shard_map.162
  34.2 1.6 %collective-permute-start.9 = (bf16[416,1024]{1,0:T(8,128)(2,1)S(1)}, bf16[416,1024]{1,0:T(8,128)(2,1)S(1)}, u32[]{:S(2)}, u32[]{:S(2)}) collective-permute-start(bf16[416,1024]{1,0:T(8,128)(2,1)S(1)} %shard_map.162), channel_id=1, source_target_pairs={{0,2},{1,3},{2,0},{3,1},{4,6},{5,7},{6,4},{7,5},{8,10},{9,11},{10,... | collective-permute-start | bytes 2555912 | tf_op jit(solution)/shard_map/ppermute | solution.py:20
  35.8 0.5 collective-permute-start.12
  36.4 2.1 %collective-permute-start.13 = (bf16[192,1024]{1,0:T(8,128)(2,1)S(1)}, bf16[192,1024]{1,0:T(8,128)(2,1)S(1)}, u32[]{:S(2)}, u32[]{:S(2)}) collective-permute-start(bf16[192,1024]{1,0:T(8,128)(2,1)S(1)} %shard_map.166), channel_id=1, source_target_pairs={{0,24},{1,25},{2,26},{3,27},{4,28},{5,29},{6,30},{7,31},{8,16},{9,... | collective-permute-start | bytes 1179656 | tf_op jit(solution)/shard_map/ppermute | solution.py:20
  38.5 0.0 copy-start.10
  38.5 0.5 collective-permute-start.11
  39.1 18.1 %collective-permute-done.11.refs_3_.refs_9_ = bf16[128,1024]{1,0:T(8,128)(2,1)S(1)} collective-permute-done((bf16[128,1024]{1,0:T(8,128)(2,1)S(1)}, bf16[128,1024]{1,0:T(8,128)(2,1)S(1)}, u32[]{:S(2)}, u32[]{:S(2)}) %collective-permute-start.11) | collective-permute-done | bytes 262176 | tf_op jit(solution)/shard_map/ppermute | solution.py:20
  57.2 1.3 %collective-permute-done.13.refs_10_ = bf16[192,1024]{1,0:T(8,128)(2,1)S(1)} collective-permute-done((bf16[192,1024]{1,0:T(8,128)(2,1)S(1)}, bf16[192,1024]{1,0:T(8,128)(2,1)S(1)}, u32[]{:S(2)}, u32[]{:S(2)}) %collective-permute-start.13) | collective-permute-done | bytes 393248 | tf_op jit(solution)/shard_map/ppermute | solution.py:20
  58.4 0.2 shard_map.170.home
  58.6 0.1 collective-permute-start.15
  58.7 0.2 shard_map.167.refs_5_
  58.9 0.1 shard_map.168.mine
  59.0 0.0 copy-start.3
  59.0 0.5 collective-permute-start.14
  59.6 0.0 copy-start.7
  59.6 0.6 collective-permute-start.16
  60.2 1.2 %collective-permute-start.17 = (bf16[256,1024]{1,0:T(8,128)(2,1)S(1)}, bf16[256,1024]{1,0:T(8,128)(2,1)S(1)}, u32[]{:S(2)}, u32[]{:S(2)}) collective-permute-start(bf16[256,1024]{1,0:T(8,128)(2,1)S(1)} %shard_map.174), channel_id=1, source_target_pairs={{0,4},{1,5},{2,6},{3,7},{4,0},{5,1},{6,2},{7,3},{8,12},{9,13},{10,... | collective-permute-start | bytes 1572872 | tf_op jit(solution)/shard_map/ppermute | solution.py:20
  61.5 2.6 %collective-permute-start.18 = (bf16[128,1024]{1,0:T(8,128)(2,1)S(1)}, bf16[128,1024]{1,0:T(8,128)(2,1)S(1)}, u32[]{:S(2)}, u32[]{:S(2)}) collective-permute-start(bf16[128,1024]{1,0:T(8,128)(2,1)S(1)} %shard_map.175), channel_id=1, source_target_pairs={{0,24},{1,25},{2,26},{3,27},{4,28},{5,29},{6,30},{7,31},{8,16},{9,... | collective-permute-start | bytes 786440 | tf_op jit(solution)/shard_map/ppermute | solution.py:20
  64.1 0.1 collective-permute-done.14.theirs
  64.2 1.6 %shard_map.169.inputs = bf16[1536,1024]{1,0:T(8,128)(2,1)S(1)} custom-call(bf16[128,1024]{1,0:T(8,128)(2,1)S(1)} %copy-done.3, bf16[464,1024]{1,0:T(8,128)(2,1)S(1)} %shard_map.168.mine, bf16[464,1024]{1,0:T(8,128)(2,1)S(1)} %collective-permute-done.14.theirs), custom_call_target="tpu_custom_call" | custom-call | tf_op jit(solution)/shard_map/pallas_call | solution.py:48
  65.8 6.8 %shard_map.171.hidden = bf16[1536,2048]{1,0:T(8,128)(2,1)S(1)} custom-call(bf16[1536,1024]{1,0:T(8,128)(2,1)S(1)} %shard_map.169.inputs, bf16[1024,1024]{1,0:T(8,128)(2,1)S(1)} %shard_map.170.home, bf16[1024,1024]{1,0:T(8,128)(2,1)S(1)} %collective-permute-done.15.other, f32[1,2048]{1,0:T(1,128)S(1)} %bitcast.14), custom_call_target="tpu_custom_call" | custom-call | tf_op jit(solution)/shard_map/pallas_call | solution.py:48
  72.6 0.0 copy-start.5
  72.6 0.0 copy-start.8
  72.7 5.2 %shard_map.172.so_far = f32[1536,1024]{1,0:T(8,128)S(1)} custom-call(bf16[1536,2048]{1,0:T(8,128)(2,1)S(1)} %shard_map.171.hidden, bf16[192,1024]{1,0:T(8,128)(2,1)S(1)} %get-tuple-element.28.refs_0_, bf16[208,1024]{1,0:T(8,128)(2,1)S(1)} %collective-permute-done.4.refs_1_.refs_2_.refs_0_, ...), custom_call_target="tpu_custom_call" | custom-call | tf_op jit(solution)/shard_map/pallas_call | solution.py:48
  78.0 4.0 %shard_map.176 = (f32[8,768]{1,0:T(8,128)S(1)}, f32[8,768]{1,0:T(8,128)S(1)}) custom-call(bf16[1536,2048]{1,0:T(8,128)(2,1)S(1)} %shard_map.171.hidden, f32[1536,1024]{1,0:T(8,128)S(1)} %shard_map.172.so_far, f32[1,2048]{1,0:T(1,128)S(1)} %bitcast.15, bf16[8,2048]{1,0:T(8,128)(2,1)S(1)} %bitcast.12, bf16[256,1024]{1,0:T(8,128)(2,1)S(1)} %collective-permute-done.16.refs_0_, ...), custom_call_target="tpu_custom_call" | custom-call | tf_op jit(solution)/shard_map/pallas_call | solution.py:48
  82.0 0.2 collective-permute-start.19
  82.2 1.1 %collective-permute-done.19.theirs = f32[8,768]{1,0:T(8,128)S(1)} collective-permute-done((f32[8,768]{1,0:T(8,128)S(1)}, f32[8,768]{1,0:T(8,128)S(1)}, u32[]{:S(2)}, u32[]{:S(2)}) %collective-permute-start.19) | collective-permute-done | bytes 24608 | tf_op jit(solution)/shard_map/ppermute | solution.py:24
  83.3 0.8 shard_map.177
  (44 shorter events, 0.3 us)
Async XLA Ops:
  0.6 4.4 %collective-permute-start.1 = (bf16[64,2048]{1,0:T(8,128)(2,1)}, bf16[64,2048]{1,0:T(8,128)(2,1)S(1)}, u32[]{:S(2)}, u32[]{:S(2)}) collective-permute-start(bf16[64,2048]{1,0:T(8,128)(2,1)} %w_second.1), channel_id=1, source_target_pairs={{0,1},{1,0},{2,3},{3,2},{4,5},{5,4},{6,7},{7,6},{8,9},{9,8},{10,11... | collective-permute-start | bytes 786440 | tf_op jit(solution)/shard_map/ppermute | solution.py:24
  1.1 3.8 %collective-permute-start = (bf16[32,2048]{1,0:T(8,128)(2,1)}, bf16[32,2048]{1,0:T(8,128)(2,1)S(1)}, u32[]{:S(2)}, u32[]{:S(2)}) collective-permute-start(bf16[32,2048]{1,0:T(8,128)(2,1)} %w_first.1), channel_id=1, source_target_pairs={{0,1},{1,0},{2,3},{3,2},{4,5},{5,4},{6,7},{7,6},{8,9},{9,8},{10,11... | collective-permute-start | bytes 393224 | tf_op jit(solution)/shard_map/ppermute | solution.py:24
  1.2 3.7 %collective-permute-start.2 = (s32[1,192]{1,0:T(1,128)}, s32[1,192]{1,0:T(1,128)S(1)}, u32[]{:S(2)}, u32[]{:S(2)}) collective-permute-start(s32[1,192]{1,0:T(1,128)} %bitcast.16), channel_id=1, source_target_pairs={{0,1},{1,0},{2,3},{3,2},{4,5},{5,4},{6,7},{7,6},{8,9},{9,8},{10,11... | collective-permute-start | bytes 2312 | tf_op jit(solution)/shard_map/ppermute | solution.py:24
  1.7 3.3 %collective-permute-start.3 = (s32[1,192]{1,0:T(1,128)}, s32[1,192]{1,0:T(1,128)S(1)}, u32[]{:S(2)}, u32[]{:S(2)}) collective-permute-start(s32[1,192]{1,0:T(1,128)} %bitcast.20), channel_id=1, source_target_pairs={{0,1},{1,0},{2,3},{3,2},{4,5},{5,4},{6,7},{7,6},{8,9},{9,8},{10,11... | collective-permute-start | bytes 2312 | tf_op jit(solution)/shard_map/ppermute | solution.py:24
  1.7 0.9 %copy-start.2 = (bf16[64,2048]{1,0:T(8,128)(2,1)S(1)}, bf16[64,2048]{1,0:T(8,128)(2,1)}, u32[]{:S(2)}) copy-start(bf16[64,2048]{1,0:T(8,128)(2,1)} %w_second.1) | copy-start | bytes 786436
  2.7 0.9 %copy-start.4 = (bf16[32,2048]{1,0:T(8,128)(2,1)S(1)}, bf16[32,2048]{1,0:T(8,128)(2,1)}, u32[]{:S(2)}) copy-start(bf16[32,2048]{1,0:T(8,128)(2,1)} %w_first.1) | copy-start | bytes 393220
  3.6 0.7 copy-start.9
  4.3 0.7 copy-start.12
  5.1 25.9 %collective-permute-start.4 = (bf16[208,1024]{1,0:T(8,128)(2,1)S(1)}, bf16[208,1024]{1,0:T(8,128)(2,1)S(1)}, u32[]{:S(2)}, u32[]{:S(2)}) collective-permute-start(bf16[208,1024]{1,0:T(8,128)(2,1)S(1)} %get-tuple-element.27.refs_0_), channel_id=1, source_target_pairs={{0,2},{1,3},{2,0},{3,1},{4,6},{5,7},{6,4},{7,5},{8,10},{9,11},{10,... | collective-permute-start | bytes 1277960 | tf_op jit(solution)/shard_map/ppermute | solution.py:20
  8.1 22.9 %collective-permute-start.5 = (bf16[208,1024]{1,0:T(8,128)(2,1)S(1)}, bf16[208,1024]{1,0:T(8,128)(2,1)S(1)}, u32[]{:S(2)}, u32[]{:S(2)}) collective-permute-start(bf16[208,1024]{1,0:T(8,128)(2,1)S(1)} %get-tuple-element.27.refs_0_), channel_id=1, source_target_pairs={{0,4},{1,5},{2,6},{3,7},{4,0},{5,1},{6,2},{7,3},{8,12},{9,13},{10,... | collective-permute-start | bytes 1277960 | tf_op jit(solution)/shard_map/ppermute | solution.py:20
  9.6 21.4 %collective-permute-start.6 = (bf16[208,1024]{1,0:T(8,128)(2,1)S(1)}, bf16[208,1024]{1,0:T(8,128)(2,1)S(1)}, u32[]{:S(2)}, u32[]{:S(2)}) collective-permute-start(bf16[208,1024]{1,0:T(8,128)(2,1)S(1)} %get-tuple-element.27.refs_0_), channel_id=1, source_target_pairs={{0,6},{1,7},{2,4},{3,5},{4,2},{5,3},{6,0},{7,1},{8,14},{9,15},{10,... | collective-permute-start | bytes 1277960 | tf_op jit(solution)/shard_map/ppermute | solution.py:20
  9.6 18.9 %collective-permute-start.7 = (bf16[192,1024]{1,0:T(8,128)(2,1)S(1)}, bf16[192,1024]{1,0:T(8,128)(2,1)S(1)}, u32[]{:S(2)}, u32[]{:S(2)}) collective-permute-start(bf16[192,1024]{1,0:T(8,128)(2,1)S(1)} %get-tuple-element.28.refs_0_), channel_id=1, source_target_pairs={{0,8},{1,9},{2,10},{3,11},{4,12},{5,13},{6,14},{7,15},{8,0},{9,1},... | collective-permute-start | bytes 1179656 | tf_op jit(solution)/shard_map/ppermute | solution.py:20
  11.6 19.3 %collective-permute-start.8 = (bf16[192,1024]{1,0:T(8,128)(2,1)S(1)}, bf16[192,1024]{1,0:T(8,128)(2,1)S(1)}, u32[]{:S(2)}, u32[]{:S(2)}) collective-permute-start(bf16[192,1024]{1,0:T(8,128)(2,1)S(1)} %get-tuple-element.28.refs_0_), channel_id=1, source_target_pairs={{0,16},{1,17},{2,18},{3,19},{4,20},{5,21},{6,22},{7,23},{8,24},{9,... | collective-permute-start | bytes 1179656 | tf_op jit(solution)/shard_map/ppermute | solution.py:20
  14.2 1.0 %copy-start = (bf16[256,1024]{1,0:T(8,128)(2,1)S(1)}, bf16[256,1024]{1,0:T(8,128)(2,1)}, u32[]{:S(2)}) copy-start(bf16[256,1024]{1,0:T(8,128)(2,1)} %refs_0_.1) | copy-start | bytes 1572868
  32.6 25.9 %collective-permute-start.10 = (bf16[416,1024]{1,0:T(8,128)(2,1)S(1)}, bf16[416,1024]{1,0:T(8,128)(2,1)S(1)}, u32[]{:S(2)}, u32[]{:S(2)}) collective-permute-start(bf16[416,1024]{1,0:T(8,128)(2,1)S(1)} %shard_map.163), channel_id=1, source_target_pairs={{0,4},{1,5},{2,6},{3,7},{4,0},{5,1},{6,2},{7,3},{8,12},{9,13},{10,... | collective-permute-start | bytes 2555912 | tf_op jit(solution)/shard_map/ppermute | solution.py:20
  34.2 24.2 %collective-permute-start.9 = (bf16[416,1024]{1,0:T(8,128)(2,1)S(1)}, bf16[416,1024]{1,0:T(8,128)(2,1)S(1)}, u32[]{:S(2)}, u32[]{:S(2)}) collective-permute-start(bf16[416,1024]{1,0:T(8,128)(2,1)S(1)} %shard_map.162), channel_id=1, source_target_pairs={{0,2},{1,3},{2,0},{3,1},{4,6},{5,7},{6,4},{7,5},{8,10},{9,11},{10,... | collective-permute-start | bytes 2555912 | tf_op jit(solution)/shard_map/ppermute | solution.py:20
  35.8 22.6 %collective-permute-start.12 = (bf16[320,1024]{1,0:T(8,128)(2,1)S(1)}, bf16[320,1024]{1,0:T(8,128)(2,1)S(1)}, u32[]{:S(2)}, u32[]{:S(2)}) collective-permute-start(bf16[320,1024]{1,0:T(8,128)(2,1)S(1)} %shard_map.165), channel_id=1, source_target_pairs={{0,8},{1,9},{2,10},{3,11},{4,12},{5,13},{6,14},{7,15},{8,0},{9,1},... | collective-permute-start | bytes 1966088 | tf_op jit(solution)/shard_map/ppermute | solution.py:20
  36.4 22.1 %collective-permute-start.13 = (bf16[192,1024]{1,0:T(8,128)(2,1)S(1)}, bf16[192,1024]{1,0:T(8,128)(2,1)S(1)}, u32[]{:S(2)}, u32[]{:S(2)}) collective-permute-start(bf16[192,1024]{1,0:T(8,128)(2,1)S(1)} %shard_map.166), channel_id=1, source_target_pairs={{0,24},{1,25},{2,26},{3,27},{4,28},{5,29},{6,30},{7,31},{8,16},{9,... | collective-permute-start | bytes 1179656 | tf_op jit(solution)/shard_map/ppermute | solution.py:20
  38.5 20.2 %copy-start.10 = (s32[192,1]{0,1:T(1,128)S(1)}, s32[192,1]{0,1:T(1,128)}, u32[]{:S(2)}) copy-start(s32[192,1]{0,1:T(1,128)} %param.26) | copy-start | bytes 2308
  38.5 20.2 %copy-start.11 = (s32[192,4]{0,1:T(4,128)S(1)}, s32[192,4]{0,1:T(4,128)}, u32[]{:S(2)}) copy-start(s32[192,4]{0,1:T(4,128)} %param.25) | copy-start | bytes 9220
  38.5 20.4 %copy-start.1 = (bf16[192,1024]{1,0:T(8,128)(2,1)S(1)}, bf16[192,1024]{1,0:T(8,128)(2,1)}, u32[]{:S(2)}) copy-start(bf16[192,1024]{1,0:T(8,128)(2,1)} %refs_4_.1) | copy-start | bytes 1179652
  38.5 18.6 %collective-permute-start.11 = (bf16[128,1024]{1,0:T(8,128)(2,1)S(1)}, bf16[128,1024]{1,0:T(8,128)(2,1)S(1)}, u32[]{:S(2)}, u32[]{:S(2)}) collective-permute-start(bf16[128,1024]{1,0:T(8,128)(2,1)S(1)} %shard_map.164), channel_id=1, source_target_pairs={{0,6},{1,7},{2,4},{3,5},{4,2},{5,3},{6,0},{7,1},{8,14},{9,15},{10,... | collective-permute-start | bytes 786440 | tf_op jit(solution)/shard_map/ppermute | solution.py:20
  58.6 7.2 %collective-permute-start.15 = (bf16[1024,1024]{1,0:T(8,128)(2,1)S(1)}, bf16[1024,1024]{1,0:T(8,128)(2,1)S(1)}, u32[]{:S(2)}, u32[]{:S(2)}) collective-permute-start(bf16[1024,1024]{1,0:T(8,128)(2,1)S(1)} %shard_map.170.home), channel_id=1, source_target_pairs={{0,1},{1,0},{2,3},{3,2},{4,5},{5,4},{6,7},{7,6},{8,9},{9,8},{10,11... | collective-permute-start | bytes 6291464 | tf_op jit(solution)/shard_map/ppermute | solution.py:24
  59.0 5.2 %copy-start.3 = (bf16[128,1024]{1,0:T(8,128)(2,1)S(1)}, bf16[128,1024]{1,0:T(8,128)(2,1)}, u32[]{:S(2)}) copy-start(bf16[128,1024]{1,0:T(8,128)(2,1)} %act_table.1) | copy-start | bytes 786436
  59.0 5.2 %collective-permute-start.14 = (bf16[464,1024]{1,0:T(8,128)(2,1)S(1)}, bf16[464,1024]{1,0:T(8,128)(2,1)S(1)}, u32[]{:S(2)}, u32[]{:S(2)}) collective-permute-start(bf16[464,1024]{1,0:T(8,128)(2,1)S(1)} %shard_map.168.mine), channel_id=1, source_target_pairs={{0,1},{1,0},{2,3},{3,2},{4,5},{5,4},{6,7},{7,6},{8,9},{9,8},{10,11... | collective-permute-start | bytes 2850824 | tf_op jit(solution)/shard_map/ppermute | solution.py:24
  59.6 6.2 %copy-start.7 = (f32[2048]{0:T(1024)S(1)}, f32[2048]{0:T(1024)}, u32[]{:S(2)}) copy-start(f32[2048]{0:T(1024)} %param.19) | copy-start | bytes 24580
  59.6 18.3 %collective-permute-start.16 = (bf16[256,1024]{1,0:T(8,128)(2,1)S(1)}, bf16[256,1024]{1,0:T(8,128)(2,1)S(1)}, u32[]{:S(2)}, u32[]{:S(2)}) collective-permute-start(bf16[256,1024]{1,0:T(8,128)(2,1)S(1)} %shard_map.173), channel_id=1, source_target_pairs={{0,2},{1,3},{2,0},{3,1},{4,6},{5,7},{6,4},{7,5},{8,10},{9,11},{10,... | collective-permute-start | bytes 1572872 | tf_op jit(solution)/shard_map/ppermute | solution.py:20
  60.2 17.7 %collective-permute-start.17 = (bf16[256,1024]{1,0:T(8,128)(2,1)S(1)}, bf16[256,1024]{1,0:T(8,128)(2,1)S(1)}, u32[]{:S(2)}, u32[]{:S(2)}) collective-permute-start(bf16[256,1024]{1,0:T(8,128)(2,1)S(1)} %shard_map.174), channel_id=1, source_target_pairs={{0,4},{1,5},{2,6},{3,7},{4,0},{5,1},{6,2},{7,3},{8,12},{9,13},{10,... | collective-permute-start | bytes 1572872 | tf_op jit(solution)/shard_map/ppermute | solution.py:20
  61.5 16.4 %collective-permute-start.18 = (bf16[128,1024]{1,0:T(8,128)(2,1)S(1)}, bf16[128,1024]{1,0:T(8,128)(2,1)S(1)}, u32[]{:S(2)}, u32[]{:S(2)}) collective-permute-start(bf16[128,1024]{1,0:T(8,128)(2,1)S(1)} %shard_map.175), channel_id=1, source_target_pairs={{0,24},{1,25},{2,26},{3,27},{4,28},{5,29},{6,30},{7,31},{8,16},{9,... | collective-permute-start | bytes 786440 | tf_op jit(solution)/shard_map/ppermute | solution.py:20
  72.6 5.3 %copy-start.5 = (bf16[2048,8]{0,1:T(8,128)(2,1)S(1)}, bf16[2048,8]{0,1:T(8,128)(2,1)}, u32[]{:S(2)}) copy-start(bf16[2048,8]{0,1:T(8,128)(2,1)} %param.22) | copy-start | bytes 98308
  72.6 5.3 %copy-start.8 = (f32[2048]{0:T(1024)S(1)}, f32[2048]{0:T(1024)}, u32[]{:S(2)}) copy-start(f32[2048]{0:T(1024)} %param.21) | copy-start | bytes 24580
  77.9 5.3 %copy-start.6 = (s32[192,32]{0,1:T(8,128)S(1)}, s32[192,32]{0,1:T(8,128)}, u32[]{:S(2)}) copy-start(s32[192,32]{0,1:T(8,128)} %param.28) | copy-start | bytes 73732
  77.9 5.3 %copy-start.13 = (s32[192]{0:T(256)S(1)}, s32[192]{0:T(256)}, u32[]{:S(2)}) copy-start(s32[192]{0:T(256)} %param.24) | copy-start | bytes 2308
  78.0 5.3 %copy-start.14 = (s32[192]{0:T(256)S(1)}, s32[192]{0:T(256)}, u32[]{:S(2)}) copy-start(s32[192]{0:T(256)} %param.29) | copy-start | bytes 2308
  78.0 5.3 %copy-start.15 = (f32[8]{0:T(128)S(1)}, f32[8]{0:T(128)}, u32[]{:S(2)}) copy-start(f32[8]{0:T(128)} %param.23) | copy-start | bytes 100
  82.0 1.2 %collective-permute-start.19 = (f32[8,768]{1,0:T(8,128)S(1)}, f32[8,768]{1,0:T(8,128)S(1)}, u32[]{:S(2)}, u32[]{:S(2)}) collective-permute-start(f32[8,768]{1,0:T(8,128)S(1)} %get-tuple-element.45), channel_id=1, source_target_pairs={{0,1},{1,0},{2,3},{3,2},{4,5},{5,4},{6,7},{7,6},{8,9},{9,8},{10,11... | collective-permute-start | bytes 73736 | tf_op jit(solution)/shard_map/ppermute | solution.py:24

commit v4 on v3

--- a/solution.py
+++ b/solution.py
@@ -67,13 +67,11 @@
     )
 
 
-def keep_kernel(w_first, w_second, owner, row, keep, ids):
+def keep_kernel(w_first, w_second, keep):
     one, half = w_first.shape[0], keep.shape[1]
     here = pl.ds(pl.multiple_of(my_core() * half, half), half)
     keep[:one, :] = w_first[:, here]
     keep[one:, :] = w_second[:, here]
-    ids[:1, :] = owner[...]
-    ids[1:, :] = row[...]
 
 
 def join_kernel(depths, keep, ids, other_first, other_second, other_owner, other_row, out, out_ids):
@@ -125,14 +123,15 @@
     hits = (owners.astype(jnp.int32) == me).astype(jnp.float32)
     ranks = ranks_of(hits).astype(jnp.int32)
     rows = (rows * hits).astype(jnp.bfloat16)
+    wants = []
+    for j in range(2 * len(PLANE)):
+        at_rank = (ranks[j : j + 1, :] == iota((capacity, count), 0)).astype(jnp.bfloat16)
+        wants.append(across(rows, at_rank)[j : j + 1, :])
+    want = jnp.concatenate(wants, axis=1).astype(jnp.int32)
+    onehot = (iota((buckets, want.shape[1]), 0) == want).astype(jnp.bfloat16)
+    found = over_rows(onehot, table[...]).astype(jnp.bfloat16)
     for n, out in enumerate(outs):
-        wants = []
-        for j in (2 * n, 2 * n + 1):
-            at_rank = (ranks[j : j + 1, :] == iota((capacity, count), 0)).astype(jnp.bfloat16)
-            wants.append(across(rows, at_rank)[j : j + 1, :])
-        want = jnp.concatenate(wants, axis=1).astype(jnp.int32)
-        onehot = (iota((buckets, want.shape[1]), 0) == want).astype(jnp.bfloat16)
-        out[...] = over_rows(onehot, table[...]).astype(jnp.bfloat16)
+        out[...] = found[2 * n * capacity : 2 * (n + 1) * capacity, :]
 
 
 def inputs_kernel(capacity, branch_slots, act_table, mine, theirs, out):
@@ -150,9 +149,11 @@
         onehot = (meta[branch_slots : branch_slots + 1, :] == iota((served, rows), 0)).astype(jnp.bfloat16)
         bucket = over_rows(onehot, buckets)
         parent = ref[served : served + rows, :].astype(jnp.float32)
+        acts = jnp.concatenate([meta[c : c + 1, :] for c in range(branch_slots)], axis=1)
+        onehot = (acts == iota((act_table.shape[0], branch_slots * rows), 0)).astype(jnp.bfloat16)
+        change = over_rows(onehot, act_table[...])
         for c in range(branch_slots):
-            onehot = (meta[c : c + 1, :] == iota((act_table.shape[0], rows), 0)).astype(jnp.bfloat16)
-            base = (parent + over_rows(onehot, act_table[...])).astype(jnp.bfloat16)
+            base = (parent + change[c * rows : (c + 1) * rows, :]).astype(jnp.bfloat16)
             out[to : to + rows, :] = (base.astype(jnp.float32) + bucket).astype(jnp.bfloat16)
             to += rows
 
@@ -287,9 +288,8 @@
     wide = 2 * capacity
 
     owner, row = bucket_owner.T, bucket_row[None, :]
-    keep, ids = call(keep_kernel, (shape(depth // 2, half), shape(2, par_count, jnp.int32)), 4)(
-        w_first, w_second, owner, row
-    )
+    keep = call(keep_kernel, shape(depth // 2, half), 4)(w_first, w_second)
+    ids = jnp.concatenate([owner, row], axis=0)
     own, own_ids = call(
         functools.partial(join_kernel, (depth_one, depth_two)), (shape(depth, half), shape(depth + ID_ROWS, half)), 4
     )(keep, ids, swap_core(w_first), swap_core(w_second), swap_core(owner), swap_core(row))
@@ -309,7 +309,7 @@
     y_ab = swap_chip(stack((from_a, few, depth - few), (from_b, 0, depth), (served[2], 0, wide)), Y)
     rows_d = swap_chip(stack((served[3], 0, wide), (from_b, 0, chip_one)), D)
     c_da = swap_chip(stack((from_b, 0, depth), (from_d, 0, chip_one), (from_x, 0, few), (from_y, 0, few)), A)
-    plane_c = swap_chip(stack(*((rows, 0, chip_one) for rows in (from_x, from_y, from_d))), C)
+    plane_c = swap_chip(stack((from_x, 0, chip_one), (from_y, 0, chip_one), (from_d, 0, chip_one)), C)
     x_ab, y_ab, rows_d, c_da, plane_c = lax.optimization_barrier((x_ab, y_ab, rows_d, c_da, plane_c))
 
     cut = chip_two // 2
@@ -342,7 +342,7 @@
         inputs, weights, swap_core(weights), b_first[None, :]
     )
 
-    early = [(chip, n, chip_one, 0, chip_two) for chip, n in near] + [(C, 8, chip_one, 0, chip_two)]
+    early = [(chip, n, chip_one, 0, chip_two) for chip, n in near]
     for n, chip in ((6, X), (7, Y)):
         early += [(chip ^ A, n, at_a, 0, chip_two), (chip ^ B, n, at_b, 0, chip_two)]
     early.sort()
@@ -352,15 +352,16 @@
         16,
         [pltpu.VMEM((len(early) * chip_two, half), jnp.bfloat16)],
     )(hidden, *arrays)
-    late = [(X ^ C, 0, 0, 0, chip_two), (Y ^ C, 1, 0, 0, chip_two), (D ^ C, 2, 0, 0, chip_two)]
+    late = [(C, 3, chip_one, 0, chip_two), (X ^ C, 0, 0, 0, chip_two), (Y ^ C, 1, 0, 0, chip_two)]
+    late += [(D ^ C, 2, 0, 0, chip_two)]
     late += [(D ^ A, 0, chip_two, 0, cut), (D ^ A, 1, chip_two, cut, cut)]
     late += [(D ^ B, 0, chip_two + cut, 0, cut), (D ^ B, 1, chip_two + cut, cut, cut)]
     mine, theirs = call(
         functools.partial(finish_second_kernel, late, chip_two),
         (shape(w_head.shape[1], branches, jnp.float32),) * 2,
         14,
-        [pltpu.VMEM((5 * chip_two, half), jnp.bfloat16)],
-    )(hidden, so_far, b_second[None, :], w_head.T, x_c, y_c, d_c)
+        [pltpu.VMEM((6 * chip_two, half), jnp.bfloat16)],
+    )(hidden, so_far, b_second[None, :], w_head.T, x_c, y_c, d_c, c_da)
     strategy, values = call(
         last_kernel, (shape(legal_mask.shape[1], par_count, jnp.float32), shape(1, par_count // 4, jnp.float32)), 4
     )(branch_counts[None, :], ancestor[None, :], legal_mask.T, b_head[None, :], mine, swap_core(theirs))

time: 84.4 us -> 81.9 us (0.970)
  Pallas kernels: 20.8 us -> 19 us
  local copies, waits for them, and re-layouts: 4.32 us -> 2.96 us
    pallas_call x20, Pallas kernels: 20.8 us -> 19 us  [run(): pl.pallas_call(kernel, out_shape=tuple(outs) if many else outs, in_specs=...]
    unnamed x32 -> x28, local copies, waits for them, and re-layouts: 4.32 us -> 2.96 us
  transfers between devices with their start and end apart: 20 -> 20, of which waited for: 6 -> 6; matrix products, arithmetic and copies ran while one was open for 0% -> 1% of each run, Pallas kernels for 17% -> 16%
where the time goes in v4:
time: 81.9 us; the launch traced here: 81.7 us
  waiting for transfers between devices  36.2 us (44%)
  starting transfers between devices  21.8 us (27%)
  Pallas kernels  19 us (23%)
  local copies, waits for them, and re-layouts  2.96 us (4%)
  between operations  0.97 us (1%)
    ppermute x13, waiting for transfers between devices, swap_chip(): lax.ppermute(value, AXES, [(i, i ^ chip << 1) for i in range(TRAV * BULK)])  35.1 us
    ppermute x13, starting transfers between devices, swap_chip(): lax.ppermute(value, AXES, [(i, i ^ chip << 1) for i in range(TRAV * BULK)])  19.9 us
    pallas_call x20, Pallas kernels, run(): pl.pallas_call(kernel, out_shape=tuple(outs) if many else outs, in_specs=...  19 us
    unnamed x28, local copies, waits for them, and re-layouts  2.96 us
    ppermute x7, starting transfers between devices, swap_core(): return lax.ppermute(value, AXES, [(i, i ^ 1) for i in range(TRAV * BULK)])  1.91 us
  transfers between devices with their start and end apart: 20, of which 6 were waited for; matrix products, arithmetic and copies ran while one was open for 1% of the time, Pallas kernels for 16%

profile of v4, /device:TPU:0, one launch (start us, length us, event | category | flops | bytes accessed | tf_op | source)
XLA Modules:
  0.0 81.7 jit_solution(2012775994162339873)
XLA Ops:
  0.6 0.5 collective-permute-start.1
  1.1 0.1 collective-permute-start
  1.2 0.4 collective-permute-start.2
  1.7 0.1 collective-permute-start.3
  1.7 0.7 pad_add_fusion.ids
  2.4 0.9 %copy-done.2 = bf16[64,2048]{1,0:T(8,128)(2,1)S(1)} copy-done((bf16[64,2048]{1,0:T(8,128)(2,1)S(1)}, bf16[64,2048]{1,0:T(8,128)(2,1)}, u32[]{:S(2)}) %copy-start.2) | copy-done | bytes 262168
  3.4 0.9 %copy-done.4 = bf16[32,2048]{1,0:T(8,128)(2,1)S(1)} copy-done((bf16[32,2048]{1,0:T(8,128)(2,1)S(1)}, bf16[32,2048]{1,0:T(8,128)(2,1)}, u32[]{:S(2)}) %copy-start.4) | copy-done | bytes 131096
  4.4 0.1 shard_map.159
  4.4 3.0 %collective-permute-start.4 = (bf16[208,1024]{1,0:T(8,128)(2,1)S(1)}, bf16[208,1024]{1,0:T(8,128)(2,1)S(1)}, u32[]{:S(2)}, u32[]{:S(2)}) collective-permute-start(bf16[208,1024]{1,0:T(8,128)(2,1)S(1)} %get-tuple-element.23.refs_0_), channel_id=1, source_target_pairs={{0,2},{1,3},{2,0},{3,1},{4,6},{5,7},{6,4},{7,5},{8,10},{9,11},{10,... | collective-permute-start | bytes 1277960 | tf_op jit(solution)/shard_map/ppermute | solution.py:20
  7.4 1.5 %collective-permute-start.5 = (bf16[208,1024]{1,0:T(8,128)(2,1)S(1)}, bf16[208,1024]{1,0:T(8,128)(2,1)S(1)}, u32[]{:S(2)}, u32[]{:S(2)}) collective-permute-start(bf16[208,1024]{1,0:T(8,128)(2,1)S(1)} %get-tuple-element.23.refs_0_), channel_id=1, source_target_pairs={{0,4},{1,5},{2,6},{3,7},{4,0},{5,1},{6,2},{7,3},{8,12},{9,13},{10,... | collective-permute-start | bytes 1277960 | tf_op jit(solution)/shard_map/ppermute | solution.py:20
  8.9 0.0 collective-permute-start.6
  9.0 2.0 %collective-permute-start.7 = (bf16[192,1024]{1,0:T(8,128)(2,1)S(1)}, bf16[192,1024]{1,0:T(8,128)(2,1)S(1)}, u32[]{:S(2)}, u32[]{:S(2)}) collective-permute-start(bf16[192,1024]{1,0:T(8,128)(2,1)S(1)} %get-tuple-element.24.refs_0_), channel_id=1, source_target_pairs={{0,8},{1,9},{2,10},{3,11},{4,12},{5,13},{6,14},{7,15},{8,0},{9,1},... | collective-permute-start | bytes 1179656 | tf_op jit(solution)/shard_map/ppermute | solution.py:20
  11.0 2.6 %collective-permute-start.8 = (bf16[192,1024]{1,0:T(8,128)(2,1)S(1)}, bf16[192,1024]{1,0:T(8,128)(2,1)S(1)}, u32[]{:S(2)}, u32[]{:S(2)}) collective-permute-start(bf16[192,1024]{1,0:T(8,128)(2,1)S(1)} %get-tuple-element.24.refs_0_), channel_id=1, source_target_pairs={{0,16},{1,17},{2,18},{3,19},{4,20},{5,21},{6,22},{7,23},{8,24},{9,... | collective-permute-start | bytes 1179656 | tf_op jit(solution)/shard_map/ppermute | solution.py:20
  13.6 1.0 %copy-done = bf16[256,1024]{1,0:T(8,128)(2,1)S(1)} copy-done((bf16[256,1024]{1,0:T(8,128)(2,1)S(1)}, bf16[256,1024]{1,0:T(8,128)(2,1)}, u32[]{:S(2)}) %copy-start) | copy-done | bytes 524312
  14.7 13.2 %collective-permute-done.7.refs_0_.refs_3_ = bf16[192,1024]{1,0:T(8,128)(2,1)S(1)} collective-permute-done((bf16[192,1024]{1,0:T(8,128)(2,1)S(1)}, bf16[192,1024]{1,0:T(8,128)(2,1)S(1)}, u32[]{:S(2)}, u32[]{:S(2)}) %collective-permute-start.7) | collective-permute-done | bytes 393248 | tf_op jit(solution)/shard_map/ppermute | solution.py:20
  27.8 2.5 %collective-permute-done.8.refs_1_.refs_0_.refs_4_ = bf16[192,1024]{1,0:T(8,128)(2,1)S(1)} collective-permute-done((bf16[192,1024]{1,0:T(8,128)(2,1)S(1)}, bf16[192,1024]{1,0:T(8,128)(2,1)S(1)}, u32[]{:S(2)}, u32[]{:S(2)}) %collective-permute-start.8) | collective-permute-done | bytes 393248 | tf_op jit(solution)/shard_map/ppermute | solution.py:20
  30.3 0.7 shard_map.161
  31.0 0.1 shard_map.163
  31.1 1.6 %collective-permute-start.10 = (bf16[416,1024]{1,0:T(8,128)(2,1)S(1)}, bf16[416,1024]{1,0:T(8,128)(2,1)S(1)}, u32[]{:S(2)}, u32[]{:S(2)}) collective-permute-start(bf16[416,1024]{1,0:T(8,128)(2,1)S(1)} %shard_map.163), channel_id=1, source_target_pairs={{0,4},{1,5},{2,6},{3,7},{4,0},{5,1},{6,2},{7,3},{8,12},{9,13},{10,... | collective-permute-start | bytes 2555912 | tf_op jit(solution)/shard_map/ppermute | solution.py:20
  32.7 0.1 shard_map.162
  32.8 1.6 %collective-permute-start.9 = (bf16[416,1024]{1,0:T(8,128)(2,1)S(1)}, bf16[416,1024]{1,0:T(8,128)(2,1)S(1)}, u32[]{:S(2)}, u32[]{:S(2)}) collective-permute-start(bf16[416,1024]{1,0:T(8,128)(2,1)S(1)} %shard_map.162), channel_id=1, source_target_pairs={{0,2},{1,3},{2,0},{3,1},{4,6},{5,7},{6,4},{7,5},{8,10},{9,11},{10,... | collective-permute-start | bytes 2555912 | tf_op jit(solution)/shard_map/ppermute | solution.py:20
  34.4 0.5 collective-permute-start.12
  34.9 2.1 %collective-permute-start.13 = (bf16[192,1024]{1,0:T(8,128)(2,1)S(1)}, bf16[192,1024]{1,0:T(8,128)(2,1)S(1)}, u32[]{:S(2)}, u32[]{:S(2)}) collective-permute-start(bf16[192,1024]{1,0:T(8,128)(2,1)S(1)} %shard_map.166), channel_id=1, source_target_pairs={{0,24},{1,25},{2,26},{3,27},{4,28},{5,29},{6,30},{7,31},{8,16},{9,... | collective-permute-start | bytes 1179656 | tf_op jit(solution)/shard_map/ppermute | solution.py:20
  37.0 0.0 copy-start.9
  37.0 0.0 copy-start.10
  37.1 0.5 collective-permute-start.11
  37.6 18.1 %collective-permute-done.11.refs_3_.refs_9_ = bf16[128,1024]{1,0:T(8,128)(2,1)S(1)} collective-permute-done((bf16[128,1024]{1,0:T(8,128)(2,1)S(1)}, bf16[128,1024]{1,0:T(8,128)(2,1)S(1)}, u32[]{:S(2)}, u32[]{:S(2)}) %collective-permute-start.11) | collective-permute-done | bytes 262176 | tf_op jit(solution)/shard_map/ppermute | solution.py:20
  55.7 1.3 %collective-permute-done.13.refs_10_ = bf16[192,1024]{1,0:T(8,128)(2,1)S(1)} collective-permute-done((bf16[192,1024]{1,0:T(8,128)(2,1)S(1)}, bf16[192,1024]{1,0:T(8,128)(2,1)S(1)}, u32[]{:S(2)}, u32[]{:S(2)}) %collective-permute-start.13) | collective-permute-done | bytes 393248 | tf_op jit(solution)/shard_map/ppermute | solution.py:20
  57.0 0.2 shard_map.170.home
  57.2 0.1 collective-permute-start.15
  57.3 0.2 shard_map.167.refs_5_
  57.4 0.1 shard_map.168.mine
  57.5 0.5 collective-permute-start.14
  58.2 0.6 collective-permute-start.16
  58.8 1.2 %collective-permute-start.17 = (bf16[256,1024]{1,0:T(8,128)(2,1)S(1)}, bf16[256,1024]{1,0:T(8,128)(2,1)S(1)}, u32[]{:S(2)}, u32[]{:S(2)}) collective-permute-start(bf16[256,1024]{1,0:T(8,128)(2,1)S(1)} %shard_map.174), channel_id=1, source_target_pairs={{0,4},{1,5},{2,6},{3,7},{4,0},{5,1},{6,2},{7,3},{8,12},{9,13},{10,... | collective-permute-start | bytes 1572872 | tf_op jit(solution)/shard_map/ppermute | solution.py:20
  60.0 2.6 %collective-permute-start.18 = (bf16[128,1024]{1,0:T(8,128)(2,1)S(1)}, bf16[128,1024]{1,0:T(8,128)(2,1)S(1)}, u32[]{:S(2)}, u32[]{:S(2)}) collective-permute-start(bf16[128,1024]{1,0:T(8,128)(2,1)S(1)} %shard_map.175), channel_id=1, source_target_pairs={{0,24},{1,25},{2,26},{3,27},{4,28},{5,29},{6,30},{7,31},{8,16},{9,... | collective-permute-start | bytes 786440 | tf_op jit(solution)/shard_map/ppermute | solution.py:20
  62.6 0.1 collective-permute-done.14.theirs
  62.7 1.4 %shard_map.169.inputs = bf16[1536,1024]{1,0:T(8,128)(2,1)S(1)} custom-call(bf16[128,1024]{1,0:T(8,128)(2,1)S(1)} %copy-done.3, bf16[464,1024]{1,0:T(8,128)(2,1)S(1)} %shard_map.168.mine, bf16[464,1024]{1,0:T(8,128)(2,1)S(1)} %collective-permute-done.14.theirs), custom_call_target="tpu_custom_call" | custom-call | tf_op jit(solution)/shard_map/pallas_call | solution.py:48
  64.2 6.8 %shard_map.171.hidden = bf16[1536,2048]{1,0:T(8,128)(2,1)S(1)} custom-call(bf16[1536,1024]{1,0:T(8,128)(2,1)S(1)} %shard_map.169.inputs, bf16[1024,1024]{1,0:T(8,128)(2,1)S(1)} %shard_map.170.home, bf16[1024,1024]{1,0:T(8,128)(2,1)S(1)} %collective-permute-done.15.other, f32[1,2048]{1,0:T(1,128)S(1)} %bitcast.14), custom_call_target="tpu_custom_call" | custom-call | tf_op jit(solution)/shard_map/pallas_call | solution.py:48
  71.0 0.0 copy-start.5
  71.0 0.0 copy-start.8
  71.0 4.4 %shard_map.172.so_far = f32[1536,1024]{1,0:T(8,128)S(1)} custom-call(bf16[1536,2048]{1,0:T(8,128)(2,1)S(1)} %shard_map.171.hidden, bf16[192,1024]{1,0:T(8,128)(2,1)S(1)} %get-tuple-element.24.refs_0_, bf16[208,1024]{1,0:T(8,128)(2,1)S(1)} %collective-permute-done.4.refs_1_.refs_2_.refs_0_, ...), custom_call_target="tpu_custom_call" | custom-call | tf_op jit(solution)/shard_map/pallas_call | solution.py:48
  75.5 0.0 copy-start.6
  75.5 0.0 copy-start.13
  75.5 4.0 %shard_map.176 = (f32[8,768]{1,0:T(8,128)S(1)}, f32[8,768]{1,0:T(8,128)S(1)}) custom-call(bf16[1536,2048]{1,0:T(8,128)(2,1)S(1)} %shard_map.171.hidden, f32[1536,1024]{1,0:T(8,128)S(1)} %shard_map.172.so_far, f32[1,2048]{1,0:T(1,128)S(1)} %bitcast.15, bf16[8,2048]{1,0:T(8,128)(2,1)S(1)} %bitcast.12, bf16[256,1024]{1,0:T(8,128)(2,1)S(1)} %collective-permute-done.16.refs_0_, ...), custom_call_target="tpu_custom_call" | custom-call | tf_op jit(solution)/shard_map/pallas_call | solution.py:48
  79.6 0.2 collective-permute-start.19
  79.7 1.0 %collective-permute-done.19.theirs = f32[8,768]{1,0:T(8,128)S(1)} collective-permute-done((f32[8,768]{1,0:T(8,128)S(1)}, f32[8,768]{1,0:T(8,128)S(1)}, u32[]{:S(2)}, u32[]{:S(2)}) %collective-permute-start.19) | collective-permute-done | bytes 24608 | tf_op jit(solution)/shard_map/ppermute | solution.py:24
  80.8 0.8 %shard_map.177 = (f32[32,192]{1,0:T(8,128)}, f32[1,48]{1,0:T(1,128)}) custom-call(s32[1,192]{1,0:T(1,128)S(1)} %bitcast.20, s32[1,192]{1,0:T(1,128)S(1)} %bitcast.21, s32[32,192]{1,0:T(8,128)S(1)} %bitcast.13, f32[1,8]{1,0:T(1,128)S(1)} %bitcast.22, f32[8,768]{1,0:T(8,128)S(1)} %get-tuple-element.40.mine, f32[8,768]{1,0:T(8,128)S(1)} %collective-permute-done.19.theirs), custom_call_target="tpu_custom_call" | custom-call | tf_op jit(solution)/shard_map/pallas_call | solution.py:48
  (41 shorter events, 0.3 us)
Async XLA Ops:
  0.6 3.7 %collective-permute-start.1 = (bf16[64,2048]{1,0:T(8,128)(2,1)}, bf16[64,2048]{1,0:T(8,128)(2,1)S(1)}, u32[]{:S(2)}, u32[]{:S(2)}) collective-permute-start(bf16[64,2048]{1,0:T(8,128)(2,1)} %w_second.1), channel_id=1, source_target_pairs={{0,1},{1,0},{2,3},{3,2},{4,5},{5,4},{6,7},{7,6},{8,9},{9,8},{10,11... | collective-permute-start | bytes 786440 | tf_op jit(solution)/shard_map/ppermute | solution.py:24
  1.1 3.2 %collective-permute-start = (bf16[32,2048]{1,0:T(8,128)(2,1)}, bf16[32,2048]{1,0:T(8,128)(2,1)S(1)}, u32[]{:S(2)}, u32[]{:S(2)}) collective-permute-start(bf16[32,2048]{1,0:T(8,128)(2,1)} %w_first.1), channel_id=1, source_target_pairs={{0,1},{1,0},{2,3},{3,2},{4,5},{5,4},{6,7},{7,6},{8,9},{9,8},{10,11... | collective-permute-start | bytes 393224 | tf_op jit(solution)/shard_map/ppermute | solution.py:24
  1.2 3.1 %collective-permute-start.2 = (s32[1,192]{1,0:T(1,128)}, s32[1,192]{1,0:T(1,128)S(1)}, u32[]{:S(2)}, u32[]{:S(2)}) collective-permute-start(s32[1,192]{1,0:T(1,128)} %bitcast.17), channel_id=1, source_target_pairs={{0,1},{1,0},{2,3},{3,2},{4,5},{5,4},{6,7},{7,6},{8,9},{9,8},{10,11... | collective-permute-start | bytes 2312 | tf_op jit(solution)/shard_map/ppermute | solution.py:24
  1.7 2.7 %collective-permute-start.3 = (s32[1,192]{1,0:T(1,128)}, s32[1,192]{1,0:T(1,128)S(1)}, u32[]{:S(2)}, u32[]{:S(2)}) collective-permute-start(s32[1,192]{1,0:T(1,128)} %bitcast.23), channel_id=1, source_target_pairs={{0,1},{1,0},{2,3},{3,2},{4,5},{5,4},{6,7},{7,6},{8,9},{9,8},{10,11... | collective-permute-start | bytes 2312 | tf_op jit(solution)/shard_map/ppermute | solution.py:24
  2.4 0.9 %copy-start.2 = (bf16[64,2048]{1,0:T(8,128)(2,1)S(1)}, bf16[64,2048]{1,0:T(8,128)(2,1)}, u32[]{:S(2)}) copy-start(bf16[64,2048]{1,0:T(8,128)(2,1)} %w_second.1) | copy-start | bytes 786436
  3.4 0.9 %copy-start.4 = (bf16[32,2048]{1,0:T(8,128)(2,1)S(1)}, bf16[32,2048]{1,0:T(8,128)(2,1)}, u32[]{:S(2)}) copy-start(bf16[32,2048]{1,0:T(8,128)(2,1)} %w_first.1) | copy-start | bytes 393220
  4.4 25.9 %collective-permute-start.4 = (bf16[208,1024]{1,0:T(8,128)(2,1)S(1)}, bf16[208,1024]{1,0:T(8,128)(2,1)S(1)}, u32[]{:S(2)}, u32[]{:S(2)}) collective-permute-start(bf16[208,1024]{1,0:T(8,128)(2,1)S(1)} %get-tuple-element.23.refs_0_), channel_id=1, source_target_pairs={{0,2},{1,3},{2,0},{3,1},{4,6},{5,7},{6,4},{7,5},{8,10},{9,11},{10,... | collective-permute-start | bytes 1277960 | tf_op jit(solution)/shard_map/ppermute | solution.py:20
  7.4 22.9 %collective-permute-start.5 = (bf16[208,1024]{1,0:T(8,128)(2,1)S(1)}, bf16[208,1024]{1,0:T(8,128)(2,1)S(1)}, u32[]{:S(2)}, u32[]{:S(2)}) collective-permute-start(bf16[208,1024]{1,0:T(8,128)(2,1)S(1)} %get-tuple-element.23.refs_0_), channel_id=1, source_target_pairs={{0,4},{1,5},{2,6},{3,7},{4,0},{5,1},{6,2},{7,3},{8,12},{9,13},{10,... | collective-permute-start | bytes 1277960 | tf_op jit(solution)/shard_map/ppermute | solution.py:20
  8.9 21.4 %collective-permute-start.6 = (bf16[208,1024]{1,0:T(8,128)(2,1)S(1)}, bf16[208,1024]{1,0:T(8,128)(2,1)S(1)}, u32[]{:S(2)}, u32[]{:S(2)}) collective-permute-start(bf16[208,1024]{1,0:T(8,128)(2,1)S(1)} %get-tuple-element.23.refs_0_), channel_id=1, source_target_pairs={{0,6},{1,7},{2,4},{3,5},{4,2},{5,3},{6,0},{7,1},{8,14},{9,15},{10,... | collective-permute-start | bytes 1277960 | tf_op jit(solution)/shard_map/ppermute | solution.py:20
  9.0 18.9 %collective-permute-start.7 = (bf16[192,1024]{1,0:T(8,128)(2,1)S(1)}, bf16[192,1024]{1,0:T(8,128)(2,1)S(1)}, u32[]{:S(2)}, u32[]{:S(2)}) collective-permute-start(bf16[192,1024]{1,0:T(8,128)(2,1)S(1)} %get-tuple-element.24.refs_0_), channel_id=1, source_target_pairs={{0,8},{1,9},{2,10},{3,11},{4,12},{5,13},{6,14},{7,15},{8,0},{9,1},... | collective-permute-start | bytes 1179656 | tf_op jit(solution)/shard_map/ppermute | solution.py:20
  11.0 19.4 %collective-permute-start.8 = (bf16[192,1024]{1,0:T(8,128)(2,1)S(1)}, bf16[192,1024]{1,0:T(8,128)(2,1)S(1)}, u32[]{:S(2)}, u32[]{:S(2)}) collective-permute-start(bf16[192,1024]{1,0:T(8,128)(2,1)S(1)} %get-tuple-element.24.refs_0_), channel_id=1, source_target_pairs={{0,16},{1,17},{2,18},{3,19},{4,20},{5,21},{6,22},{7,23},{8,24},{9,... | collective-permute-start | bytes 1179656 | tf_op jit(solution)/shard_map/ppermute | solution.py:20
  13.6 1.0 %copy-start = (bf16[256,1024]{1,0:T(8,128)(2,1)S(1)}, bf16[256,1024]{1,0:T(8,128)(2,1)}, u32[]{:S(2)}) copy-start(bf16[256,1024]{1,0:T(8,128)(2,1)} %refs_0_.1) | copy-start | bytes 1572868
  31.1 25.9 %collective-permute-start.10 = (bf16[416,1024]{1,0:T(8,128)(2,1)S(1)}, bf16[416,1024]{1,0:T(8,128)(2,1)S(1)}, u32[]{:S(2)}, u32[]{:S(2)}) collective-permute-start(bf16[416,1024]{1,0:T(8,128)(2,1)S(1)} %shard_map.163), channel_id=1, source_target_pairs={{0,4},{1,5},{2,6},{3,7},{4,0},{5,1},{6,2},{7,3},{8,12},{9,13},{10,... | collective-permute-start | bytes 2555912 | tf_op jit(solution)/shard_map/ppermute | solution.py:20
  32.8 24.2 %collective-permute-start.9 = (bf16[416,1024]{1,0:T(8,128)(2,1)S(1)}, bf16[416,1024]{1,0:T(8,128)(2,1)S(1)}, u32[]{:S(2)}, u32[]{:S(2)}) collective-permute-start(bf16[416,1024]{1,0:T(8,128)(2,1)S(1)} %shard_map.162), channel_id=1, source_target_pairs={{0,2},{1,3},{2,0},{3,1},{4,6},{5,7},{6,4},{7,5},{8,10},{9,11},{10,... | collective-permute-start | bytes 2555912 | tf_op jit(solution)/shard_map/ppermute | solution.py:20
  34.4 22.6 %collective-permute-start.12 = (bf16[320,1024]{1,0:T(8,128)(2,1)S(1)}, bf16[320,1024]{1,0:T(8,128)(2,1)S(1)}, u32[]{:S(2)}, u32[]{:S(2)}) collective-permute-start(bf16[320,1024]{1,0:T(8,128)(2,1)S(1)} %shard_map.165), channel_id=1, source_target_pairs={{0,8},{1,9},{2,10},{3,11},{4,12},{5,13},{6,14},{7,15},{8,0},{9,1},... | collective-permute-start | bytes 1966088 | tf_op jit(solution)/shard_map/ppermute | solution.py:20
  34.9 22.1 %collective-permute-start.13 = (bf16[192,1024]{1,0:T(8,128)(2,1)S(1)}, bf16[192,1024]{1,0:T(8,128)(2,1)S(1)}, u32[]{:S(2)}, u32[]{:S(2)}) collective-permute-start(bf16[192,1024]{1,0:T(8,128)(2,1)S(1)} %shard_map.166), channel_id=1, source_target_pairs={{0,24},{1,25},{2,26},{3,27},{4,28},{5,29},{6,30},{7,31},{8,16},{9,... | collective-permute-start | bytes 1179656 | tf_op jit(solution)/shard_map/ppermute | solution.py:20
  37.0 20.2 %copy-start.9 = (s32[192,4]{0,1:T(4,128)S(1)}, s32[192,4]{0,1:T(4,128)}, u32[]{:S(2)}) copy-start(s32[192,4]{0,1:T(4,128)} %param.25) | copy-start | bytes 9220
  37.0 20.2 %copy-start.10 = (s32[192,1]{0,1:T(1,128)S(1)}, s32[192,1]{0,1:T(1,128)}, u32[]{:S(2)}) copy-start(s32[192,1]{0,1:T(1,128)} %param.26) | copy-start | bytes 2308
  37.1 20.4 %copy-start.1 = (bf16[192,1024]{1,0:T(8,128)(2,1)S(1)}, bf16[192,1024]{1,0:T(8,128)(2,1)}, u32[]{:S(2)}) copy-start(bf16[192,1024]{1,0:T(8,128)(2,1)} %refs_4_.1) | copy-start | bytes 1179652
  37.1 18.6 %collective-permute-start.11 = (bf16[128,1024]{1,0:T(8,128)(2,1)S(1)}, bf16[128,1024]{1,0:T(8,128)(2,1)S(1)}, u32[]{:S(2)}, u32[]{:S(2)}) collective-permute-start(bf16[128,1024]{1,0:T(8,128)(2,1)S(1)} %shard_map.164), channel_id=1, source_target_pairs={{0,6},{1,7},{2,4},{3,5},{4,2},{5,3},{6,0},{7,1},{8,14},{9,15},{10,... | collective-permute-start | bytes 786440 | tf_op jit(solution)/shard_map/ppermute | solution.py:20
  57.2 7.0 %collective-permute-start.15 = (bf16[1024,1024]{1,0:T(8,128)(2,1)S(1)}, bf16[1024,1024]{1,0:T(8,128)(2,1)S(1)}, u32[]{:S(2)}, u32[]{:S(2)}) collective-permute-start(bf16[1024,1024]{1,0:T(8,128)(2,1)S(1)} %shard_map.170.home), channel_id=1, source_target_pairs={{0,1},{1,0},{2,3},{3,2},{4,5},{5,4},{6,7},{7,6},{8,9},{9,8},{10,11... | collective-permute-start | bytes 6291464 | tf_op jit(solution)/shard_map/ppermute | solution.py:24
  57.5 5.2 %copy-start.3 = (bf16[128,1024]{1,0:T(8,128)(2,1)S(1)}, bf16[128,1024]{1,0:T(8,128)(2,1)}, u32[]{:S(2)}) copy-start(bf16[128,1024]{1,0:T(8,128)(2,1)} %act_table.1) | copy-start | bytes 786436
  57.5 5.2 %collective-permute-start.14 = (bf16[464,1024]{1,0:T(8,128)(2,1)S(1)}, bf16[464,1024]{1,0:T(8,128)(2,1)S(1)}, u32[]{:S(2)}, u32[]{:S(2)}) collective-permute-start(bf16[464,1024]{1,0:T(8,128)(2,1)S(1)} %shard_map.168.mine), channel_id=1, source_target_pairs={{0,1},{1,0},{2,3},{3,2},{4,5},{5,4},{6,7},{7,6},{8,9},{9,8},{10,11... | collective-permute-start | bytes 2850824 | tf_op jit(solution)/shard_map/ppermute | solution.py:24
  58.1 6.1 %copy-start.7 = (f32[2048]{0:T(1024)S(1)}, f32[2048]{0:T(1024)}, u32[]{:S(2)}) copy-start(f32[2048]{0:T(1024)} %param.19) | copy-start | bytes 24580
  58.2 17.3 %collective-permute-start.16 = (bf16[256,1024]{1,0:T(8,128)(2,1)S(1)}, bf16[256,1024]{1,0:T(8,128)(2,1)S(1)}, u32[]{:S(2)}, u32[]{:S(2)}) collective-permute-start(bf16[256,1024]{1,0:T(8,128)(2,1)S(1)} %shard_map.173), channel_id=1, source_target_pairs={{0,2},{1,3},{2,0},{3,1},{4,6},{5,7},{6,4},{7,5},{8,10},{9,11},{10,... | collective-permute-start | bytes 1572872 | tf_op jit(solution)/shard_map/ppermute | solution.py:20
  58.8 16.7 %collective-permute-start.17 = (bf16[256,1024]{1,0:T(8,128)(2,1)S(1)}, bf16[256,1024]{1,0:T(8,128)(2,1)S(1)}, u32[]{:S(2)}, u32[]{:S(2)}) collective-permute-start(bf16[256,1024]{1,0:T(8,128)(2,1)S(1)} %shard_map.174), channel_id=1, source_target_pairs={{0,4},{1,5},{2,6},{3,7},{4,0},{5,1},{6,2},{7,3},{8,12},{9,13},{10,... | collective-permute-start | bytes 1572872 | tf_op jit(solution)/shard_map/ppermute | solution.py:20
  60.0 15.4 %collective-permute-start.18 = (bf16[128,1024]{1,0:T(8,128)(2,1)S(1)}, bf16[128,1024]{1,0:T(8,128)(2,1)S(1)}, u32[]{:S(2)}, u32[]{:S(2)}) collective-permute-start(bf16[128,1024]{1,0:T(8,128)(2,1)S(1)} %shard_map.175), channel_id=1, source_target_pairs={{0,24},{1,25},{2,26},{3,27},{4,28},{5,29},{6,30},{7,31},{8,16},{9,... | collective-permute-start | bytes 786440 | tf_op jit(solution)/shard_map/ppermute | solution.py:20
  71.0 4.4 %copy-start.5 = (bf16[2048,8]{0,1:T(8,128)(2,1)S(1)}, bf16[2048,8]{0,1:T(8,128)(2,1)}, u32[]{:S(2)}) copy-start(bf16[2048,8]{0,1:T(8,128)(2,1)} %param.22) | copy-start | bytes 98308
  71.0 4.4 %copy-start.8 = (f32[2048]{0:T(1024)S(1)}, f32[2048]{0:T(1024)}, u32[]{:S(2)}) copy-start(f32[2048]{0:T(1024)} %param.21) | copy-start | bytes 24580
  75.5 5.3 %copy-start.6 = (s32[192,32]{0,1:T(8,128)S(1)}, s32[192,32]{0,1:T(8,128)}, u32[]{:S(2)}) copy-start(s32[192,32]{0,1:T(8,128)} %param.28) | copy-start | bytes 73732
  75.5 5.3 %copy-start.11 = (s32[192]{0:T(256)S(1)}, s32[192]{0:T(256)}, u32[]{:S(2)}) copy-start(s32[192]{0:T(256)} %param.24) | copy-start | bytes 2308
  75.5 5.3 %copy-start.12 = (s32[192]{0:T(256)S(1)}, s32[192]{0:T(256)}, u32[]{:S(2)}) copy-start(s32[192]{0:T(256)} %param.29) | copy-start | bytes 2308
  75.5 5.3 %copy-start.13 = (f32[8]{0:T(128)S(1)}, f32[8]{0:T(128)}, u32[]{:S(2)}) copy-start(f32[8]{0:T(128)} %param.23) | copy-start | bytes 100
  79.6 1.2 %collective-permute-start.19 = (f32[8,768]{1,0:T(8,128)S(1)}, f32[8,768]{1,0:T(8,128)S(1)}, u32[]{:S(2)}, u32[]{:S(2)}) collective-permute-start(f32[8,768]{1,0:T(8,128)S(1)} %get-tuple-element.41), channel_id=1, source_target_pairs={{0,1},{1,0},{2,3},{3,2},{4,5},{5,4},{6,7},{7,6},{8,9},{9,8},{10,11... | collective-permute-start | bytes 73736 | tf_op jit(solution)/shard_map/ppermute | solution.py:24

commit v5 on v4

--- a/solution.py
+++ b/solution.py
@@ -11,7 +11,7 @@
 AXES = ("trav", "bulk")
 
 TRAV, BULK = 4, 8
-X, Y, D, A, B, C = 1, 2, 3, 4, 8, 12
+X, Y, D, A, B, C = 1, 2, 3, 4, 12, 8
 PLANE = (0, X, Y, D)
 ID_ROWS = 16
 
@@ -205,22 +205,26 @@
             )
 
 
-def finish_second_kernel(pieces, depth, hidden, so_far, bias, w_head, *refs):
-    refs, (out_mine, out_theirs, weights) = refs[:-3], refs[-3:]
-    columns = line_up(pieces, refs, depth, weights)
-    half, core = so_far.shape[1], my_core()
-    step, rows = 512, hidden.shape[0] // 2
-    for m, out in ((0, out_mine), (rows, out_theirs)):
-        picked = jnp.concatenate([hidden[m : m + rows, column] for column in columns], axis=1)
-        advantage = jnp.zeros((rows, w_head.shape[0]), jnp.float32)
-        for n in range(0, half, step):
-            here = pl.ds(pl.multiple_of(core * half + n, step), step)
-            total = so_far[m : m + rows, n : n + step] + jnp.dot(
-                picked, weights[:, n : n + step], preferred_element_type=jnp.float32
-            )
-            layer = jnp.maximum(total + bias[:, here], 0.0).astype(jnp.bfloat16)
-            advantage = advantage + across(layer, w_head[:, here])
-        out[...] = advantage.T
+def finish_second(names, depth, first, hidden, so_far, bias, w_head, weights, out):
+    half, core, rows = so_far.shape[1], my_core(), out.shape[1]
+    here = slice(first, first + rows)
+    picked = jnp.concatenate([hidden[here, name * depth : (name + 1) * depth] for name in names], axis=1)
+    advantage = jnp.zeros((rows, w_head.shape[0]), jnp.float32)
+    step = 512
+    for n in range(0, half, step):
+        columns = pl.ds(pl.multiple_of(core * half + n, step), step)
+        total = so_far[here, n : n + step] + jnp.dot(
+            picked, weights[:, n : n + step], preferred_element_type=jnp.float32
+        )
+        layer = jnp.maximum(total + bias[:, columns], 0.0).astype(jnp.bfloat16)
+        advantage = advantage + across(layer, w_head[:, columns])
+    out[...] = advantage.T
+
+
+def theirs_kernel(pieces, names, depth, first, hidden, so_far, bias, w_head, *refs):
+    refs, (out, weights) = refs[:-2], refs[-2:]
+    line_up(pieces, refs, depth, weights)
+    finish_second(names, depth, first, hidden, so_far, bias, w_head, weights, out)
 
 
 def stack_kernel(places, *refs):
@@ -297,9 +301,7 @@
     from_a, from_b = [swap_chip(own, chip) for chip in (A, B)]
     meta = call(functools.partial(meta_kernel, capacity), shape(ID_ROWS, feature_count), 4)(owner, sampled_actions.T)
     table = stack((bucket_table, 0, bucket_table.shape[0]))
-    from_x, from_y, from_d, from_a, from_b, table = lax.optimization_barrier(
-        (from_x, from_y, from_d, from_a, from_b, table)
-    )
+    from_x, from_y, from_d, from_a, table = lax.optimization_barrier((from_x, from_y, from_d, from_a, table))
 
     served = call(
         functools.partial(serve_kernel, capacity, par_count), (shape(wide, feature_count),) * len(PLANE), 6
@@ -350,18 +352,21 @@
         functools.partial(second_kernel, early, chip_two),
         shape(2 * branches, half, jnp.float32),
         16,
-        [pltpu.VMEM((len(early) * chip_two, half), jnp.bfloat16)],
+        [pltpu.VMEM((len({piece[0] for piece in early}) * chip_two, half), jnp.bfloat16)],
     )(hidden, *arrays)
     late = [(C, 3, chip_one, 0, chip_two), (X ^ C, 0, 0, 0, chip_two), (Y ^ C, 1, 0, 0, chip_two)]
     late += [(D ^ C, 2, 0, 0, chip_two)]
     late += [(D ^ A, 0, chip_two, 0, cut), (D ^ A, 1, chip_two, cut, cut)]
     late += [(D ^ B, 0, chip_two + cut, 0, cut), (D ^ B, 1, chip_two + cut, cut, cut)]
-    mine, theirs = call(
-        functools.partial(finish_second_kernel, late, chip_two),
-        (shape(w_head.shape[1], branches, jnp.float32),) * 2,
-        14,
-        [pltpu.VMEM((6 * chip_two, half), jnp.bfloat16)],
-    )(hidden, so_far, b_second[None, :], w_head.T, x_c, y_c, d_c, c_da)
+    names = list(dict.fromkeys(piece[0] for piece in late))
+    partial = shape(w_head.shape[1], branches, jnp.float32)
+    common = (hidden, so_far, b_second[None, :], w_head.T)
+    theirs, late_weights = call(
+        functools.partial(theirs_kernel, late, names, chip_two, branches),
+        (partial, shape(len(names) * chip_two, half)),
+        12,
+    )(*common, x_c, y_c, d_c, c_da)
+    mine = call(functools.partial(finish_second, names, chip_two, 0), partial, 10)(*common, late_weights)
     strategy, values = call(
         last_kernel, (shape(legal_mask.shape[1], par_count, jnp.float32), shape(1, par_count // 4, jnp.float32)), 4
     )(branch_counts[None, :], ancestor[None, :], legal_mask.T, b_head[None, :], mine, swap_core(theirs))

time: 81.9 us -> 80.9 us (0.988)
  waiting for transfers between devices: 36.2 us -> 34.9 us
    pallas_call x20 -> x21, Pallas kernels: 19 us -> 19.7 us  [run(): pl.pallas_call(kernel, out_shape=tuple(outs) if many else outs, in_specs=...]
  transfers between devices with their start and end apart: 20 -> 20, of which waited for: 6 -> 5; matrix products, arithmetic and copies ran while one was open for 1% -> 1% of each run, Pallas kernels for 16% -> 20%
where the time goes in v5:
time: 80.9 us; the launch traced here: 80.7 us
  waiting for transfers between devices  34.9 us (43%)
  starting transfers between devices  21.5 us (27%)
  Pallas kernels  19.7 us (24%)
  local copies, waits for them, and re-layouts  2.95 us (4%)
  between operations  0.95 us (1%)
    ppermute x13, waiting for transfers between devices, swap_chip(): lax.ppermute(value, AXES, [(i, i ^ chip << 1) for i in range(TRAV * BULK)])  34.3 us
    pallas_call x21, Pallas kernels, run(): pl.pallas_call(kernel, out_shape=tuple(outs) if many else outs, in_specs=...  19.7 us
    ppermute x13, starting transfers between devices, swap_chip(): lax.ppermute(value, AXES, [(i, i ^ chip << 1) for i in range(TRAV * BULK)])  19.6 us
    unnamed x28, local copies, waits for them, and re-layouts  2.95 us
    ppermute x7, starting transfers between devices, swap_core(): return lax.ppermute(value, AXES, [(i, i ^ 1) for i in range(TRAV * BULK)])  1.9 us
  transfers between devices with their start and end apart: 20, of which 5 were waited for; matrix products, arithmetic and copies ran while one was open for 1% of the time, Pallas kernels for 20%

profile of v5, /device:TPU:0, one launch (start us, length us, event | category | flops | bytes accessed | tf_op | source)
XLA Modules:
  0.0 80.7 jit_solution(9838815842711789804)
XLA Ops:
  0.6 0.5 collective-permute-start.1
  1.1 0.1 collective-permute-start
  1.2 0.4 collective-permute-start.2
  1.7 0.1 collective-permute-start.3
  1.7 0.7 pad_add_fusion.ids
  2.4 0.9 %copy-done.2 = bf16[64,2048]{1,0:T(8,128)(2,1)S(1)} copy-done((bf16[64,2048]{1,0:T(8,128)(2,1)S(1)}, bf16[64,2048]{1,0:T(8,128)(2,1)}, u32[]{:S(2)}) %copy-start.2) | copy-done | bytes 262168
  3.4 0.9 %copy-done.5 = bf16[32,2048]{1,0:T(8,128)(2,1)S(1)} copy-done((bf16[32,2048]{1,0:T(8,128)(2,1)S(1)}, bf16[32,2048]{1,0:T(8,128)(2,1)}, u32[]{:S(2)}) %copy-start.5) | copy-done | bytes 131096
  4.4 0.1 shard_map.159
  4.4 3.0 %collective-permute-start.4 = (bf16[208,1024]{1,0:T(8,128)(2,1)S(1)}, bf16[208,1024]{1,0:T(8,128)(2,1)S(1)}, u32[]{:S(2)}, u32[]{:S(2)}) collective-permute-start(bf16[208,1024]{1,0:T(8,128)(2,1)S(1)} %get-tuple-element.22.refs_0_), channel_id=1, source_target_pairs={{0,2},{1,3},{2,0},{3,1},{4,6},{5,7},{6,4},{7,5},{8,10},{9,11},{10,... | collective-permute-start | bytes 1277960 | tf_op jit(solution)/shard_map/ppermute | solution.py:20
  7.4 1.5 %collective-permute-start.5 = (bf16[208,1024]{1,0:T(8,128)(2,1)S(1)}, bf16[208,1024]{1,0:T(8,128)(2,1)S(1)}, u32[]{:S(2)}, u32[]{:S(2)}) collective-permute-start(bf16[208,1024]{1,0:T(8,128)(2,1)S(1)} %get-tuple-element.22.refs_0_), channel_id=1, source_target_pairs={{0,4},{1,5},{2,6},{3,7},{4,0},{5,1},{6,2},{7,3},{8,12},{9,13},{10,... | collective-permute-start | bytes 1277960 | tf_op jit(solution)/shard_map/ppermute | solution.py:20
  8.9 0.0 collective-permute-start.6
  9.0 2.0 %collective-permute-start.7 = (bf16[192,1024]{1,0:T(8,128)(2,1)S(1)}, bf16[192,1024]{1,0:T(8,128)(2,1)S(1)}, u32[]{:S(2)}, u32[]{:S(2)}) collective-permute-start(bf16[192,1024]{1,0:T(8,128)(2,1)S(1)} %get-tuple-element.23.refs_0_), channel_id=1, source_target_pairs={{0,8},{1,9},{2,10},{3,11},{4,12},{5,13},{6,14},{7,15},{8,0},{9,1},... | collective-permute-start | bytes 1179656 | tf_op jit(solution)/shard_map/ppermute | solution.py:20
  11.0 2.5 %collective-permute-start.8 = (bf16[192,1024]{1,0:T(8,128)(2,1)S(1)}, bf16[192,1024]{1,0:T(8,128)(2,1)S(1)}, u32[]{:S(2)}, u32[]{:S(2)}) collective-permute-start(bf16[192,1024]{1,0:T(8,128)(2,1)S(1)} %get-tuple-element.23.refs_0_), channel_id=1, source_target_pairs={{0,24},{1,25},{2,26},{3,27},{4,28},{5,29},{6,30},{7,31},{8,16},{9,... | collective-permute-start | bytes 1179656 | tf_op jit(solution)/shard_map/ppermute | solution.py:20
  13.5 1.0 %copy-done = bf16[256,1024]{1,0:T(8,128)(2,1)S(1)} copy-done((bf16[256,1024]{1,0:T(8,128)(2,1)S(1)}, bf16[256,1024]{1,0:T(8,128)(2,1)}, u32[]{:S(2)}) %copy-start) | copy-done | bytes 524312
  14.5 6.0 %collective-permute-done.7.refs_0_.refs_3_ = bf16[192,1024]{1,0:T(8,128)(2,1)S(1)} collective-permute-done((bf16[192,1024]{1,0:T(8,128)(2,1)S(1)}, bf16[192,1024]{1,0:T(8,128)(2,1)S(1)}, u32[]{:S(2)}, u32[]{:S(2)}) %collective-permute-start.7) | collective-permute-done | bytes 393248 | tf_op jit(solution)/shard_map/ppermute | solution.py:20
  20.6 7.5 %collective-permute-done.5.refs_2_.refs_3_.refs_1_ = bf16[208,1024]{1,0:T(8,128)(2,1)S(1)} collective-permute-done((bf16[208,1024]{1,0:T(8,128)(2,1)S(1)}, bf16[208,1024]{1,0:T(8,128)(2,1)S(1)}, u32[]{:S(2)}, u32[]{:S(2)}) %collective-permute-start.5) | collective-permute-done | bytes 426016 | tf_op jit(solution)/shard_map/ppermute | solution.py:20
  28.1 0.7 shard_map.161
  28.8 1.5 %collective-permute-done.8.refs_1_.refs_0_.refs_4_ = bf16[192,1024]{1,0:T(8,128)(2,1)S(1)} collective-permute-done((bf16[192,1024]{1,0:T(8,128)(2,1)S(1)}, bf16[192,1024]{1,0:T(8,128)(2,1)S(1)}, u32[]{:S(2)}, u32[]{:S(2)}) %collective-permute-start.8) | collective-permute-done | bytes 393248 | tf_op jit(solution)/shard_map/ppermute | solution.py:20
  30.2 0.1 shard_map.163
  30.3 1.6 %collective-permute-start.10 = (bf16[416,1024]{1,0:T(8,128)(2,1)S(1)}, bf16[416,1024]{1,0:T(8,128)(2,1)S(1)}, u32[]{:S(2)}, u32[]{:S(2)}) collective-permute-start(bf16[416,1024]{1,0:T(8,128)(2,1)S(1)} %shard_map.163), channel_id=1, source_target_pairs={{0,4},{1,5},{2,6},{3,7},{4,0},{5,1},{6,2},{7,3},{8,12},{9,13},{10,... | collective-permute-start | bytes 2555912 | tf_op jit(solution)/shard_map/ppermute | solution.py:20
  31.9 0.1 shard_map.162
  31.9 1.6 %collective-permute-start.9 = (bf16[416,1024]{1,0:T(8,128)(2,1)S(1)}, bf16[416,1024]{1,0:T(8,128)(2,1)S(1)}, u32[]{:S(2)}, u32[]{:S(2)}) collective-permute-start(bf16[416,1024]{1,0:T(8,128)(2,1)S(1)} %shard_map.162), channel_id=1, source_target_pairs={{0,2},{1,3},{2,0},{3,1},{4,6},{5,7},{6,4},{7,5},{8,10},{9,11},{10,... | collective-permute-start | bytes 2555912 | tf_op jit(solution)/shard_map/ppermute | solution.py:20
  33.5 0.6 collective-permute-start.12
  34.2 2.3 %collective-permute-start.13 = (bf16[192,1024]{1,0:T(8,128)(2,1)S(1)}, bf16[192,1024]{1,0:T(8,128)(2,1)S(1)}, u32[]{:S(2)}, u32[]{:S(2)}) collective-permute-start(bf16[192,1024]{1,0:T(8,128)(2,1)S(1)} %shard_map.166), channel_id=1, source_target_pairs={{0,16},{1,17},{2,18},{3,19},{4,20},{5,21},{6,22},{7,23},{8,24},{9,... | collective-permute-start | bytes 1179656 | tf_op jit(solution)/shard_map/ppermute | solution.py:20
  36.5 0.0 copy-start.9
  36.5 0.0 copy-start.10
  36.5 0.0 copy-start.1
  36.5 0.5 collective-permute-start.11
  37.1 19.3 %collective-permute-done.11.refs_3_.refs_9_ = bf16[128,1024]{1,0:T(8,128)(2,1)S(1)} collective-permute-done((bf16[128,1024]{1,0:T(8,128)(2,1)S(1)}, bf16[128,1024]{1,0:T(8,128)(2,1)S(1)}, u32[]{:S(2)}, u32[]{:S(2)}) %collective-permute-start.11) | collective-permute-done | bytes 262176 | tf_op jit(solution)/shard_map/ppermute | solution.py:20
  56.4 0.2 shard_map.170.home
  56.6 0.1 collective-permute-start.15
  56.7 0.2 shard_map.167.refs_5_
  56.9 0.1 shard_map.168.mine
  56.9 0.0 copy-start.3
  56.9 0.5 collective-permute-start.14
  57.6 0.0 copy-start.8
  57.6 1.6 %collective-permute-start.16 = (bf16[256,1024]{1,0:T(8,128)(2,1)S(1)}, bf16[256,1024]{1,0:T(8,128)(2,1)S(1)}, u32[]{:S(2)}, u32[]{:S(2)}) collective-permute-start(bf16[256,1024]{1,0:T(8,128)(2,1)S(1)} %shard_map.173), channel_id=1, source_target_pairs={{0,2},{1,3},{2,0},{3,1},{4,6},{5,7},{6,4},{7,5},{8,10},{9,11},{10,... | collective-permute-start | bytes 1572872 | tf_op jit(solution)/shard_map/ppermute | solution.py:20
  59.1 1.5 %collective-permute-start.17 = (bf16[256,1024]{1,0:T(8,128)(2,1)S(1)}, bf16[256,1024]{1,0:T(8,128)(2,1)S(1)}, u32[]{:S(2)}, u32[]{:S(2)}) collective-permute-start(bf16[256,1024]{1,0:T(8,128)(2,1)S(1)} %shard_map.174), channel_id=1, source_target_pairs={{0,4},{1,5},{2,6},{3,7},{4,0},{5,1},{6,2},{7,3},{8,12},{9,13},{10,... | collective-permute-start | bytes 1572872 | tf_op jit(solution)/shard_map/ppermute | solution.py:20
  60.7 1.0 %collective-permute-start.18 = (bf16[128,1024]{1,0:T(8,128)(2,1)S(1)}, bf16[128,1024]{1,0:T(8,128)(2,1)S(1)}, u32[]{:S(2)}, u32[]{:S(2)}) collective-permute-start(bf16[128,1024]{1,0:T(8,128)(2,1)S(1)} %shard_map.175), channel_id=1, source_target_pairs={{0,16},{1,17},{2,18},{3,19},{4,20},{5,21},{6,22},{7,23},{8,24},{9,... | collective-permute-start | bytes 786440 | tf_op jit(solution)/shard_map/ppermute | solution.py:20
  61.6 0.5 collective-permute-done.14.theirs
  62.2 1.4 %shard_map.169.inputs = bf16[1536,1024]{1,0:T(8,128)(2,1)S(1)} custom-call(bf16[128,1024]{1,0:T(8,128)(2,1)S(1)} %copy-done.3, bf16[464,1024]{1,0:T(8,128)(2,1)S(1)} %shard_map.168.mine, bf16[464,1024]{1,0:T(8,128)(2,1)S(1)} %collective-permute-done.14.theirs), custom_call_target="tpu_custom_call" | custom-call | tf_op jit(solution)/shard_map/pallas_call | solution.py:48
  63.6 6.8 %shard_map.171.hidden = bf16[1536,2048]{1,0:T(8,128)(2,1)S(1)} custom-call(bf16[1536,1024]{1,0:T(8,128)(2,1)S(1)} %shard_map.169.inputs, bf16[1024,1024]{1,0:T(8,128)(2,1)S(1)} %shard_map.170.home, bf16[1024,1024]{1,0:T(8,128)(2,1)S(1)} %collective-permute-done.15.other, f32[1,2048]{1,0:T(1,128)S(1)} %bitcast.17), custom_call_target="tpu_custom_call" | custom-call | tf_op jit(solution)/shard_map/pallas_call | solution.py:48
  70.4 0.0 copy-start.6
  70.5 4.4 %shard_map.172.so_far = f32[1536,1024]{1,0:T(8,128)S(1)} custom-call(bf16[1536,2048]{1,0:T(8,128)(2,1)S(1)} %shard_map.171.hidden, bf16[192,1024]{1,0:T(8,128)(2,1)S(1)} %get-tuple-element.23.refs_0_, bf16[208,1024]{1,0:T(8,128)(2,1)S(1)} %collective-permute-done.4.refs_1_.refs_2_.refs_0_, ...), custom_call_target="tpu_custom_call" | custom-call | tf_op jit(solution)/shard_map/pallas_call | solution.py:48
  74.9 2.4 %shard_map.176 = (f32[8,768]{1,0:T(8,128)S(1)}, bf16[768,1024]{1,0:T(8,128)(2,1)S(1)}) custom-call(bf16[1536,2048]{1,0:T(8,128)(2,1)S(1)} %shard_map.171.hidden, f32[1536,1024]{1,0:T(8,128)S(1)} %shard_map.172.so_far, f32[1,2048]{1,0:T(1,128)S(1)} %bitcast.14, bf16[8,2048]{1,0:T(8,128)(2,1)S(1)} %bitcast.12, ...), custom_call_target="tpu_custom_call" | custom-call | tf_op jit(solution)/shard_map/pallas_call | solution.py:48
  77.3 0.2 collective-permute-start.19
  77.4 2.4 %shard_map.177.mine = f32[8,768]{1,0:T(8,128)S(1)} custom-call(bf16[1536,2048]{1,0:T(8,128)(2,1)S(1)} %shard_map.171.hidden, f32[1536,1024]{1,0:T(8,128)S(1)} %shard_map.172.so_far, f32[1,2048]{1,0:T(1,128)S(1)} %bitcast.15, bf16[8,2048]{1,0:T(8,128)(2,1)S(1)} %bitcast.13, bf16[768,1024]{1,0:T(8,128)(2,1)S(1)} %get-tuple-element.38.weights), custom_call_target="tpu_custom_call" | custom-call | tf_op jit(solution)/shard_map/pallas_call | solution.py:48
  79.9 0.8 %shard_map.178 = (f32[32,192]{1,0:T(8,128)}, f32[1,48]{1,0:T(1,128)}) custom-call(s32[1,192]{1,0:T(1,128)S(1)} %bitcast.22, s32[1,192]{1,0:T(1,128)S(1)} %bitcast.23, s32[32,192]{1,0:T(8,128)S(1)} %bitcast.16, f32[1,8]{1,0:T(1,128)S(1)} %bitcast.24, f32[8,768]{1,0:T(8,128)S(1)} %shard_map.177.mine, f32[8,768]{1,0:T(8,128)S(1)} %collective-permute-done.19.theirs), custom_call_target="tpu_custom_call" | custom-call | tf_op jit(solution)/shard_map/pallas_call | solution.py:48
  (42 shorter events, 0.3 us)
Async XLA Ops:
  0.6 3.7 %collective-permute-start.1 = (bf16[64,2048]{1,0:T(8,128)(2,1)}, bf16[64,2048]{1,0:T(8,128)(2,1)S(1)}, u32[]{:S(2)}, u32[]{:S(2)}) collective-permute-start(bf16[64,2048]{1,0:T(8,128)(2,1)} %w_second.1), channel_id=1, source_target_pairs={{0,1},{1,0},{2,3},{3,2},{4,5},{5,4},{6,7},{7,6},{8,9},{9,8},{10,11... | collective-permute-start | bytes 786440 | tf_op jit(solution)/shard_map/ppermute | solution.py:24
  1.1 3.2 %collective-permute-start = (bf16[32,2048]{1,0:T(8,128)(2,1)}, bf16[32,2048]{1,0:T(8,128)(2,1)S(1)}, u32[]{:S(2)}, u32[]{:S(2)}) collective-permute-start(bf16[32,2048]{1,0:T(8,128)(2,1)} %w_first.1), channel_id=1, source_target_pairs={{0,1},{1,0},{2,3},{3,2},{4,5},{5,4},{6,7},{7,6},{8,9},{9,8},{10,11... | collective-permute-start | bytes 393224 | tf_op jit(solution)/shard_map/ppermute | solution.py:24
  1.2 3.1 %collective-permute-start.2 = (s32[1,192]{1,0:T(1,128)}, s32[1,192]{1,0:T(1,128)S(1)}, u32[]{:S(2)}, u32[]{:S(2)}) collective-permute-start(s32[1,192]{1,0:T(1,128)} %bitcast.19), channel_id=1, source_target_pairs={{0,1},{1,0},{2,3},{3,2},{4,5},{5,4},{6,7},{7,6},{8,9},{9,8},{10,11... | collective-permute-start | bytes 2312 | tf_op jit(solution)/shard_map/ppermute | solution.py:24
  1.7 2.7 %collective-permute-start.3 = (s32[1,192]{1,0:T(1,128)}, s32[1,192]{1,0:T(1,128)S(1)}, u32[]{:S(2)}, u32[]{:S(2)}) collective-permute-start(s32[1,192]{1,0:T(1,128)} %bitcast.25), channel_id=1, source_target_pairs={{0,1},{1,0},{2,3},{3,2},{4,5},{5,4},{6,7},{7,6},{8,9},{9,8},{10,11... | collective-permute-start | bytes 2312 | tf_op jit(solution)/shard_map/ppermute | solution.py:24
  2.4 0.9 %copy-start.2 = (bf16[64,2048]{1,0:T(8,128)(2,1)S(1)}, bf16[64,2048]{1,0:T(8,128)(2,1)}, u32[]{:S(2)}) copy-start(bf16[64,2048]{1,0:T(8,128)(2,1)} %w_second.1) | copy-start | bytes 786436
  3.4 0.9 %copy-start.5 = (bf16[32,2048]{1,0:T(8,128)(2,1)S(1)}, bf16[32,2048]{1,0:T(8,128)(2,1)}, u32[]{:S(2)}) copy-start(bf16[32,2048]{1,0:T(8,128)(2,1)} %w_first.1) | copy-start | bytes 393220
  4.4 16.1 %collective-permute-start.4 = (bf16[208,1024]{1,0:T(8,128)(2,1)S(1)}, bf16[208,1024]{1,0:T(8,128)(2,1)S(1)}, u32[]{:S(2)}, u32[]{:S(2)}) collective-permute-start(bf16[208,1024]{1,0:T(8,128)(2,1)S(1)} %get-tuple-element.22.refs_0_), channel_id=1, source_target_pairs={{0,2},{1,3},{2,0},{3,1},{4,6},{5,7},{6,4},{7,5},{8,10},{9,11},{10,... | collective-permute-start | bytes 1277960 | tf_op jit(solution)/shard_map/ppermute | solution.py:20
  7.4 20.7 %collective-permute-start.5 = (bf16[208,1024]{1,0:T(8,128)(2,1)S(1)}, bf16[208,1024]{1,0:T(8,128)(2,1)S(1)}, u32[]{:S(2)}, u32[]{:S(2)}) collective-permute-start(bf16[208,1024]{1,0:T(8,128)(2,1)S(1)} %get-tuple-element.22.refs_0_), channel_id=1, source_target_pairs={{0,4},{1,5},{2,6},{3,7},{4,0},{5,1},{6,2},{7,3},{8,12},{9,13},{10,... | collective-permute-start | bytes 1277960 | tf_op jit(solution)/shard_map/ppermute | solution.py:20
  8.9 19.1 %collective-permute-start.6 = (bf16[208,1024]{1,0:T(8,128)(2,1)S(1)}, bf16[208,1024]{1,0:T(8,128)(2,1)S(1)}, u32[]{:S(2)}, u32[]{:S(2)}) collective-permute-start(bf16[208,1024]{1,0:T(8,128)(2,1)S(1)} %get-tuple-element.22.refs_0_), channel_id=1, source_target_pairs={{0,6},{1,7},{2,4},{3,5},{4,2},{5,3},{6,0},{7,1},{8,14},{9,15},{10,... | collective-permute-start | bytes 1277960 | tf_op jit(solution)/shard_map/ppermute | solution.py:20
  9.0 11.6 %collective-permute-start.7 = (bf16[192,1024]{1,0:T(8,128)(2,1)S(1)}, bf16[192,1024]{1,0:T(8,128)(2,1)S(1)}, u32[]{:S(2)}, u32[]{:S(2)}) collective-permute-start(bf16[192,1024]{1,0:T(8,128)(2,1)S(1)} %get-tuple-element.23.refs_0_), channel_id=1, source_target_pairs={{0,8},{1,9},{2,10},{3,11},{4,12},{5,13},{6,14},{7,15},{8,0},{9,1},... | collective-permute-start | bytes 1179656 | tf_op jit(solution)/shard_map/ppermute | solution.py:20
  11.0 19.2 %collective-permute-start.8 = (bf16[192,1024]{1,0:T(8,128)(2,1)S(1)}, bf16[192,1024]{1,0:T(8,128)(2,1)S(1)}, u32[]{:S(2)}, u32[]{:S(2)}) collective-permute-start(bf16[192,1024]{1,0:T(8,128)(2,1)S(1)} %get-tuple-element.23.refs_0_), channel_id=1, source_target_pairs={{0,24},{1,25},{2,26},{3,27},{4,28},{5,29},{6,30},{7,31},{8,16},{9,... | collective-permute-start | bytes 1179656 | tf_op jit(solution)/shard_map/ppermute | solution.py:20
  13.5 1.0 %copy-start = (bf16[256,1024]{1,0:T(8,128)(2,1)S(1)}, bf16[256,1024]{1,0:T(8,128)(2,1)}, u32[]{:S(2)}) copy-start(bf16[256,1024]{1,0:T(8,128)(2,1)} %refs_0_.1) | copy-start | bytes 1572868
  30.3 26.1 %collective-permute-start.10 = (bf16[416,1024]{1,0:T(8,128)(2,1)S(1)}, bf16[416,1024]{1,0:T(8,128)(2,1)S(1)}, u32[]{:S(2)}, u32[]{:S(2)}) collective-permute-start(bf16[416,1024]{1,0:T(8,128)(2,1)S(1)} %shard_map.163), channel_id=1, source_target_pairs={{0,4},{1,5},{2,6},{3,7},{4,0},{5,1},{6,2},{7,3},{8,12},{9,13},{10,... | collective-permute-start | bytes 2555912 | tf_op jit(solution)/shard_map/ppermute | solution.py:20
  31.9 24.5 %collective-permute-start.9 = (bf16[416,1024]{1,0:T(8,128)(2,1)S(1)}, bf16[416,1024]{1,0:T(8,128)(2,1)S(1)}, u32[]{:S(2)}, u32[]{:S(2)}) collective-permute-start(bf16[416,1024]{1,0:T(8,128)(2,1)S(1)} %shard_map.162), channel_id=1, source_target_pairs={{0,2},{1,3},{2,0},{3,1},{4,6},{5,7},{6,4},{7,5},{8,10},{9,11},{10,... | collective-permute-start | bytes 2555912 | tf_op jit(solution)/shard_map/ppermute | solution.py:20
  33.5 22.9 %collective-permute-start.12 = (bf16[320,1024]{1,0:T(8,128)(2,1)S(1)}, bf16[320,1024]{1,0:T(8,128)(2,1)S(1)}, u32[]{:S(2)}, u32[]{:S(2)}) collective-permute-start(bf16[320,1024]{1,0:T(8,128)(2,1)S(1)} %shard_map.165), channel_id=1, source_target_pairs={{0,8},{1,9},{2,10},{3,11},{4,12},{5,13},{6,14},{7,15},{8,0},{9,1},... | collective-permute-start | bytes 1966088 | tf_op jit(solution)/shard_map/ppermute | solution.py:20
  34.2 22.2 %collective-permute-start.13 = (bf16[192,1024]{1,0:T(8,128)(2,1)S(1)}, bf16[192,1024]{1,0:T(8,128)(2,1)S(1)}, u32[]{:S(2)}, u32[]{:S(2)}) collective-permute-start(bf16[192,1024]{1,0:T(8,128)(2,1)S(1)} %shard_map.166), channel_id=1, source_target_pairs={{0,16},{1,17},{2,18},{3,19},{4,20},{5,21},{6,22},{7,23},{8,24},{9,... | collective-permute-start | bytes 1179656 | tf_op jit(solution)/shard_map/ppermute | solution.py:20
  36.5 20.2 %copy-start.9 = (s32[192,4]{0,1:T(4,128)S(1)}, s32[192,4]{0,1:T(4,128)}, u32[]{:S(2)}) copy-start(s32[192,4]{0,1:T(4,128)} %param.25) | copy-start | bytes 9220
  36.5 20.2 %copy-start.10 = (s32[192,1]{0,1:T(1,128)S(1)}, s32[192,1]{0,1:T(1,128)}, u32[]{:S(2)}) copy-start(s32[192,1]{0,1:T(1,128)} %param.26) | copy-start | bytes 2308
  36.5 20.3 %copy-start.1 = (bf16[192,1024]{1,0:T(8,128)(2,1)S(1)}, bf16[192,1024]{1,0:T(8,128)(2,1)}, u32[]{:S(2)}) copy-start(bf16[192,1024]{1,0:T(8,128)(2,1)} %refs_4_.1) | copy-start | bytes 1179652
  36.5 19.9 %collective-permute-start.11 = (bf16[128,1024]{1,0:T(8,128)(2,1)S(1)}, bf16[128,1024]{1,0:T(8,128)(2,1)S(1)}, u32[]{:S(2)}, u32[]{:S(2)}) collective-permute-start(bf16[128,1024]{1,0:T(8,128)(2,1)S(1)} %shard_map.164), channel_id=1, source_target_pairs={{0,6},{1,7},{2,4},{3,5},{4,2},{5,3},{6,0},{7,1},{8,14},{9,15},{10,... | collective-permute-start | bytes 786440 | tf_op jit(solution)/shard_map/ppermute | solution.py:20
  56.6 7.0 %collective-permute-start.15 = (bf16[1024,1024]{1,0:T(8,128)(2,1)S(1)}, bf16[1024,1024]{1,0:T(8,128)(2,1)S(1)}, u32[]{:S(2)}, u32[]{:S(2)}) collective-permute-start(bf16[1024,1024]{1,0:T(8,128)(2,1)S(1)} %shard_map.170.home), channel_id=1, source_target_pairs={{0,1},{1,0},{2,3},{3,2},{4,5},{5,4},{6,7},{7,6},{8,9},{9,8},{10,11... | collective-permute-start | bytes 6291464 | tf_op jit(solution)/shard_map/ppermute | solution.py:24
  56.9 5.2 %copy-start.3 = (bf16[128,1024]{1,0:T(8,128)(2,1)S(1)}, bf16[128,1024]{1,0:T(8,128)(2,1)}, u32[]{:S(2)}) copy-start(bf16[128,1024]{1,0:T(8,128)(2,1)} %act_table.1) | copy-start | bytes 786436
  56.9 5.2 %collective-permute-start.14 = (bf16[464,1024]{1,0:T(8,128)(2,1)S(1)}, bf16[464,1024]{1,0:T(8,128)(2,1)S(1)}, u32[]{:S(2)}, u32[]{:S(2)}) collective-permute-start(bf16[464,1024]{1,0:T(8,128)(2,1)S(1)} %shard_map.168.mine), channel_id=1, source_target_pairs={{0,1},{1,0},{2,3},{3,2},{4,5},{5,4},{6,7},{7,6},{8,9},{9,8},{10,11... | collective-permute-start | bytes 2850824 | tf_op jit(solution)/shard_map/ppermute | solution.py:24
  57.6 6.1 %copy-start.8 = (f32[2048]{0:T(1024)S(1)}, f32[2048]{0:T(1024)}, u32[]{:S(2)}) copy-start(f32[2048]{0:T(1024)} %param.19) | copy-start | bytes 24580
  57.6 17.3 %collective-permute-start.16 = (bf16[256,1024]{1,0:T(8,128)(2,1)S(1)}, bf16[256,1024]{1,0:T(8,128)(2,1)S(1)}, u32[]{:S(2)}, u32[]{:S(2)}) collective-permute-start(bf16[256,1024]{1,0:T(8,128)(2,1)S(1)} %shard_map.173), channel_id=1, source_target_pairs={{0,2},{1,3},{2,0},{3,1},{4,6},{5,7},{6,4},{7,5},{8,10},{9,11},{10,... | collective-permute-start | bytes 1572872 | tf_op jit(solution)/shard_map/ppermute | solution.py:20
  59.1 15.7 %collective-permute-start.17 = (bf16[256,1024]{1,0:T(8,128)(2,1)S(1)}, bf16[256,1024]{1,0:T(8,128)(2,1)S(1)}, u32[]{:S(2)}, u32[]{:S(2)}) collective-permute-start(bf16[256,1024]{1,0:T(8,128)(2,1)S(1)} %shard_map.174), channel_id=1, source_target_pairs={{0,4},{1,5},{2,6},{3,7},{4,0},{5,1},{6,2},{7,3},{8,12},{9,13},{10,... | collective-permute-start | bytes 1572872 | tf_op jit(solution)/shard_map/ppermute | solution.py:20
  60.7 14.2 %collective-permute-start.18 = (bf16[128,1024]{1,0:T(8,128)(2,1)S(1)}, bf16[128,1024]{1,0:T(8,128)(2,1)S(1)}, u32[]{:S(2)}, u32[]{:S(2)}) collective-permute-start(bf16[128,1024]{1,0:T(8,128)(2,1)S(1)} %shard_map.175), channel_id=1, source_target_pairs={{0,16},{1,17},{2,18},{3,19},{4,20},{5,21},{6,22},{7,23},{8,24},{9,... | collective-permute-start | bytes 786440 | tf_op jit(solution)/shard_map/ppermute | solution.py:20
  70.4 4.4 %copy-start.4 = (bf16[2048,8]{0,1:T(8,128)(2,1)S(1)}, bf16[2048,8]{0,1:T(8,128)(2,1)}, u32[]{:S(2)}) copy-start(bf16[2048,8]{0,1:T(8,128)(2,1)} %param.22) | copy-start | bytes 98308
  70.4 4.4 %copy-start.6 = (f32[2048]{0:T(1024)S(1)}, f32[2048]{0:T(1024)}, u32[]{:S(2)}) copy-start(f32[2048]{0:T(1024)} %param.21) | copy-start | bytes 24580
  77.3 2.6 %collective-permute-start.19 = (f32[8,768]{1,0:T(8,128)S(1)}, f32[8,768]{1,0:T(8,128)S(1)}, u32[]{:S(2)}, u32[]{:S(2)}) collective-permute-start(f32[8,768]{1,0:T(8,128)S(1)} %get-tuple-element.39), channel_id=1, source_target_pairs={{0,1},{1,0},{2,3},{3,2},{4,5},{5,4},{6,7},{7,6},{8,9},{9,8},{10,11... | collective-permute-start | bytes 73736 | tf_op jit(solution)/shard_map/ppermute | solution.py:24
  77.4 2.4 %copy-start.7 = (s32[192,32]{0,1:T(8,128)S(1)}, s32[192,32]{0,1:T(8,128)}, u32[]{:S(2)}) copy-start(s32[192,32]{0,1:T(8,128)} %param.28) | copy-start | bytes 73732
  77.4 2.4 %copy-start.11 = (s32[192]{0:T(256)S(1)}, s32[192]{0:T(256)}, u32[]{:S(2)}) copy-start(s32[192]{0:T(256)} %param.24) | copy-start | bytes 2308
  77.4 2.4 %copy-start.12 = (s32[192]{0:T(256)S(1)}, s32[192]{0:T(256)}, u32[]{:S(2)}) copy-start(s32[192]{0:T(256)} %param.29) | copy-start | bytes 2308
  77.4 2.4 %copy-start.13 = (f32[8]{0:T(128)S(1)}, f32[8]{0:T(128)}, u32[]{:S(2)}) copy-start(f32[8]{0:T(128)} %param.23) | copy-start | bytes 100

commit v6 on v5

--- a/solution.py
+++ b/solution.py
@@ -306,21 +306,36 @@
     served = call(
         functools.partial(serve_kernel, capacity, par_count), (shape(wide, feature_count),) * len(PLANE), 6
     )(own_ids, from_x, from_y, from_d, table)
-    few = chip_one // 2
-    x_ab = swap_chip(stack((from_a, few, depth - few), (from_b, 0, depth), (served[1], 0, wide)), X)
-    y_ab = swap_chip(stack((from_a, few, depth - few), (from_b, 0, depth), (served[2], 0, wide)), Y)
+    some = chip_one // 4
+    few, rest = chip_one // 4, 3 * chip_two // 8
+    x_ab = swap_chip(
+        stack(
+            (from_a, few, depth - few), (from_b, 0, chip_one), (from_b, chip_one + rest, chip_two - rest),
+            (served[1], 0, wide)
+        ),
+        X,
+    )
+    y_ab = swap_chip(stack((from_a, few, depth - few), (from_b, 0, depth - rest), (served[2], 0, wide)), Y)
     rows_d = swap_chip(stack((served[3], 0, wide), (from_b, 0, chip_one)), D)
     c_da = swap_chip(stack((from_b, 0, depth), (from_d, 0, chip_one), (from_x, 0, few), (from_y, 0, few)), A)
-    plane_c = swap_chip(stack((from_x, 0, chip_one), (from_y, 0, chip_one), (from_d, 0, chip_one)), C)
+    plane_c = swap_chip(stack((from_x, 0, chip_one), (from_y, 0, chip_one), (from_d, 0, chip_one + some)), C)
     x_ab, y_ab, rows_d, c_da, plane_c = lax.optimization_barrier((x_ab, y_ab, rows_d, c_da, plane_c))
 
     cut = chip_two // 2
     at_a, at_b = chip_one - few, depth - few + chip_one
-    x_c = swap_chip(stack((c_da, chip_one, chip_two), (y_ab, at_a, cut), (y_ab, at_b, cut)), X)
-    y_c = swap_chip(stack((c_da, chip_one, chip_two), (x_ab, at_a + cut, cut), (x_ab, at_b + cut, cut)), Y)
-    d_c = swap_chip(stack((from_d, chip_one, chip_two)), C)
-
-    end = 2 * depth - few
+    x_c = swap_chip(
+        stack((c_da, chip_one, chip_two), (y_ab, at_a, cut), (y_ab, at_b, cut), (from_b, chip_one, rest)), X
+    )
+    y_c = swap_chip(
+        stack(
+            (c_da, chip_one, chip_two), (x_ab, at_a + cut, cut), (x_ab, at_b + cut - rest, cut),
+            (from_b, depth - rest, rest)
+        ),
+        Y,
+    )
+    d_c = swap_chip(stack((from_d, chip_one + some, chip_two - some)), C)
+
+    end = 2 * depth - few - rest
     mine = stack(
         (served[0], 0, wide), (x_ab, end, wide), (y_ab, end, wide), (rows_d, 0, wide),
         (parents, 0, par_count), (meta, 0, ID_ROWS)
@@ -346,7 +361,7 @@
 
     early = [(chip, n, chip_one, 0, chip_two) for chip, n in near]
     for n, chip in ((6, X), (7, Y)):
-        early += [(chip ^ A, n, at_a, 0, chip_two), (chip ^ B, n, at_b, 0, chip_two)]
+        early.append((chip ^ A, n, at_a, 0, chip_two))
     early.sort()
     so_far = call(
         functools.partial(second_kernel, early, chip_two),
@@ -355,17 +370,20 @@
         [pltpu.VMEM((len({piece[0] for piece in early}) * chip_two, half), jnp.bfloat16)],
     )(hidden, *arrays)
     late = [(C, 3, chip_one, 0, chip_two), (X ^ C, 0, 0, 0, chip_two), (Y ^ C, 1, 0, 0, chip_two)]
-    late += [(D ^ C, 2, 0, 0, chip_two)]
+    late += [(D ^ C, 6, 3 * chip_one, 0, some), (D ^ C, 2, 0, some, chip_two - some)]
     late += [(D ^ A, 0, chip_two, 0, cut), (D ^ A, 1, chip_two, cut, cut)]
     late += [(D ^ B, 0, chip_two + cut, 0, cut), (D ^ B, 1, chip_two + cut, cut, cut)]
+    tail = chip_two + 2 * cut
+    late += [(X ^ B, 4, at_b, rest, chip_two - rest), (X ^ B, 0, tail, 0, rest)]
+    late += [(Y ^ B, 5, at_b, 0, chip_two - rest), (Y ^ B, 1, tail, chip_two - rest, rest)]
     names = list(dict.fromkeys(piece[0] for piece in late))
     partial = shape(w_head.shape[1], branches, jnp.float32)
     common = (hidden, so_far, b_second[None, :], w_head.T)
     theirs, late_weights = call(
         functools.partial(theirs_kernel, late, names, chip_two, branches),
         (partial, shape(len(names) * chip_two, half)),
-        12,
-    )(*common, x_c, y_c, d_c, c_da)
+        16,
+    )(*common, x_c, y_c, d_c, c_da, x_ab, y_ab, plane_c)
     mine = call(functools.partial(finish_second, names, chip_two, 0), partial, 10)(*common, late_weights)
     strategy, values = call(
         last_kernel, (shape(legal_mask.shape[1], par_count, jnp.float32), shape(1, par_count // 4, jnp.float32)), 4

time: 80.9 us -> 80.4 us (level)
  transfers between devices with their start and end apart: 20 -> 20, of which waited for: 5 -> 7; matrix products, arithmetic and copies ran while one was open for 1% -> 1% of each run, Pallas kernels for 20% -> 19%
where the time goes in v6:
time: 80.4 us; the launch traced here: 80.2 us
  waiting for transfers between devices  35.1 us (44%)
  starting transfers between devices  20.8 us (26%)
  Pallas kernels  19.7 us (25%)
  local copies, waits for them, and re-layouts  2.96 us (4%)
  between operations  0.95 us (1%)
    ppermute x13, waiting for transfers between devices, swap_chip(): lax.ppermute(value, AXES, [(i, i ^ chip << 1) for i in range(TRAV * BULK)])  34 us
    pallas_call x21, Pallas kernels, run(): pl.pallas_call(kernel, out_shape=tuple(outs) if many else outs, in_specs=...  19.7 us
    ppermute x13, starting transfers between devices, swap_chip(): lax.ppermute(value, AXES, [(i, i ^ chip << 1) for i in range(TRAV * BULK)])  19.1 us
    unnamed x28, local copies, waits for them, and re-layouts  2.96 us
    ppermute x7, starting transfers between devices, swap_core(): return lax.ppermute(value, AXES, [(i, i ^ 1) for i in range(TRAV * BULK)])  1.77 us
  transfers between devices with their start and end apart: 20, of which 7 were waited for; matrix products, arithmetic and copies ran while one was open for 1% of the time, Pallas kernels for 19%

profile of v6, /device:TPU:0, one launch (start us, length us, event | category | flops | bytes accessed | tf_op | source)
XLA Modules:
  0.0 80.2 jit_solution(5328626081207356520)
XLA Ops:
  0.6 0.5 collective-permute-start.1
  1.1 0.1 collective-permute-start
  1.2 0.4 collective-permute-start.2
  1.7 0.1 collective-permute-start.3
  1.7 0.7 pad_add_fusion.ids
  2.4 0.9 %copy-done.2 = bf16[64,2048]{1,0:T(8,128)(2,1)S(1)} copy-done((bf16[64,2048]{1,0:T(8,128)(2,1)S(1)}, bf16[64,2048]{1,0:T(8,128)(2,1)}, u32[]{:S(2)}) %copy-start.2) | copy-done | bytes 262168
  3.4 0.9 %copy-done.5 = bf16[32,2048]{1,0:T(8,128)(2,1)S(1)} copy-done((bf16[32,2048]{1,0:T(8,128)(2,1)S(1)}, bf16[32,2048]{1,0:T(8,128)(2,1)}, u32[]{:S(2)}) %copy-start.5) | copy-done | bytes 131096
  4.4 0.1 shard_map.159
  4.4 3.0 %collective-permute-start.4 = (bf16[208,1024]{1,0:T(8,128)(2,1)S(1)}, bf16[208,1024]{1,0:T(8,128)(2,1)S(1)}, u32[]{:S(2)}, u32[]{:S(2)}) collective-permute-start(bf16[208,1024]{1,0:T(8,128)(2,1)S(1)} %get-tuple-element.22.refs_0_), channel_id=1, source_target_pairs={{0,2},{1,3},{2,0},{3,1},{4,6},{5,7},{6,4},{7,5},{8,10},{9,11},{10,... | collective-permute-start | bytes 1277960 | tf_op jit(solution)/shard_map/ppermute | solution.py:20
  7.4 1.5 %collective-permute-start.5 = (bf16[208,1024]{1,0:T(8,128)(2,1)S(1)}, bf16[208,1024]{1,0:T(8,128)(2,1)S(1)}, u32[]{:S(2)}, u32[]{:S(2)}) collective-permute-start(bf16[208,1024]{1,0:T(8,128)(2,1)S(1)} %get-tuple-element.22.refs_0_), channel_id=1, source_target_pairs={{0,4},{1,5},{2,6},{3,7},{4,0},{5,1},{6,2},{7,3},{8,12},{9,13},{10,... | collective-permute-start | bytes 1277960 | tf_op jit(solution)/shard_map/ppermute | solution.py:20
  8.9 0.0 collective-permute-start.6
  9.0 2.0 %collective-permute-start.7 = (bf16[192,1024]{1,0:T(8,128)(2,1)S(1)}, bf16[192,1024]{1,0:T(8,128)(2,1)S(1)}, u32[]{:S(2)}, u32[]{:S(2)}) collective-permute-start(bf16[192,1024]{1,0:T(8,128)(2,1)S(1)} %get-tuple-element.23.refs_0_), channel_id=1, source_target_pairs={{0,8},{1,9},{2,10},{3,11},{4,12},{5,13},{6,14},{7,15},{8,0},{9,1},... | collective-permute-start | bytes 1179656 | tf_op jit(solution)/shard_map/ppermute | solution.py:20
  11.0 2.5 %collective-permute-start.8 = (bf16[192,1024]{1,0:T(8,128)(2,1)S(1)}, bf16[192,1024]{1,0:T(8,128)(2,1)S(1)}, u32[]{:S(2)}, u32[]{:S(2)}) collective-permute-start(bf16[192,1024]{1,0:T(8,128)(2,1)S(1)} %get-tuple-element.23.refs_0_), channel_id=1, source_target_pairs={{0,24},{1,25},{2,26},{3,27},{4,28},{5,29},{6,30},{7,31},{8,16},{9,... | collective-permute-start | bytes 1179656 | tf_op jit(solution)/shard_map/ppermute | solution.py:20
  13.5 1.0 %copy-done = bf16[256,1024]{1,0:T(8,128)(2,1)S(1)} copy-done((bf16[256,1024]{1,0:T(8,128)(2,1)S(1)}, bf16[256,1024]{1,0:T(8,128)(2,1)}, u32[]{:S(2)}) %copy-start) | copy-done | bytes 524312
  14.5 6.0 %collective-permute-done.7.refs_0_.refs_3_ = bf16[192,1024]{1,0:T(8,128)(2,1)S(1)} collective-permute-done((bf16[192,1024]{1,0:T(8,128)(2,1)S(1)}, bf16[192,1024]{1,0:T(8,128)(2,1)S(1)}, u32[]{:S(2)}, u32[]{:S(2)}) %collective-permute-start.7) | collective-permute-done | bytes 393248 | tf_op jit(solution)/shard_map/ppermute | solution.py:20
  20.6 7.5 %collective-permute-done.5.refs_2_.refs_3_.refs_1_ = bf16[208,1024]{1,0:T(8,128)(2,1)S(1)} collective-permute-done((bf16[208,1024]{1,0:T(8,128)(2,1)S(1)}, bf16[208,1024]{1,0:T(8,128)(2,1)S(1)}, u32[]{:S(2)}, u32[]{:S(2)}) %collective-permute-start.5) | collective-permute-done | bytes 426016 | tf_op jit(solution)/shard_map/ppermute | solution.py:20
  28.1 0.7 shard_map.161
  28.8 1.5 %collective-permute-done.8.refs_1_.refs_2_.refs_0_.refs_4_.refs_3_ = bf16[192,1024]{1,0:T(8,128)(2,1)S(1)} collective-permute-done((bf16[192,1024]{1,0:T(8,128)(2,1)S(1)}, bf16[192,1024]{1,0:T(8,128)(2,1)S(1)}, u32[]{:S(2)}, u32[]{:S(2)}) %collective-permute-start.8) | collective-permute-done | bytes 393248 | tf_op jit(solution)/shard_map/ppermute | solution.py:20
  30.2 0.1 shard_map.163
  30.3 1.6 %collective-permute-start.10 = (bf16[384,1024]{1,0:T(8,128)(2,1)S(1)}, bf16[384,1024]{1,0:T(8,128)(2,1)S(1)}, u32[]{:S(2)}, u32[]{:S(2)}) collective-permute-start(bf16[384,1024]{1,0:T(8,128)(2,1)S(1)} %shard_map.163), channel_id=1, source_target_pairs={{0,4},{1,5},{2,6},{3,7},{4,0},{5,1},{6,2},{7,3},{8,12},{9,13},{10,... | collective-permute-start | bytes 2359304 | tf_op jit(solution)/shard_map/ppermute | solution.py:20
  31.9 0.1 shard_map.162
  31.9 1.6 %collective-permute-start.9 = (bf16[384,1024]{1,0:T(8,128)(2,1)S(1)}, bf16[384,1024]{1,0:T(8,128)(2,1)S(1)}, u32[]{:S(2)}, u32[]{:S(2)}) collective-permute-start(bf16[384,1024]{1,0:T(8,128)(2,1)S(1)} %shard_map.162), channel_id=1, source_target_pairs={{0,2},{1,3},{2,0},{3,1},{4,6},{5,7},{6,4},{7,5},{8,10},{9,11},{10,... | collective-permute-start | bytes 2359304 | tf_op jit(solution)/shard_map/ppermute | solution.py:20
  33.5 0.6 collective-permute-start.12
  34.2 2.3 %collective-permute-start.13 = (bf16[208,1024]{1,0:T(8,128)(2,1)S(1)}, bf16[208,1024]{1,0:T(8,128)(2,1)S(1)}, u32[]{:S(2)}, u32[]{:S(2)}) collective-permute-start(bf16[208,1024]{1,0:T(8,128)(2,1)S(1)} %shard_map.166), channel_id=1, source_target_pairs={{0,16},{1,17},{2,18},{3,19},{4,20},{5,21},{6,22},{7,23},{8,24},{9,... | collective-permute-start | bytes 1277960 | tf_op jit(solution)/shard_map/ppermute | solution.py:20
  36.5 0.0 copy-start.1
  36.5 0.5 collective-permute-start.11
  37.0 17.9 %collective-permute-done.11.refs_3_.refs_9_ = bf16[128,1024]{1,0:T(8,128)(2,1)S(1)} collective-permute-done((bf16[128,1024]{1,0:T(8,128)(2,1)S(1)}, bf16[128,1024]{1,0:T(8,128)(2,1)S(1)}, u32[]{:S(2)}, u32[]{:S(2)}) %collective-permute-start.11) | collective-permute-done | bytes 262176 | tf_op jit(solution)/shard_map/ppermute | solution.py:20
  55.0 0.7 collective-permute-done.12.refs_8_.refs_0_.refs_3_
  55.7 0.2 shard_map.170.home
  55.8 0.1 collective-permute-start.15
  55.9 0.2 shard_map.167.refs_5_
  56.1 0.1 shard_map.168.mine
  56.2 0.0 copy-start.3
  56.2 0.5 collective-permute-start.14
  56.8 0.9 %collective-permute-start.16 = (bf16[304,1024]{1,0:T(8,128)(2,1)S(1)}, bf16[304,1024]{1,0:T(8,128)(2,1)S(1)}, u32[]{:S(2)}, u32[]{:S(2)}) collective-permute-start(bf16[304,1024]{1,0:T(8,128)(2,1)S(1)} %shard_map.173), channel_id=1, source_target_pairs={{0,2},{1,3},{2,0},{3,1},{4,6},{5,7},{6,4},{7,5},{8,10},{9,11},{10,... | collective-permute-start | bytes 1867784 | tf_op jit(solution)/shard_map/ppermute | solution.py:20
  57.7 0.0 copy-start.8
  57.7 1.6 %collective-permute-start.17 = (bf16[304,1024]{1,0:T(8,128)(2,1)S(1)}, bf16[304,1024]{1,0:T(8,128)(2,1)S(1)}, u32[]{:S(2)}, u32[]{:S(2)}) collective-permute-start(bf16[304,1024]{1,0:T(8,128)(2,1)S(1)} %shard_map.174), channel_id=1, source_target_pairs={{0,4},{1,5},{2,6},{3,7},{4,0},{5,1},{6,2},{7,3},{8,12},{9,13},{10,... | collective-permute-start | bytes 1867784 | tf_op jit(solution)/shard_map/ppermute | solution.py:20
  59.3 1.0 %collective-permute-start.18 = (bf16[112,1024]{1,0:T(8,128)(2,1)S(1)}, bf16[112,1024]{1,0:T(8,128)(2,1)S(1)}, u32[]{:S(2)}, u32[]{:S(2)}) collective-permute-start(bf16[112,1024]{1,0:T(8,128)(2,1)S(1)} %shard_map.175), channel_id=1, source_target_pairs={{0,16},{1,17},{2,18},{3,19},{4,20},{5,21},{6,22},{7,23},{8,24},{9,... | collective-permute-start | bytes 688136 | tf_op jit(solution)/shard_map/ppermute | solution.py:20
  60.3 1.1 %collective-permute-done.14.theirs = bf16[464,1024]{1,0:T(8,128)(2,1)S(1)} collective-permute-done((bf16[464,1024]{1,0:T(8,128)(2,1)S(1)}, bf16[464,1024]{1,0:T(8,128)(2,1)S(1)}, u32[]{:S(2)}, u32[]{:S(2)}) %collective-permute-start.14) | collective-permute-done | bytes 950304 | tf_op jit(solution)/shard_map/ppermute | solution.py:24
  61.4 1.4 %shard_map.169.inputs = bf16[1536,1024]{1,0:T(8,128)(2,1)S(1)} custom-call(bf16[128,1024]{1,0:T(8,128)(2,1)S(1)} %copy-done.3, bf16[464,1024]{1,0:T(8,128)(2,1)S(1)} %shard_map.168.mine, bf16[464,1024]{1,0:T(8,128)(2,1)S(1)} %collective-permute-done.14.theirs), custom_call_target="tpu_custom_call" | custom-call | tf_op jit(solution)/shard_map/pallas_call | solution.py:48
  62.9 6.8 %shard_map.171.hidden = bf16[1536,2048]{1,0:T(8,128)(2,1)S(1)} custom-call(bf16[1536,1024]{1,0:T(8,128)(2,1)S(1)} %shard_map.169.inputs, bf16[1024,1024]{1,0:T(8,128)(2,1)S(1)} %shard_map.170.home, bf16[1024,1024]{1,0:T(8,128)(2,1)S(1)} %collective-permute-done.15.other, f32[1,2048]{1,0:T(1,128)S(1)} %bitcast.17), custom_call_target="tpu_custom_call" | custom-call | tf_op jit(solution)/shard_map/pallas_call | solution.py:48
  69.7 0.0 copy-start.6
  69.7 3.4 %shard_map.172.so_far = f32[1536,1024]{1,0:T(8,128)S(1)} custom-call(bf16[1536,2048]{1,0:T(8,128)(2,1)S(1)} %shard_map.171.hidden, bf16[192,1024]{1,0:T(8,128)(2,1)S(1)} %get-tuple-element.23.refs_0_, bf16[208,1024]{1,0:T(8,128)(2,1)S(1)} %collective-permute-done.4.refs_1_.refs_2_.refs_0_, ...), custom_call_target="tpu_custom_call" | custom-call | tf_op jit(solution)/shard_map/pallas_call | solution.py:48
  73.1 0.4 collective-permute-done.17.refs_1_
  73.5 3.0 %shard_map.176 = (f32[8,768]{1,0:T(8,128)S(1)}, bf16[1024,1024]{1,0:T(8,128)(2,1)S(1)}) custom-call(bf16[1536,2048]{1,0:T(8,128)(2,1)S(1)} %shard_map.171.hidden, f32[1536,1024]{1,0:T(8,128)S(1)} %shard_map.172.so_far, f32[1,2048]{1,0:T(1,128)S(1)} %bitcast.14, bf16[8,2048]{1,0:T(8,128)(2,1)S(1)} %bitcast.12, ...), custom_call_target="tpu_custom_call" | custom-call | tf_op jit(solution)/shard_map/pallas_call | solution.py:48
  76.5 0.0 collective-permute-start.19
  76.6 2.8 %shard_map.177.mine = f32[8,768]{1,0:T(8,128)S(1)} custom-call(bf16[1536,2048]{1,0:T(8,128)(2,1)S(1)} %shard_map.171.hidden, f32[1536,1024]{1,0:T(8,128)S(1)} %shard_map.172.so_far, f32[1,2048]{1,0:T(1,128)S(1)} %bitcast.15, bf16[8,2048]{1,0:T(8,128)(2,1)S(1)} %bitcast.13, bf16[1024,1024]{1,0:T(8,128)(2,1)S(1)} %get-tuple-element.38.weights), custom_call_target="tpu_custom_call" | custom-call | tf_op jit(solution)/shard_map/pallas_call | solution.py:48
  79.4 0.8 %shard_map.178 = (f32[32,192]{1,0:T(8,128)}, f32[1,48]{1,0:T(1,128)}) custom-call(s32[1,192]{1,0:T(1,128)S(1)} %bitcast.22, s32[1,192]{1,0:T(1,128)S(1)} %bitcast.23, s32[32,192]{1,0:T(8,128)S(1)} %bitcast.16, f32[1,8]{1,0:T(1,128)S(1)} %bitcast.24, f32[8,768]{1,0:T(8,128)S(1)} %shard_map.177.mine, f32[8,768]{1,0:T(8,128)S(1)} %collective-permute-done.19.theirs), custom_call_target="tpu_custom_call" | custom-call | tf_op jit(solution)/shard_map/pallas_call | solution.py:48
  (42 shorter events, 0.3 us)
Async XLA Ops:
  0.6 3.7 %collective-permute-start.1 = (bf16[64,2048]{1,0:T(8,128)(2,1)}, bf16[64,2048]{1,0:T(8,128)(2,1)S(1)}, u32[]{:S(2)}, u32[]{:S(2)}) collective-permute-start(bf16[64,2048]{1,0:T(8,128)(2,1)} %w_second.1), channel_id=1, source_target_pairs={{0,1},{1,0},{2,3},{3,2},{4,5},{5,4},{6,7},{7,6},{8,9},{9,8},{10,11... | collective-permute-start | bytes 786440 | tf_op jit(solution)/shard_map/ppermute | solution.py:24
  1.1 3.2 %collective-permute-start = (bf16[32,2048]{1,0:T(8,128)(2,1)}, bf16[32,2048]{1,0:T(8,128)(2,1)S(1)}, u32[]{:S(2)}, u32[]{:S(2)}) collective-permute-start(bf16[32,2048]{1,0:T(8,128)(2,1)} %w_first.1), channel_id=1, source_target_pairs={{0,1},{1,0},{2,3},{3,2},{4,5},{5,4},{6,7},{7,6},{8,9},{9,8},{10,11... | collective-permute-start | bytes 393224 | tf_op jit(solution)/shard_map/ppermute | solution.py:24
  1.2 3.1 %collective-permute-start.2 = (s32[1,192]{1,0:T(1,128)}, s32[1,192]{1,0:T(1,128)S(1)}, u32[]{:S(2)}, u32[]{:S(2)}) collective-permute-start(s32[1,192]{1,0:T(1,128)} %bitcast.19), channel_id=1, source_target_pairs={{0,1},{1,0},{2,3},{3,2},{4,5},{5,4},{6,7},{7,6},{8,9},{9,8},{10,11... | collective-permute-start | bytes 2312 | tf_op jit(solution)/shard_map/ppermute | solution.py:24
  1.7 2.7 %collective-permute-start.3 = (s32[1,192]{1,0:T(1,128)}, s32[1,192]{1,0:T(1,128)S(1)}, u32[]{:S(2)}, u32[]{:S(2)}) collective-permute-start(s32[1,192]{1,0:T(1,128)} %bitcast.25), channel_id=1, source_target_pairs={{0,1},{1,0},{2,3},{3,2},{4,5},{5,4},{6,7},{7,6},{8,9},{9,8},{10,11... | collective-permute-start | bytes 2312 | tf_op jit(solution)/shard_map/ppermute | solution.py:24
  2.4 0.9 %copy-start.2 = (bf16[64,2048]{1,0:T(8,128)(2,1)S(1)}, bf16[64,2048]{1,0:T(8,128)(2,1)}, u32[]{:S(2)}) copy-start(bf16[64,2048]{1,0:T(8,128)(2,1)} %w_second.1) | copy-start | bytes 786436
  3.4 0.9 %copy-start.5 = (bf16[32,2048]{1,0:T(8,128)(2,1)S(1)}, bf16[32,2048]{1,0:T(8,128)(2,1)}, u32[]{:S(2)}) copy-start(bf16[32,2048]{1,0:T(8,128)(2,1)} %w_first.1) | copy-start | bytes 393220
  4.4 16.1 %collective-permute-start.4 = (bf16[208,1024]{1,0:T(8,128)(2,1)S(1)}, bf16[208,1024]{1,0:T(8,128)(2,1)S(1)}, u32[]{:S(2)}, u32[]{:S(2)}) collective-permute-start(bf16[208,1024]{1,0:T(8,128)(2,1)S(1)} %get-tuple-element.22.refs_0_), channel_id=1, source_target_pairs={{0,2},{1,3},{2,0},{3,1},{4,6},{5,7},{6,4},{7,5},{8,10},{9,11},{10,... | collective-permute-start | bytes 1277960 | tf_op jit(solution)/shard_map/ppermute | solution.py:20
  7.4 20.7 %collective-permute-start.5 = (bf16[208,1024]{1,0:T(8,128)(2,1)S(1)}, bf16[208,1024]{1,0:T(8,128)(2,1)S(1)}, u32[]{:S(2)}, u32[]{:S(2)}) collective-permute-start(bf16[208,1024]{1,0:T(8,128)(2,1)S(1)} %get-tuple-element.22.refs_0_), channel_id=1, source_target_pairs={{0,4},{1,5},{2,6},{3,7},{4,0},{5,1},{6,2},{7,3},{8,12},{9,13},{10,... | collective-permute-start | bytes 1277960 | tf_op jit(solution)/shard_map/ppermute | solution.py:20
  8.9 19.1 %collective-permute-start.6 = (bf16[208,1024]{1,0:T(8,128)(2,1)S(1)}, bf16[208,1024]{1,0:T(8,128)(2,1)S(1)}, u32[]{:S(2)}, u32[]{:S(2)}) collective-permute-start(bf16[208,1024]{1,0:T(8,128)(2,1)S(1)} %get-tuple-element.22.refs_0_), channel_id=1, source_target_pairs={{0,6},{1,7},{2,4},{3,5},{4,2},{5,3},{6,0},{7,1},{8,14},{9,15},{10,... | collective-permute-start | bytes 1277960 | tf_op jit(solution)/shard_map/ppermute | solution.py:20
  9.0 11.6 %collective-permute-start.7 = (bf16[192,1024]{1,0:T(8,128)(2,1)S(1)}, bf16[192,1024]{1,0:T(8,128)(2,1)S(1)}, u32[]{:S(2)}, u32[]{:S(2)}) collective-permute-start(bf16[192,1024]{1,0:T(8,128)(2,1)S(1)} %get-tuple-element.23.refs_0_), channel_id=1, source_target_pairs={{0,8},{1,9},{2,10},{3,11},{4,12},{5,13},{6,14},{7,15},{8,0},{9,1},... | collective-permute-start | bytes 1179656 | tf_op jit(solution)/shard_map/ppermute | solution.py:20
  11.0 19.2 %collective-permute-start.8 = (bf16[192,1024]{1,0:T(8,128)(2,1)S(1)}, bf16[192,1024]{1,0:T(8,128)(2,1)S(1)}, u32[]{:S(2)}, u32[]{:S(2)}) collective-permute-start(bf16[192,1024]{1,0:T(8,128)(2,1)S(1)} %get-tuple-element.23.refs_0_), channel_id=1, source_target_pairs={{0,24},{1,25},{2,26},{3,27},{4,28},{5,29},{6,30},{7,31},{8,16},{9,... | collective-permute-start | bytes 1179656 | tf_op jit(solution)/shard_map/ppermute | solution.py:20
  13.5 1.0 %copy-start = (bf16[256,1024]{1,0:T(8,128)(2,1)S(1)}, bf16[256,1024]{1,0:T(8,128)(2,1)}, u32[]{:S(2)}) copy-start(bf16[256,1024]{1,0:T(8,128)(2,1)} %refs_0_.1) | copy-start | bytes 1572868
  30.3 25.4 %collective-permute-start.10 = (bf16[384,1024]{1,0:T(8,128)(2,1)S(1)}, bf16[384,1024]{1,0:T(8,128)(2,1)S(1)}, u32[]{:S(2)}, u32[]{:S(2)}) collective-permute-start(bf16[384,1024]{1,0:T(8,128)(2,1)S(1)} %shard_map.163), channel_id=1, source_target_pairs={{0,4},{1,5},{2,6},{3,7},{4,0},{5,1},{6,2},{7,3},{8,12},{9,13},{10,... | collective-permute-start | bytes 2359304 | tf_op jit(solution)/shard_map/ppermute | solution.py:20
  31.9 23.7 %collective-permute-start.9 = (bf16[384,1024]{1,0:T(8,128)(2,1)S(1)}, bf16[384,1024]{1,0:T(8,128)(2,1)S(1)}, u32[]{:S(2)}, u32[]{:S(2)}) collective-permute-start(bf16[384,1024]{1,0:T(8,128)(2,1)S(1)} %shard_map.162), channel_id=1, source_target_pairs={{0,2},{1,3},{2,0},{3,1},{4,6},{5,7},{6,4},{7,5},{8,10},{9,11},{10,... | collective-permute-start | bytes 2359304 | tf_op jit(solution)/shard_map/ppermute | solution.py:20
  33.5 22.1 %collective-permute-start.12 = (bf16[288,1024]{1,0:T(8,128)(2,1)S(1)}, bf16[288,1024]{1,0:T(8,128)(2,1)S(1)}, u32[]{:S(2)}, u32[]{:S(2)}) collective-permute-start(bf16[288,1024]{1,0:T(8,128)(2,1)S(1)} %shard_map.165), channel_id=1, source_target_pairs={{0,8},{1,9},{2,10},{3,11},{4,12},{5,13},{6,14},{7,15},{8,0},{9,1},... | collective-permute-start | bytes 1769480 | tf_op jit(solution)/shard_map/ppermute | solution.py:20
  34.2 20.8 %collective-permute-start.13 = (bf16[208,1024]{1,0:T(8,128)(2,1)S(1)}, bf16[208,1024]{1,0:T(8,128)(2,1)S(1)}, u32[]{:S(2)}, u32[]{:S(2)}) collective-permute-start(bf16[208,1024]{1,0:T(8,128)(2,1)S(1)} %shard_map.166), channel_id=1, source_target_pairs={{0,16},{1,17},{2,18},{3,19},{4,20},{5,21},{6,22},{7,23},{8,24},{9,... | collective-permute-start | bytes 1277960 | tf_op jit(solution)/shard_map/ppermute | solution.py:20
  36.5 19.4 %copy-start.9 = (s32[192,4]{0,1:T(4,128)S(1)}, s32[192,4]{0,1:T(4,128)}, u32[]{:S(2)}) copy-start(s32[192,4]{0,1:T(4,128)} %param.25) | copy-start | bytes 9220
  36.5 19.4 %copy-start.10 = (s32[192,1]{0,1:T(1,128)S(1)}, s32[192,1]{0,1:T(1,128)}, u32[]{:S(2)}) copy-start(s32[192,1]{0,1:T(1,128)} %param.26) | copy-start | bytes 2308
  36.5 19.6 %copy-start.1 = (bf16[192,1024]{1,0:T(8,128)(2,1)S(1)}, bf16[192,1024]{1,0:T(8,128)(2,1)}, u32[]{:S(2)}) copy-start(bf16[192,1024]{1,0:T(8,128)(2,1)} %refs_4_.1) | copy-start | bytes 1179652
  36.5 18.5 %collective-permute-start.11 = (bf16[128,1024]{1,0:T(8,128)(2,1)S(1)}, bf16[128,1024]{1,0:T(8,128)(2,1)S(1)}, u32[]{:S(2)}, u32[]{:S(2)}) collective-permute-start(bf16[128,1024]{1,0:T(8,128)(2,1)S(1)} %shard_map.164), channel_id=1, source_target_pairs={{0,6},{1,7},{2,4},{3,5},{4,2},{5,3},{6,0},{7,1},{8,14},{9,15},{10,... | collective-permute-start | bytes 786440 | tf_op jit(solution)/shard_map/ppermute | solution.py:20
  55.8 7.0 %collective-permute-start.15 = (bf16[1024,1024]{1,0:T(8,128)(2,1)S(1)}, bf16[1024,1024]{1,0:T(8,128)(2,1)S(1)}, u32[]{:S(2)}, u32[]{:S(2)}) collective-permute-start(bf16[1024,1024]{1,0:T(8,128)(2,1)S(1)} %shard_map.170.home), channel_id=1, source_target_pairs={{0,1},{1,0},{2,3},{3,2},{4,5},{5,4},{6,7},{7,6},{8,9},{9,8},{10,11... | collective-permute-start | bytes 6291464 | tf_op jit(solution)/shard_map/ppermute | solution.py:24
  56.2 5.2 %copy-start.3 = (bf16[128,1024]{1,0:T(8,128)(2,1)S(1)}, bf16[128,1024]{1,0:T(8,128)(2,1)}, u32[]{:S(2)}) copy-start(bf16[128,1024]{1,0:T(8,128)(2,1)} %act_table.1) | copy-start | bytes 786436
  56.2 5.2 %collective-permute-start.14 = (bf16[464,1024]{1,0:T(8,128)(2,1)S(1)}, bf16[464,1024]{1,0:T(8,128)(2,1)S(1)}, u32[]{:S(2)}, u32[]{:S(2)}) collective-permute-start(bf16[464,1024]{1,0:T(8,128)(2,1)S(1)} %shard_map.168.mine), channel_id=1, source_target_pairs={{0,1},{1,0},{2,3},{3,2},{4,5},{5,4},{6,7},{7,6},{8,9},{9,8},{10,11... | collective-permute-start | bytes 2850824 | tf_op jit(solution)/shard_map/ppermute | solution.py:24
  56.8 16.3 %collective-permute-start.16 = (bf16[304,1024]{1,0:T(8,128)(2,1)S(1)}, bf16[304,1024]{1,0:T(8,128)(2,1)S(1)}, u32[]{:S(2)}, u32[]{:S(2)}) collective-permute-start(bf16[304,1024]{1,0:T(8,128)(2,1)S(1)} %shard_map.173), channel_id=1, source_target_pairs={{0,2},{1,3},{2,0},{3,1},{4,6},{5,7},{6,4},{7,5},{8,10},{9,11},{10,... | collective-permute-start | bytes 1867784 | tf_op jit(solution)/shard_map/ppermute | solution.py:20
  57.7 5.2 %copy-start.8 = (f32[2048]{0:T(1024)S(1)}, f32[2048]{0:T(1024)}, u32[]{:S(2)}) copy-start(f32[2048]{0:T(1024)} %param.19) | copy-start | bytes 24580
  57.7 15.7 %collective-permute-start.17 = (bf16[304,1024]{1,0:T(8,128)(2,1)S(1)}, bf16[304,1024]{1,0:T(8,128)(2,1)S(1)}, u32[]{:S(2)}, u32[]{:S(2)}) collective-permute-start(bf16[304,1024]{1,0:T(8,128)(2,1)S(1)} %shard_map.174), channel_id=1, source_target_pairs={{0,4},{1,5},{2,6},{3,7},{4,0},{5,1},{6,2},{7,3},{8,12},{9,13},{10,... | collective-permute-start | bytes 1867784 | tf_op jit(solution)/shard_map/ppermute | solution.py:20
  59.3 13.8 %collective-permute-start.18 = (bf16[112,1024]{1,0:T(8,128)(2,1)S(1)}, bf16[112,1024]{1,0:T(8,128)(2,1)S(1)}, u32[]{:S(2)}, u32[]{:S(2)}) collective-permute-start(bf16[112,1024]{1,0:T(8,128)(2,1)S(1)} %shard_map.175), channel_id=1, source_target_pairs={{0,16},{1,17},{2,18},{3,19},{4,20},{5,21},{6,22},{7,23},{8,24},{9,... | collective-permute-start | bytes 688136 | tf_op jit(solution)/shard_map/ppermute | solution.py:20
  69.7 3.8 %copy-start.4 = (bf16[2048,8]{0,1:T(8,128)(2,1)S(1)}, bf16[2048,8]{0,1:T(8,128)(2,1)}, u32[]{:S(2)}) copy-start(bf16[2048,8]{0,1:T(8,128)(2,1)} %param.22) | copy-start | bytes 98308
  69.7 3.8 %copy-start.6 = (f32[2048]{0:T(1024)S(1)}, f32[2048]{0:T(1024)}, u32[]{:S(2)}) copy-start(f32[2048]{0:T(1024)} %param.21) | copy-start | bytes 24580
  76.5 2.9 %collective-permute-start.19 = (f32[8,768]{1,0:T(8,128)S(1)}, f32[8,768]{1,0:T(8,128)S(1)}, u32[]{:S(2)}, u32[]{:S(2)}) collective-permute-start(f32[8,768]{1,0:T(8,128)S(1)} %get-tuple-element.39), channel_id=1, source_target_pairs={{0,1},{1,0},{2,3},{3,2},{4,5},{5,4},{6,7},{7,6},{8,9},{9,8},{10,11... | collective-permute-start | bytes 73736 | tf_op jit(solution)/shard_map/ppermute | solution.py:24
  76.5 2.8 %copy-start.7 = (s32[192,32]{0,1:T(8,128)S(1)}, s32[192,32]{0,1:T(8,128)}, u32[]{:S(2)}) copy-start(s32[192,32]{0,1:T(8,128)} %param.28) | copy-start | bytes 73732
  76.5 2.8 %copy-start.11 = (s32[192]{0:T(256)S(1)}, s32[192]{0:T(256)}, u32[]{:S(2)}) copy-start(s32[192]{0:T(256)} %param.24) | copy-start | bytes 2308
  76.5 2.8 %copy-start.12 = (s32[192]{0:T(256)S(1)}, s32[192]{0:T(256)}, u32[]{:S(2)}) copy-start(s32[192]{0:T(256)} %param.29) | copy-start | bytes 2308
  76.5 2.8 %copy-start.13 = (f32[8]{0:T(128)S(1)}, f32[8]{0:T(128)}, u32[]{:S(2)}) copy-start(f32[8]{0:T(128)} %param.23) | copy-start | bytes 100

commit v7 on v6

--- a/solution.py
+++ b/solution.py
@@ -165,7 +165,8 @@
         out[pl.ds(to, count), :] = refs[which][begin : begin + count, :]
 
 
-def first_kernel(depth, inputs, home, other, bias, out):
+def first_kernel(depth, capacity, branch_slots, act_table, mine, theirs, home, other, bias, out, inputs):
+    inputs_kernel(capacity, branch_slots, act_table, mine, theirs, inputs)
     half = home.shape[1]
     chips = half // depth
     me, core = my_chip(), my_core()
@@ -336,14 +337,10 @@
     d_c = swap_chip(stack((from_d, chip_one + some, chip_two - some)), C)
 
     end = 2 * depth - few - rest
-    mine = stack(
+    mine_rows = stack(
         (served[0], 0, wide), (x_ab, end, wide), (y_ab, end, wide), (rows_d, 0, wide),
         (parents, 0, par_count), (meta, 0, ID_ROWS)
     )
-    inputs = call(functools.partial(inputs_kernel, capacity, branch_slots), shape(2 * branches, feature_count), 10)(
-        act_table, mine, swap_core(mine)
-    )
-
     arrays = [own, from_x, from_y, from_a, from_b, from_d, x_ab, y_ab, c_da]
     near = [(chip, n) for n, chip in enumerate((0, X, Y, A, B, D))]
     first_pieces = [(chip, n, 0, 0, chip_one) for chip, n in near] + [(C, 8, 0, 0, chip_one)]
@@ -355,9 +352,12 @@
     weights = call(functools.partial(place_kernel, first_pieces, chip_one), shape(feature_count, half), 4)(
         *arrays, rows_d, plane_c
     )
-    hidden = call(functools.partial(first_kernel, chip_two), shape(2 * branches, hidden_units), 12)(
-        inputs, weights, swap_core(weights), b_first[None, :]
-    )
+    hidden = call(
+        functools.partial(first_kernel, chip_two, capacity, branch_slots),
+        shape(2 * branches, hidden_units),
+        16,
+        [pltpu.VMEM((2 * branches, feature_count), jnp.bfloat16)],
+    )(act_table, mine_rows, swap_core(mine_rows), weights, swap_core(weights), b_first[None, :])
 
     early = [(chip, n, chip_one, 0, chip_two) for chip, n in near]
     for n, chip in ((6, X), (7, Y)):

time: 80.4 us -> 80.2 us (level)
    pallas_call x21 -> x20, Pallas kernels: 19.7 us -> 19.4 us  [run(): pl.pallas_call(kernel, out_shape=tuple(outs) if many else outs, in_specs=...]
where the time goes in v7:
time: 80.2 us; the launch traced here: 80 us
  waiting for transfers between devices  35.2 us (44%)
  starting transfers between devices  20.8 us (26%)
  Pallas kernels  19.4 us (24%)
  local copies, waits for them, and re-layouts  2.96 us (4%)
  between operations  0.93 us (1%)
    ppermute x13, waiting for transfers between devices, swap_chip(): lax.ppermute(value, AXES, [(i, i ^ chip << 1) for i in range(TRAV * BULK)])  34.1 us
    pallas_call x20, Pallas kernels, run(): pl.pallas_call(kernel, out_shape=tuple(outs) if many else outs, in_specs=...  19.4 us
    ppermute x13, starting transfers between devices, swap_chip(): lax.ppermute(value, AXES, [(i, i ^ chip << 1) for i in range(TRAV * BULK)])  19.1 us
    unnamed x28, local copies, waits for them, and re-layouts  2.96 us
    ppermute x7, starting transfers between devices, swap_core(): return lax.ppermute(value, AXES, [(i, i ^ 1) for i in range(TRAV * BULK)])  1.77 us
  transfers between devices with their start and end apart: 20, of which 7 were waited for; matrix products, arithmetic and copies ran while one was open for 1% of the time, Pallas kernels for 19%

profile of v7, /device:TPU:0, one launch (start us, length us, event | category | flops | bytes accessed | tf_op | source)
XLA Modules:
  0.0 80.0 jit_solution(5654437352684851994)
XLA Ops:
  0.6 0.5 collective-permute-start.1
  1.1 0.1 collective-permute-start
  1.2 0.4 collective-permute-start.2
  1.7 0.1 collective-permute-start.3
  1.7 0.7 pad_add_fusion.ids
  2.4 0.9 %copy-done.3 = bf16[64,2048]{1,0:T(8,128)(2,1)S(1)} copy-done((bf16[64,2048]{1,0:T(8,128)(2,1)S(1)}, bf16[64,2048]{1,0:T(8,128)(2,1)}, u32[]{:S(2)}) %copy-start.3) | copy-done | bytes 262168
  3.4 0.9 %copy-done.5 = bf16[32,2048]{1,0:T(8,128)(2,1)S(1)} copy-done((bf16[32,2048]{1,0:T(8,128)(2,1)S(1)}, bf16[32,2048]{1,0:T(8,128)(2,1)}, u32[]{:S(2)}) %copy-start.5) | copy-done | bytes 131096
  4.4 0.1 shard_map.159
  4.4 3.0 %collective-permute-start.4 = (bf16[208,1024]{1,0:T(8,128)(2,1)S(1)}, bf16[208,1024]{1,0:T(8,128)(2,1)S(1)}, u32[]{:S(2)}, u32[]{:S(2)}) collective-permute-start(bf16[208,1024]{1,0:T(8,128)(2,1)S(1)} %get-tuple-element.22.refs_0_), channel_id=1, source_target_pairs={{0,2},{1,3},{2,0},{3,1},{4,6},{5,7},{6,4},{7,5},{8,10},{9,11},{10,... | collective-permute-start | bytes 1277960 | tf_op jit(solution)/shard_map/ppermute | solution.py:20
  7.4 1.5 %collective-permute-start.5 = (bf16[208,1024]{1,0:T(8,128)(2,1)S(1)}, bf16[208,1024]{1,0:T(8,128)(2,1)S(1)}, u32[]{:S(2)}, u32[]{:S(2)}) collective-permute-start(bf16[208,1024]{1,0:T(8,128)(2,1)S(1)} %get-tuple-element.22.refs_0_), channel_id=1, source_target_pairs={{0,4},{1,5},{2,6},{3,7},{4,0},{5,1},{6,2},{7,3},{8,12},{9,13},{10,... | collective-permute-start | bytes 1277960 | tf_op jit(solution)/shard_map/ppermute | solution.py:20
  8.9 0.0 collective-permute-start.6
  9.0 2.0 %collective-permute-start.7 = (bf16[192,1024]{1,0:T(8,128)(2,1)S(1)}, bf16[192,1024]{1,0:T(8,128)(2,1)S(1)}, u32[]{:S(2)}, u32[]{:S(2)}) collective-permute-start(bf16[192,1024]{1,0:T(8,128)(2,1)S(1)} %get-tuple-element.23.refs_0_), channel_id=1, source_target_pairs={{0,8},{1,9},{2,10},{3,11},{4,12},{5,13},{6,14},{7,15},{8,0},{9,1},... | collective-permute-start | bytes 1179656 | tf_op jit(solution)/shard_map/ppermute | solution.py:20
  11.0 2.5 %collective-permute-start.8 = (bf16[192,1024]{1,0:T(8,128)(2,1)S(1)}, bf16[192,1024]{1,0:T(8,128)(2,1)S(1)}, u32[]{:S(2)}, u32[]{:S(2)}) collective-permute-start(bf16[192,1024]{1,0:T(8,128)(2,1)S(1)} %get-tuple-element.23.refs_0_), channel_id=1, source_target_pairs={{0,24},{1,25},{2,26},{3,27},{4,28},{5,29},{6,30},{7,31},{8,16},{9,... | collective-permute-start | bytes 1179656 | tf_op jit(solution)/shard_map/ppermute | solution.py:20
  13.5 1.0 %copy-done = bf16[256,1024]{1,0:T(8,128)(2,1)S(1)} copy-done((bf16[256,1024]{1,0:T(8,128)(2,1)S(1)}, bf16[256,1024]{1,0:T(8,128)(2,1)}, u32[]{:S(2)}) %copy-start) | copy-done | bytes 524312
  14.5 6.0 %collective-permute-done.7.refs_0_.refs_3_ = bf16[192,1024]{1,0:T(8,128)(2,1)S(1)} collective-permute-done((bf16[192,1024]{1,0:T(8,128)(2,1)S(1)}, bf16[192,1024]{1,0:T(8,128)(2,1)S(1)}, u32[]{:S(2)}, u32[]{:S(2)}) %collective-permute-start.7) | collective-permute-done | bytes 393248 | tf_op jit(solution)/shard_map/ppermute | solution.py:20
  20.6 7.5 %collective-permute-done.5.refs_2_.refs_3_.refs_1_ = bf16[208,1024]{1,0:T(8,128)(2,1)S(1)} collective-permute-done((bf16[208,1024]{1,0:T(8,128)(2,1)S(1)}, bf16[208,1024]{1,0:T(8,128)(2,1)S(1)}, u32[]{:S(2)}, u32[]{:S(2)}) %collective-permute-start.5) | collective-permute-done | bytes 426016 | tf_op jit(solution)/shard_map/ppermute | solution.py:20
  28.1 0.7 shard_map.161
  28.8 1.5 %collective-permute-done.8.refs_1_.refs_2_.refs_0_.refs_4_.refs_3_ = bf16[192,1024]{1,0:T(8,128)(2,1)S(1)} collective-permute-done((bf16[192,1024]{1,0:T(8,128)(2,1)S(1)}, bf16[192,1024]{1,0:T(8,128)(2,1)S(1)}, u32[]{:S(2)}, u32[]{:S(2)}) %collective-permute-start.8) | collective-permute-done | bytes 393248 | tf_op jit(solution)/shard_map/ppermute | solution.py:20
  30.2 0.1 shard_map.163
  30.3 1.6 %collective-permute-start.10 = (bf16[384,1024]{1,0:T(8,128)(2,1)S(1)}, bf16[384,1024]{1,0:T(8,128)(2,1)S(1)}, u32[]{:S(2)}, u32[]{:S(2)}) collective-permute-start(bf16[384,1024]{1,0:T(8,128)(2,1)S(1)} %shard_map.163), channel_id=1, source_target_pairs={{0,4},{1,5},{2,6},{3,7},{4,0},{5,1},{6,2},{7,3},{8,12},{9,13},{10,... | collective-permute-start | bytes 2359304 | tf_op jit(solution)/shard_map/ppermute | solution.py:20
  31.9 0.1 shard_map.162
  31.9 1.6 %collective-permute-start.9 = (bf16[384,1024]{1,0:T(8,128)(2,1)S(1)}, bf16[384,1024]{1,0:T(8,128)(2,1)S(1)}, u32[]{:S(2)}, u32[]{:S(2)}) collective-permute-start(bf16[384,1024]{1,0:T(8,128)(2,1)S(1)} %shard_map.162), channel_id=1, source_target_pairs={{0,2},{1,3},{2,0},{3,1},{4,6},{5,7},{6,4},{7,5},{8,10},{9,11},{10,... | collective-permute-start | bytes 2359304 | tf_op jit(solution)/shard_map/ppermute | solution.py:20
  33.5 0.6 collective-permute-start.12
  34.2 2.3 %collective-permute-start.13 = (bf16[208,1024]{1,0:T(8,128)(2,1)S(1)}, bf16[208,1024]{1,0:T(8,128)(2,1)S(1)}, u32[]{:S(2)}, u32[]{:S(2)}) collective-permute-start(bf16[208,1024]{1,0:T(8,128)(2,1)S(1)} %shard_map.166), channel_id=1, source_target_pairs={{0,16},{1,17},{2,18},{3,19},{4,20},{5,21},{6,22},{7,23},{8,24},{9,... | collective-permute-start | bytes 1277960 | tf_op jit(solution)/shard_map/ppermute | solution.py:20
  36.5 0.0 copy-start.10
  36.5 0.0 copy-start.1
  36.5 0.5 collective-permute-start.11
  37.0 17.9 %collective-permute-done.11.refs_3_.refs_9_ = bf16[128,1024]{1,0:T(8,128)(2,1)S(1)} collective-permute-done((bf16[128,1024]{1,0:T(8,128)(2,1)S(1)}, bf16[128,1024]{1,0:T(8,128)(2,1)S(1)}, u32[]{:S(2)}, u32[]{:S(2)}) %collective-permute-start.11) | collective-permute-done | bytes 262176 | tf_op jit(solution)/shard_map/ppermute | solution.py:20
  55.0 0.7 collective-permute-done.12.refs_8_.refs_0_.refs_3_
  55.7 0.2 shard_map.169.home
  55.8 0.1 collective-permute-start.15
  55.9 0.2 shard_map.167.refs_5_
  56.1 0.1 shard_map.168.mine
  56.2 0.5 collective-permute-start.14
  56.8 0.0 copy-start.2
  56.8 0.0 copy-start.8
  56.8 0.9 %collective-permute-start.16 = (bf16[304,1024]{1,0:T(8,128)(2,1)S(1)}, bf16[304,1024]{1,0:T(8,128)(2,1)S(1)}, u32[]{:S(2)}, u32[]{:S(2)}) collective-permute-start(bf16[304,1024]{1,0:T(8,128)(2,1)S(1)} %shard_map.172), channel_id=1, source_target_pairs={{0,2},{1,3},{2,0},{3,1},{4,6},{5,7},{6,4},{7,5},{8,10},{9,11},{10,... | collective-permute-start | bytes 1867784 | tf_op jit(solution)/shard_map/ppermute | solution.py:20
  57.7 1.6 %collective-permute-start.17 = (bf16[304,1024]{1,0:T(8,128)(2,1)S(1)}, bf16[304,1024]{1,0:T(8,128)(2,1)S(1)}, u32[]{:S(2)}, u32[]{:S(2)}) collective-permute-start(bf16[304,1024]{1,0:T(8,128)(2,1)S(1)} %shard_map.173), channel_id=1, source_target_pairs={{0,4},{1,5},{2,6},{3,7},{4,0},{5,1},{6,2},{7,3},{8,12},{9,13},{10,... | collective-permute-start | bytes 1867784 | tf_op jit(solution)/shard_map/ppermute | solution.py:20
  59.3 1.0 %collective-permute-start.18 = (bf16[112,1024]{1,0:T(8,128)(2,1)S(1)}, bf16[112,1024]{1,0:T(8,128)(2,1)S(1)}, u32[]{:S(2)}, u32[]{:S(2)}) collective-permute-start(bf16[112,1024]{1,0:T(8,128)(2,1)S(1)} %shard_map.174), channel_id=1, source_target_pairs={{0,16},{1,17},{2,18},{3,19},{4,20},{5,21},{6,22},{7,23},{8,24},{9,... | collective-permute-start | bytes 688136 | tf_op jit(solution)/shard_map/ppermute | solution.py:20
  60.3 1.1 %collective-permute-done.14.theirs = bf16[464,1024]{1,0:T(8,128)(2,1)S(1)} collective-permute-done((bf16[464,1024]{1,0:T(8,128)(2,1)S(1)}, bf16[464,1024]{1,0:T(8,128)(2,1)S(1)}, u32[]{:S(2)}, u32[]{:S(2)}) %collective-permute-start.14) | collective-permute-done | bytes 950304 | tf_op jit(solution)/shard_map/ppermute | solution.py:24
  61.4 8.1 %shard_map.170.hidden = bf16[1536,2048]{1,0:T(8,128)(2,1)S(1)} custom-call(bf16[128,1024]{1,0:T(8,128)(2,1)S(1)} %copy-done.2, bf16[464,1024]{1,0:T(8,128)(2,1)S(1)} %shard_map.168.mine, bf16[464,1024]{1,0:T(8,128)(2,1)S(1)} %collective-permute-done.14.theirs, bf16[1024,1024]{1,0:T(8,128)(2,1)S(1)} %shard_map.169.home, ...), custom_call_target="tpu_custom_call" | custom-call | tf_op jit(solution)/shard_map/pallas_call | solution.py:48
  69.5 0.0 copy-start.4
  69.6 3.4 %shard_map.171.so_far = f32[1536,1024]{1,0:T(8,128)S(1)} custom-call(bf16[1536,2048]{1,0:T(8,128)(2,1)S(1)} %shard_map.170.hidden, bf16[192,1024]{1,0:T(8,128)(2,1)S(1)} %get-tuple-element.23.refs_0_, bf16[208,1024]{1,0:T(8,128)(2,1)S(1)} %collective-permute-done.4.refs_1_.refs_2_.refs_0_, ...), custom_call_target="tpu_custom_call" | custom-call | tf_op jit(solution)/shard_map/pallas_call | solution.py:48
  73.0 0.5 collective-permute-done.17.refs_1_
  73.5 2.8 %shard_map.175 = (f32[8,768]{1,0:T(8,128)S(1)}, bf16[1024,1024]{1,0:T(8,128)(2,1)S(1)}) custom-call(bf16[1536,2048]{1,0:T(8,128)(2,1)S(1)} %shard_map.170.hidden, f32[1536,1024]{1,0:T(8,128)S(1)} %shard_map.171.so_far, f32[1,2048]{1,0:T(1,128)S(1)} %bitcast.14, bf16[8,2048]{1,0:T(8,128)(2,1)S(1)} %bitcast.12, ...), custom_call_target="tpu_custom_call" | custom-call | tf_op jit(solution)/shard_map/pallas_call | solution.py:48
  76.3 0.0 collective-permute-start.19
  76.4 2.8 %shard_map.176.mine = f32[8,768]{1,0:T(8,128)S(1)} custom-call(bf16[1536,2048]{1,0:T(8,128)(2,1)S(1)} %shard_map.170.hidden, f32[1536,1024]{1,0:T(8,128)S(1)} %shard_map.171.so_far, f32[1,2048]{1,0:T(1,128)S(1)} %bitcast.15, bf16[8,2048]{1,0:T(8,128)(2,1)S(1)} %bitcast.13, bf16[1024,1024]{1,0:T(8,128)(2,1)S(1)} %get-tuple-element.38.weights), custom_call_target="tpu_custom_call" | custom-call | tf_op jit(solution)/shard_map/pallas_call | solution.py:48
  79.2 0.8 %shard_map.177 = (f32[32,192]{1,0:T(8,128)}, f32[1,48]{1,0:T(1,128)}) custom-call(s32[1,192]{1,0:T(1,128)S(1)} %bitcast.22, s32[1,192]{1,0:T(1,128)S(1)} %bitcast.23, s32[32,192]{1,0:T(8,128)S(1)} %bitcast.16, f32[1,8]{1,0:T(1,128)S(1)} %bitcast.24, f32[8,768]{1,0:T(8,128)S(1)} %shard_map.176.mine, f32[8,768]{1,0:T(8,128)S(1)} %collective-permute-done.19.theirs), custom_call_target="tpu_custom_call" | custom-call | tf_op jit(solution)/shard_map/pallas_call | solution.py:48
  (41 shorter events, 0.3 us)
Async XLA Ops:
  0.6 3.7 %collective-permute-start.1 = (bf16[64,2048]{1,0:T(8,128)(2,1)}, bf16[64,2048]{1,0:T(8,128)(2,1)S(1)}, u32[]{:S(2)}, u32[]{:S(2)}) collective-permute-start(bf16[64,2048]{1,0:T(8,128)(2,1)} %w_second.1), channel_id=1, source_target_pairs={{0,1},{1,0},{2,3},{3,2},{4,5},{5,4},{6,7},{7,6},{8,9},{9,8},{10,11... | collective-permute-start | bytes 786440 | tf_op jit(solution)/shard_map/ppermute | solution.py:24
  1.1 3.2 %collective-permute-start = (bf16[32,2048]{1,0:T(8,128)(2,1)}, bf16[32,2048]{1,0:T(8,128)(2,1)S(1)}, u32[]{:S(2)}, u32[]{:S(2)}) collective-permute-start(bf16[32,2048]{1,0:T(8,128)(2,1)} %w_first.1), channel_id=1, source_target_pairs={{0,1},{1,0},{2,3},{3,2},{4,5},{5,4},{6,7},{7,6},{8,9},{9,8},{10,11... | collective-permute-start | bytes 393224 | tf_op jit(solution)/shard_map/ppermute | solution.py:24
  1.2 3.1 %collective-permute-start.2 = (s32[1,192]{1,0:T(1,128)}, s32[1,192]{1,0:T(1,128)S(1)}, u32[]{:S(2)}, u32[]{:S(2)}) collective-permute-start(s32[1,192]{1,0:T(1,128)} %bitcast.19), channel_id=1, source_target_pairs={{0,1},{1,0},{2,3},{3,2},{4,5},{5,4},{6,7},{7,6},{8,9},{9,8},{10,11... | collective-permute-start | bytes 2312 | tf_op jit(solution)/shard_map/ppermute | solution.py:24
  1.7 2.7 %collective-permute-start.3 = (s32[1,192]{1,0:T(1,128)}, s32[1,192]{1,0:T(1,128)S(1)}, u32[]{:S(2)}, u32[]{:S(2)}) collective-permute-start(s32[1,192]{1,0:T(1,128)} %bitcast.25), channel_id=1, source_target_pairs={{0,1},{1,0},{2,3},{3,2},{4,5},{5,4},{6,7},{7,6},{8,9},{9,8},{10,11... | collective-permute-start | bytes 2312 | tf_op jit(solution)/shard_map/ppermute | solution.py:24
  2.4 0.9 %copy-start.3 = (bf16[64,2048]{1,0:T(8,128)(2,1)S(1)}, bf16[64,2048]{1,0:T(8,128)(2,1)}, u32[]{:S(2)}) copy-start(bf16[64,2048]{1,0:T(8,128)(2,1)} %w_second.1) | copy-start | bytes 786436
  3.4 0.9 %copy-start.5 = (bf16[32,2048]{1,0:T(8,128)(2,1)S(1)}, bf16[32,2048]{1,0:T(8,128)(2,1)}, u32[]{:S(2)}) copy-start(bf16[32,2048]{1,0:T(8,128)(2,1)} %w_first.1) | copy-start | bytes 393220
  4.4 16.1 %collective-permute-start.4 = (bf16[208,1024]{1,0:T(8,128)(2,1)S(1)}, bf16[208,1024]{1,0:T(8,128)(2,1)S(1)}, u32[]{:S(2)}, u32[]{:S(2)}) collective-permute-start(bf16[208,1024]{1,0:T(8,128)(2,1)S(1)} %get-tuple-element.22.refs_0_), channel_id=1, source_target_pairs={{0,2},{1,3},{2,0},{3,1},{4,6},{5,7},{6,4},{7,5},{8,10},{9,11},{10,... | collective-permute-start | bytes 1277960 | tf_op jit(solution)/shard_map/ppermute | solution.py:20
  7.4 20.7 %collective-permute-start.5 = (bf16[208,1024]{1,0:T(8,128)(2,1)S(1)}, bf16[208,1024]{1,0:T(8,128)(2,1)S(1)}, u32[]{:S(2)}, u32[]{:S(2)}) collective-permute-start(bf16[208,1024]{1,0:T(8,128)(2,1)S(1)} %get-tuple-element.22.refs_0_), channel_id=1, source_target_pairs={{0,4},{1,5},{2,6},{3,7},{4,0},{5,1},{6,2},{7,3},{8,12},{9,13},{10,... | collective-permute-start | bytes 1277960 | tf_op jit(solution)/shard_map/ppermute | solution.py:20
  8.9 19.1 %collective-permute-start.6 = (bf16[208,1024]{1,0:T(8,128)(2,1)S(1)}, bf16[208,1024]{1,0:T(8,128)(2,1)S(1)}, u32[]{:S(2)}, u32[]{:S(2)}) collective-permute-start(bf16[208,1024]{1,0:T(8,128)(2,1)S(1)} %get-tuple-element.22.refs_0_), channel_id=1, source_target_pairs={{0,6},{1,7},{2,4},{3,5},{4,2},{5,3},{6,0},{7,1},{8,14},{9,15},{10,... | collective-permute-start | bytes 1277960 | tf_op jit(solution)/shard_map/ppermute | solution.py:20
  9.0 11.6 %collective-permute-start.7 = (bf16[192,1024]{1,0:T(8,128)(2,1)S(1)}, bf16[192,1024]{1,0:T(8,128)(2,1)S(1)}, u32[]{:S(2)}, u32[]{:S(2)}) collective-permute-start(bf16[192,1024]{1,0:T(8,128)(2,1)S(1)} %get-tuple-element.23.refs_0_), channel_id=1, source_target_pairs={{0,8},{1,9},{2,10},{3,11},{4,12},{5,13},{6,14},{7,15},{8,0},{9,1},... | collective-permute-start | bytes 1179656 | tf_op jit(solution)/shard_map/ppermute | solution.py:20
  11.0 19.2 %collective-permute-start.8 = (bf16[192,1024]{1,0:T(8,128)(2,1)S(1)}, bf16[192,1024]{1,0:T(8,128)(2,1)S(1)}, u32[]{:S(2)}, u32[]{:S(2)}) collective-permute-start(bf16[192,1024]{1,0:T(8,128)(2,1)S(1)} %get-tuple-element.23.refs_0_), channel_id=1, source_target_pairs={{0,24},{1,25},{2,26},{3,27},{4,28},{5,29},{6,30},{7,31},{8,16},{9,... | collective-permute-start | bytes 1179656 | tf_op jit(solution)/shard_map/ppermute | solution.py:20
  13.5 1.0 %copy-start = (bf16[256,1024]{1,0:T(8,128)(2,1)S(1)}, bf16[256,1024]{1,0:T(8,128)(2,1)}, u32[]{:S(2)}) copy-start(bf16[256,1024]{1,0:T(8,128)(2,1)} %refs_0_.1) | copy-start | bytes 1572868
  30.3 25.4 %collective-permute-start.10 = (bf16[384,1024]{1,0:T(8,128)(2,1)S(1)}, bf16[384,1024]{1,0:T(8,128)(2,1)S(1)}, u32[]{:S(2)}, u32[]{:S(2)}) collective-permute-start(bf16[384,1024]{1,0:T(8,128)(2,1)S(1)} %shard_map.163), channel_id=1, source_target_pairs={{0,4},{1,5},{2,6},{3,7},{4,0},{5,1},{6,2},{7,3},{8,12},{9,13},{10,... | collective-permute-start | bytes 2359304 | tf_op jit(solution)/shard_map/ppermute | solution.py:20
  31.9 23.7 %collective-permute-start.9 = (bf16[384,1024]{1,0:T(8,128)(2,1)S(1)}, bf16[384,1024]{1,0:T(8,128)(2,1)S(1)}, u32[]{:S(2)}, u32[]{:S(2)}) collective-permute-start(bf16[384,1024]{1,0:T(8,128)(2,1)S(1)} %shard_map.162), channel_id=1, source_target_pairs={{0,2},{1,3},{2,0},{3,1},{4,6},{5,7},{6,4},{7,5},{8,10},{9,11},{10,... | collective-permute-start | bytes 2359304 | tf_op jit(solution)/shard_map/ppermute | solution.py:20
  33.5 22.1 %collective-permute-start.12 = (bf16[288,1024]{1,0:T(8,128)(2,1)S(1)}, bf16[288,1024]{1,0:T(8,128)(2,1)S(1)}, u32[]{:S(2)}, u32[]{:S(2)}) collective-permute-start(bf16[288,1024]{1,0:T(8,128)(2,1)S(1)} %shard_map.165), channel_id=1, source_target_pairs={{0,8},{1,9},{2,10},{3,11},{4,12},{5,13},{6,14},{7,15},{8,0},{9,1},... | collective-permute-start | bytes 1769480 | tf_op jit(solution)/shard_map/ppermute | solution.py:20
  34.2 20.8 %collective-permute-start.13 = (bf16[208,1024]{1,0:T(8,128)(2,1)S(1)}, bf16[208,1024]{1,0:T(8,128)(2,1)S(1)}, u32[]{:S(2)}, u32[]{:S(2)}) collective-permute-start(bf16[208,1024]{1,0:T(8,128)(2,1)S(1)} %shard_map.166), channel_id=1, source_target_pairs={{0,16},{1,17},{2,18},{3,19},{4,20},{5,21},{6,22},{7,23},{8,24},{9,... | collective-permute-start | bytes 1277960 | tf_op jit(solution)/shard_map/ppermute | solution.py:20
  36.5 19.4 %copy-start.9 = (s32[192,4]{0,1:T(4,128)S(1)}, s32[192,4]{0,1:T(4,128)}, u32[]{:S(2)}) copy-start(s32[192,4]{0,1:T(4,128)} %param.25) | copy-start | bytes 9220
  36.5 19.4 %copy-start.10 = (s32[192,1]{0,1:T(1,128)S(1)}, s32[192,1]{0,1:T(1,128)}, u32[]{:S(2)}) copy-start(s32[192,1]{0,1:T(1,128)} %param.26) | copy-start | bytes 2308
  36.5 19.6 %copy-start.1 = (bf16[192,1024]{1,0:T(8,128)(2,1)S(1)}, bf16[192,1024]{1,0:T(8,128)(2,1)}, u32[]{:S(2)}) copy-start(bf16[192,1024]{1,0:T(8,128)(2,1)} %refs_4_.1) | copy-start | bytes 1179652
  36.5 18.5 %collective-permute-start.11 = (bf16[128,1024]{1,0:T(8,128)(2,1)S(1)}, bf16[128,1024]{1,0:T(8,128)(2,1)S(1)}, u32[]{:S(2)}, u32[]{:S(2)}) collective-permute-start(bf16[128,1024]{1,0:T(8,128)(2,1)S(1)} %shard_map.164), channel_id=1, source_target_pairs={{0,6},{1,7},{2,4},{3,5},{4,2},{5,3},{6,0},{7,1},{8,14},{9,15},{10,... | collective-permute-start | bytes 786440 | tf_op jit(solution)/shard_map/ppermute | solution.py:20
  55.8 5.6 %collective-permute-start.15 = (bf16[1024,1024]{1,0:T(8,128)(2,1)S(1)}, bf16[1024,1024]{1,0:T(8,128)(2,1)S(1)}, u32[]{:S(2)}, u32[]{:S(2)}) collective-permute-start(bf16[1024,1024]{1,0:T(8,128)(2,1)S(1)} %shard_map.169.home), channel_id=1, source_target_pairs={{0,1},{1,0},{2,3},{3,2},{4,5},{5,4},{6,7},{7,6},{8,9},{9,8},{10,11... | collective-permute-start | bytes 6291464 | tf_op jit(solution)/shard_map/ppermute | solution.py:24
  56.2 5.2 %collective-permute-start.14 = (bf16[464,1024]{1,0:T(8,128)(2,1)S(1)}, bf16[464,1024]{1,0:T(8,128)(2,1)S(1)}, u32[]{:S(2)}, u32[]{:S(2)}) collective-permute-start(bf16[464,1024]{1,0:T(8,128)(2,1)S(1)} %shard_map.168.mine), channel_id=1, source_target_pairs={{0,1},{1,0},{2,3},{3,2},{4,5},{5,4},{6,7},{7,6},{8,9},{9,8},{10,11... | collective-permute-start | bytes 2850824 | tf_op jit(solution)/shard_map/ppermute | solution.py:24
  56.8 4.7 %copy-start.2 = (bf16[128,1024]{1,0:T(8,128)(2,1)S(1)}, bf16[128,1024]{1,0:T(8,128)(2,1)}, u32[]{:S(2)}) copy-start(bf16[128,1024]{1,0:T(8,128)(2,1)} %act_table.1) | copy-start | bytes 786436
  56.8 4.7 %copy-start.8 = (f32[2048]{0:T(1024)S(1)}, f32[2048]{0:T(1024)}, u32[]{:S(2)}) copy-start(f32[2048]{0:T(1024)} %param.19) | copy-start | bytes 24580
  56.8 16.2 %collective-permute-start.16 = (bf16[304,1024]{1,0:T(8,128)(2,1)S(1)}, bf16[304,1024]{1,0:T(8,128)(2,1)S(1)}, u32[]{:S(2)}, u32[]{:S(2)}) collective-permute-start(bf16[304,1024]{1,0:T(8,128)(2,1)S(1)} %shard_map.172), channel_id=1, source_target_pairs={{0,2},{1,3},{2,0},{3,1},{4,6},{5,7},{6,4},{7,5},{8,10},{9,11},{10,... | collective-permute-start | bytes 1867784 | tf_op jit(solution)/shard_map/ppermute | solution.py:20
  57.7 15.7 %collective-permute-start.17 = (bf16[304,1024]{1,0:T(8,128)(2,1)S(1)}, bf16[304,1024]{1,0:T(8,128)(2,1)S(1)}, u32[]{:S(2)}, u32[]{:S(2)}) collective-permute-start(bf16[304,1024]{1,0:T(8,128)(2,1)S(1)} %shard_map.173), channel_id=1, source_target_pairs={{0,4},{1,5},{2,6},{3,7},{4,0},{5,1},{6,2},{7,3},{8,12},{9,13},{10,... | collective-permute-start | bytes 1867784 | tf_op jit(solution)/shard_map/ppermute | solution.py:20
  59.3 13.6 %collective-permute-start.18 = (bf16[112,1024]{1,0:T(8,128)(2,1)S(1)}, bf16[112,1024]{1,0:T(8,128)(2,1)S(1)}, u32[]{:S(2)}, u32[]{:S(2)}) collective-permute-start(bf16[112,1024]{1,0:T(8,128)(2,1)S(1)} %shard_map.174), channel_id=1, source_target_pairs={{0,16},{1,17},{2,18},{3,19},{4,20},{5,21},{6,22},{7,23},{8,24},{9,... | collective-permute-start | bytes 688136 | tf_op jit(solution)/shard_map/ppermute | solution.py:20
  69.5 4.0 %copy-start.4 = (bf16[2048,8]{0,1:T(8,128)(2,1)S(1)}, bf16[2048,8]{0,1:T(8,128)(2,1)}, u32[]{:S(2)}) copy-start(bf16[2048,8]{0,1:T(8,128)(2,1)} %param.22) | copy-start | bytes 98308
  69.5 3.9 %copy-start.6 = (f32[2048]{0:T(1024)S(1)}, f32[2048]{0:T(1024)}, u32[]{:S(2)}) copy-start(f32[2048]{0:T(1024)} %param.21) | copy-start | bytes 24580
  76.3 2.9 %collective-permute-start.19 = (f32[8,768]{1,0:T(8,128)S(1)}, f32[8,768]{1,0:T(8,128)S(1)}, u32[]{:S(2)}, u32[]{:S(2)}) collective-permute-start(f32[8,768]{1,0:T(8,128)S(1)} %get-tuple-element.39), channel_id=1, source_target_pairs={{0,1},{1,0},{2,3},{3,2},{4,5},{5,4},{6,7},{7,6},{8,9},{9,8},{10,11... | collective-permute-start | bytes 73736 | tf_op jit(solution)/shard_map/ppermute | solution.py:24
  76.3 2.8 %copy-start.7 = (s32[192,32]{0,1:T(8,128)S(1)}, s32[192,32]{0,1:T(8,128)}, u32[]{:S(2)}) copy-start(s32[192,32]{0,1:T(8,128)} %param.28) | copy-start | bytes 73732
  76.3 2.8 %copy-start.11 = (s32[192]{0:T(256)S(1)}, s32[192]{0:T(256)}, u32[]{:S(2)}) copy-start(s32[192]{0:T(256)} %param.24) | copy-start | bytes 2308
  76.3 2.8 %copy-start.12 = (s32[192]{0:T(256)S(1)}, s32[192]{0:T(256)}, u32[]{:S(2)}) copy-start(s32[192]{0:T(256)} %param.29) | copy-start | bytes 2308
  76.3 2.8 %copy-start.13 = (f32[8]{0:T(128)S(1)}, f32[8]{0:T(128)}, u32[]{:S(2)}) copy-start(f32[8]{0:T(128)} %param.23) | copy-start | bytes 100
